TPU v7x, 32 devices: a whole 2x2x4 slice. The times are simulated.
32 devices in a mesh: rows: 8 (over z, y), feat: 4 (over x, core).
Axes of the slice: x: 2, y: 2, z: 4, core: 2. Of those that a mesh axis runs over, the one named last changes fastest.
Arguments:
- raw_rows: float32 [16384, 100], P('rows', 'feat'), may hold values from -400 to 400
- enc_weight: bfloat16 [100, 512], replicated, may hold values from -0.625 to 0.625
- enc_bias: float32 [512], replicated, may hold values from -3 to 3
- label_table: bfloat16 [10, 512], replicated, may hold values from -5 to 5
- w_query: bfloat16 [512, 512], replicated, may hold values from -0.25 to 0.25
- b_query: float32 [512], replicated, may hold values from -2 to 2
- w_key: bfloat16 [512, 512], replicated, may hold values from -0.25 to 0.25
- w_value: bfloat16 [512, 512], replicated, may hold values from -0.25 to 0.25
- b_value: float32 [512], replicated, may hold values from -2 to 2
- w_out: bfloat16 [512, 512], replicated, may hold values from -1 to 1
- b_out: float32 [512], replicated, may hold values from -2 to 2
- gain_one: float32 [512], replicated, may hold values from 0.5 to 1.5
- shift_one: float32 [512], replicated, may hold values from -2 to 2
- w_in: bfloat16 [512, 1024], replicated, may hold values from -0.25 to 0.25
- b_in: float32 [1024], replicated, may hold values from -2 to 2
- w_back: bfloat16 [1024, 512], replicated, may hold values from -0.1875 to 0.1875
- b_back: float32 [512], replicated, may hold values from -2 to 2
- gain_two: float32 [512], replicated, may hold values from 0.5 to 1.5
- shift_two: float32 [512], replicated, may hold values from -2 to 2
- members: int32 [64, 1100], P(('rows', 'feat')), may hold values from 0 to 16383, as said below
- labels: int32 [64, 1000], P(('rows', 'feat')), may hold values from 0 to 9
- queries: int32 [64], P(('rows', 'feat')), may hold values from 1 to 100
- cotangent: float32 [64, 1100, 512], P(('rows', 'feat')), may hold values from -6 to 6
Outputs:
- layer_out: bfloat16 [64, 1100, 512], P(('rows', 'feat'))
- raw_grad: float32 [16384, 100], P('rows', 'feat')
- grad_enc_weight: float32 [100, 512], replicated
- grad_enc_bias: float32 [512], replicated
- grad_label_table: float32 [10, 512], replicated
- grad_w_query: float32 [512, 512], replicated
- grad_b_query: float32 [512], replicated
- grad_w_key: float32 [512, 512], replicated
- grad_w_value: float32 [512, 512], replicated
- grad_b_value: float32 [512], replicated
- grad_w_out: float32 [512, 512], replicated
- grad_b_out: float32 [512], replicated
- grad_gain_one: float32 [512], replicated
- grad_shift_one: float32 [512], replicated
- grad_w_in: float32 [512, 1024], replicated
- grad_b_in: float32 [1024], replicated
- grad_w_back: float32 [1024, 512], replicated
- grad_b_back: float32 [512], replicated
- grad_gain_two: float32 [512], replicated
- grad_shift_two: float32 [512], replicated
Inputs may be any that keep to these rules, and one draw needn't show every extreme that they name: members[n, j] names a table row. Take the neighbourhoods in blocks of 2 in order, block b; every row named in block b has (row // 512) % 4 == b % 4; within one block at most 275 slots name rows of one group of 2048 consecutive rows, and some group is named exactly 275 times.
All inputs are finite; a program needn't handle non-finite values.
Results may differ from a plain program's by a relative error of at most 0.012.
Values may be sent and summed in bfloat16 or wider, within the bound.
No kernel may reach another device: no remote copies, remote signals or barrier semaphores. Data moves between devices by JAX's collectives and lax.ppermute only.
A program may use at most 192 MiB of HBM per device.

v0:
```python
import math

import jax
import jax.numpy as jnp
from jax import lax
from jax.sharding import PartitionSpec as P

HEADS = 4


epsilon = 1e-05


def product(left, right):
    return jnp.dot(left, right, preferred_element_type=jnp.float32)


def exact_product(left, right):
    return jnp.dot(left, right, preferred_element_type=jnp.float32, precision=lax.Precision.HIGHEST)


def norm_apply(values, gain, shift):
    centre = jnp.mean(values, -1, keepdims=True)
    offset = values - centre
    second = jnp.mean(offset * offset, -1, keepdims=True)
    return offset * lax.rsqrt(second + epsilon) * gain + shift


def block_pass(weights, stream, alive_rows, cot_rows, ctx_len):
    (
        w_query,
        b_query,
        w_key,
        w_value,
        b_value,
        w_out,
        b_out,
        gain_one,
        shift_one,
        w_in,
        b_in,
        w_back,
        b_back,
        gain_two,
        shift_two,
    ) = weights
    slot_span, model_width = stream.shape
    head_width = model_width // HEADS
    score_root = math.sqrt(head_width)
    stream_low = stream.astype(jnp.bfloat16)
    context = stream_low[:ctx_len]
    query_all = product(stream_low, w_query) + b_query
    keys_all = product(context, w_key)
    values_all = product(context, w_value) + b_value
    query_low = query_all.astype(jnp.bfloat16).reshape(slot_span, HEADS, head_width)
    keys_low = keys_all.astype(jnp.bfloat16).reshape(ctx_len, HEADS, head_width)
    values_low = values_all.astype(jnp.bfloat16).reshape(ctx_len, HEADS, head_width)
    scores = (
        jnp.einsum("shd,chd->hsc", query_low, keys_low, preferred_element_type=jnp.float32)
        / score_root
    )
    highest = jnp.max(scores, -1, keepdims=True)
    exponent = jnp.exp(scores - highest)
    totals = jnp.sum(exponent, -1, keepdims=True)
    log_total = highest + jnp.log(totals)
    prob_low = (exponent / totals).astype(jnp.bfloat16)
    mixed_heads = jnp.einsum(
        "hsc,chd->shd", prob_low, values_low, preferred_element_type=jnp.float32
    ).reshape(slot_span, model_width)
    mixed_low = mixed_heads.astype(jnp.bfloat16)
    attended = product(mixed_low, w_out) + b_out
    normed, first_pull = jax.vjp(norm_apply, stream + attended, gain_one, shift_one)
    normed_low = normed.astype(jnp.bfloat16)
    hidden = product(normed_low, w_in) + b_in
    active, gelu_pull = jax.vjp(jax.nn.gelu, hidden)
    active_low = active.astype(jnp.bfloat16)
    branch = product(active_low, w_back) + b_back
    final_norm, second_pull = jax.vjp(norm_apply, normed + branch, gain_two, shift_two)
    result = alive_rows[:, None] * final_norm
    d_second, g_gain_two, g_shift_two = second_pull(alive_rows[:, None] * cot_rows)
    d_branch = d_second.astype(jnp.bfloat16)
    g_back = product(active_low.T, d_branch)
    g_bias_back = jnp.sum(d_branch, 0, dtype=jnp.float32)
    (d_hidden,) = gelu_pull(product(d_branch, w_back.T))
    d_hidden_low = d_hidden.astype(jnp.bfloat16)
    g_in = product(normed_low.T, d_hidden_low)
    g_bias_in = jnp.sum(d_hidden_low, 0, dtype=jnp.float32)
    d_first, g_gain_one, g_shift_one = first_pull(d_second + product(d_hidden_low, w_in.T))
    d_attended = d_first.astype(jnp.bfloat16)
    g_out = product(mixed_low.T, d_attended)
    g_bias_out = jnp.sum(d_attended, 0, dtype=jnp.float32)
    d_mixed = (
        product(d_attended, w_out.T).astype(jnp.bfloat16).reshape(slot_span, HEADS, head_width)
    )
    scores_again = (
        jnp.einsum("shd,chd->hsc", query_low, keys_low, preferred_element_type=jnp.float32)
        / score_root
    )
    prob_values = jnp.exp(scores_again - log_total)
    prob_again = prob_values.astype(jnp.bfloat16)
    d_values = (
        jnp.einsum("hsc,shd->chd", prob_again, d_mixed, preferred_element_type=jnp.float32)
        .reshape(ctx_len, model_width)
        .astype(jnp.bfloat16)
    )
    d_probs = jnp.einsum("shd,chd->hsc", d_mixed, values_low, preferred_element_type=jnp.float32)
    d_scores = (prob_values * (d_probs - jnp.sum(d_probs * prob_values, -1, keepdims=True))).astype(
        jnp.bfloat16
    )
    d_query = (
        (
            jnp.einsum("hsc,chd->shd", d_scores, keys_low, preferred_element_type=jnp.float32)
            / score_root
        )
        .reshape(slot_span, model_width)
        .astype(jnp.bfloat16)
    )
    d_keys = (
        (
            jnp.einsum("hsc,shd->chd", d_scores, query_low, preferred_element_type=jnp.float32)
            / score_root
        )
        .reshape(ctx_len, model_width)
        .astype(jnp.bfloat16)
    )
    g_query = product(stream_low.T, d_query)
    g_bias_query = jnp.sum(d_query, 0, dtype=jnp.float32)
    g_key = product(context.T, d_keys)
    g_value = product(context.T, d_values)
    g_bias_value = jnp.sum(d_values, 0, dtype=jnp.float32)
    d_context = product(d_keys, w_key.T) + product(d_values, w_value.T)
    d_stream = (
        d_first
        + product(d_query, w_query.T)
        + jnp.concatenate(
            [d_context, jnp.zeros((slot_span - ctx_len, model_width), jnp.float32)], 0
        )
    )
    return (
        result,
        d_stream,
        (
            g_query,
            g_bias_query,
            g_key,
            g_value,
            g_bias_value,
            g_out,
            g_bias_out,
            g_gain_one,
            g_shift_one,
            g_in,
            g_bias_in,
            g_back,
            g_bias_back,
            g_gain_two,
            g_shift_two,
        ),
    )


def body(
    raw_rows,
    enc_weight,
    enc_bias,
    label_table,
    w_query,
    b_query,
    w_key,
    w_value,
    b_value,
    w_out,
    b_out,
    gain_one,
    shift_one,
    w_in,
    b_in,
    w_back,
    b_back,
    gain_two,
    shift_two,
    members,
    labels,
    queries,
    cotangent,
):
    row_count = lax.axis_size("rows")
    feat_count = lax.axis_size("feat")
    feat_index = lax.axis_index("feat")
    local_rows, col_width = raw_rows.shape
    own_rows = local_rows // feat_count
    model_width = enc_weight.shape[1]
    row_total = float(local_rows * row_count)
    stat_sums = lax.psum((jnp.sum(raw_rows, 0), jnp.sum(raw_rows * raw_rows, 0)), "rows")
    col_mean = stat_sums[0] / row_total
    spread = stat_sums[1] / row_total - col_mean * col_mean
    factor = lax.rsqrt(spread + epsilon)
    centred = raw_rows - col_mean
    standard_low = (centred * factor).astype(jnp.bfloat16)
    flat_members = members.reshape(-1)
    slot_total = flat_members.shape[0]
    capacity = (slot_total + row_count - 1) // row_count
    source = flat_members // (own_rows * feat_count)
    row_place = flat_members % own_rows
    src_hot = (source[:, None] == jnp.arange(row_count, dtype=jnp.int32)[None, :]).astype(jnp.int32)
    src_rank = jnp.sum((jnp.cumsum(src_hot, 0) - src_hot) * src_hot, 1)
    target = source * capacity + src_rank
    wanted = (
        jnp.zeros((row_count * capacity,), jnp.int32)
        .at[target]
        .set(row_place)
        .reshape(row_count, capacity)
    )
    asked_rows = lax.all_to_all(wanted, "rows", split_axis=0, concat_axis=0, tiled=True).reshape(-1)
    w_part = lax.dynamic_slice_in_dim(enc_weight, feat_index * col_width, col_width, 0)
    piece = standard_low
    embedded = (
        lax.psum_scatter(product(piece, w_part), "feat", scatter_dimension=0, tiled=True) + enc_bias
    )
    outgoing = embedded.astype(jnp.bfloat16)[asked_rows].reshape(row_count, capacity, model_width)
    arrived = lax.all_to_all(outgoing, "rows", split_axis=0, concat_axis=0, tiled=True)
    slot_values = arrived.reshape(row_count * capacity, model_width)[target].astype(jnp.float32)
    block_count, slot_span = members.shape
    ctx_len = labels.shape[1]
    slot_values = slot_values.reshape(block_count, slot_span, model_width)
    label_hot = (
        labels[:, :, None] == jnp.arange(label_table.shape[0], dtype=jnp.int32)[None, None, :]
    ).astype(jnp.float32)
    label_add = jnp.einsum(
        "nci,id->ncd", label_hot, label_table.astype(jnp.float32), precision=lax.Precision.HIGHEST
    )
    stream_in = jnp.concatenate([slot_values[:, :ctx_len] + label_add, slot_values[:, ctx_len:]], 1)
    live_mask = (
        jnp.arange(slot_span, dtype=jnp.int32)[None, :] < (ctx_len + queries)[:, None]
    ).astype(jnp.float32)
    weights = (
        w_query,
        b_query,
        w_key,
        w_value,
        b_value,
        w_out,
        b_out,
        gain_one,
        shift_one,
        w_in,
        b_in,
        w_back,
        b_back,
        gain_two,
        shift_two,
    )
    start_sums = tuple((jnp.zeros(item.shape, jnp.float32) for item in weights))

    def layer_step(carry, item):
        stream, alive_rows, cot_rows = item
        result, d_stream, grad_terms = block_pass(weights, stream, alive_rows, cot_rows, ctx_len)
        return (
            tuple((running + term for running, term in zip(carry, grad_terms))),
            (result, d_stream),
        )

    grad_sums, (results, d_streams) = lax.scan(
        layer_step, start_sums, (stream_in, live_mask, cotangent)
    )
    g_table = jnp.einsum(
        "nci,ncd->id", label_hot, d_streams[:, :ctx_len], precision=lax.Precision.HIGHEST
    )
    d_slots = d_streams.reshape(block_count * slot_span, model_width).astype(jnp.bfloat16)
    sending = (
        jnp.zeros((row_count * capacity, model_width), jnp.bfloat16)
        .at[target]
        .set(d_slots)
        .reshape(row_count, capacity, model_width)
    )
    coming = lax.all_to_all(sending, "rows", split_axis=0, concat_axis=0, tiled=True)
    d_embed = (
        jnp.zeros((own_rows, model_width), jnp.float32)
        .at[asked_rows]
        .add(coming.reshape(row_count * capacity, model_width).astype(jnp.float32))
    )
    g_enc_bias = jnp.sum(d_embed, 0)
    part_float = w_part.astype(jnp.float32)
    piece = lax.all_gather(d_embed.astype(jnp.bfloat16), "feat", axis=0, tiled=True).astype(
        jnp.float32
    )
    rows_here = standard_low.astype(jnp.float32)
    g_part = exact_product(rows_here.T, piece)
    d_part = exact_product(piece, part_float.T)
    g_part, d_standard = (g_part, d_part)
    g_encoder = lax.dynamic_update_slice_in_dim(
        jnp.zeros(enc_weight.shape, jnp.float32), g_part, feat_index * col_width, 0
    )
    stat_grads = lax.psum((jnp.sum(d_standard, 0), jnp.sum(d_standard * centred, 0)), "rows")
    d_spread = -0.5 * stat_grads[1] * factor * factor * factor
    d_mean = -factor * stat_grads[0] - 2.0 * d_spread * col_mean
    raw_grad = factor * d_standard + (d_mean + 2.0 * d_spread * raw_rows) / row_total
    summed = lax.psum(
        (
            g_encoder,
            g_enc_bias,
            g_table,
            grad_sums[0],
            grad_sums[1],
            grad_sums[2],
            grad_sums[3],
            grad_sums[4],
            grad_sums[5],
            grad_sums[6],
            grad_sums[7],
            grad_sums[8],
            grad_sums[9],
            grad_sums[10],
            grad_sums[11],
            grad_sums[12],
            grad_sums[13],
            grad_sums[14],
        ),
        ("rows", "feat"),
    )
    return (
        results.astype(jnp.bfloat16),
        raw_grad,
        summed[0],
        summed[1],
        summed[2],
        summed[3],
        summed[4],
        summed[5],
        summed[6],
        summed[7],
        summed[8],
        summed[9],
        summed[10],
        summed[11],
        summed[12],
        summed[13],
        summed[14],
        summed[15],
        summed[16],
        summed[17],
    )


def solution(mesh):
    placed = (
        P("rows", "feat"),
        P(),
        P(),
        P(),
        P(),
        P(),
        P(),
        P(),
        P(),
        P(),
        P(),
        P(),
        P(),
        P(),
        P(),
        P(),
        P(),
        P(),
        P(),
        P(("rows", "feat"), None),
        P(("rows", "feat"), None),
        P(("rows", "feat")),
        P(("rows", "feat"), None, None),
    )
    return jax.shard_map(
        body,
        mesh=mesh,
        in_specs=placed,
        out_specs=(
            P(("rows", "feat"), None, None),
            P("rows", "feat"),
            P(),
            P(),
            P(),
            P(),
            P(),
            P(),
            P(),
            P(),
            P(),
            P(),
            P(),
            P(),
            P(),
            P(),
            P(),
            P(),
            P(),
            P(),
        ),
        check_vma=False,
    )
```

profile of v0, /device:TPU:1, one launch (start us, length us, event | category | flops | bytes accessed | tf_op | source)
XLA Modules:
  0.0 907.9 jit_solution(81803885635905903)
XLA Ops:
  8.3 18.7 %all-reduce.5 = (f32[25]{0:T(128)S(1)}, f32[25]{0:T(128)S(1)}) all-reduce(f32[25]{0:T(128)S(1)} %get-tuple-element.754, f32[25]{0:T(128)S(1)} %get-tuple-element.753), channel_id=1, replica_groups=mesh['rows'=8,'feat'=4] {'rows'}, use_global_device_ids=true, to_apply=%region_3.0 | all-reduce | flops 50 | bytes 400 | tf_op jit(solution)/shard_map/psum | solution.py:194
  27.6 3.7 fusion.71
  35.4 11.1 %scatter_custom_fusion = s32[2200]{0:T(1024)S(1)} fusion(s32[2200]{0:T(1024)S(1)} %fusion.76, s32[2200]{0:T(1024)S(1)} %get-tuple-element.882, s32[]{:T(128)} %constant.160.clone.1), kind=kCustom, calls=%fused_computation.173 | custom fusion | bytes 8804 | tf_op jit(solution)/shard_map/scatter | solution.py:211
  46.6 7.8 all_to_all.19
  55.2 22.0 %reduce-scatter.2.cloned.1.call-done = f32[512,512]{1,0:T(8,128)} async-done(((f32[2048,512]{1,0:T(8,128)}), f32[512,512]{1,0:T(8,128)}) %reduce-scatter.2.cloned.1.call-update) | async-done | bytes 1048592 | tf_op jit(solution)/shard_map/reduce_scatter | solution.py:218
  78.5 7.2 gather_fusion
  87.7 5.5 all-to-all-start.1
  93.5 51.4 %all-to-all-done.1 = bf16[8,275,512]{2,1,0:T(8,128)(2,1)} async-done(((bf16[8,275,512]{2,1,0:T(8,128)(2,1)}), bf16[8,275,512]{2,1,0:T(8,128)(2,1)}, u32[]{:S(2)}, u32[]{:S(2)}) %all-to-all-start.1) | async-done | bytes 2252832 | tf_op jit(solution)/shard_map/all_to_all | solution.py:221
  147.2 7.5 gather_fusion.1
  154.7 4.2 reshape.372
  164.5 411.7 %while.45 = (s32[]{:T(128)}, f32[512,512]{1,0:T(8,128)}, f32[512]{0:T(512)}, f32[512,512]{1,0:T(8,128)}, f32[512,512]{1,0:T(8,128)}, /*index=5*/f32[512]{0:T(512...) while((s32[]{:T(128)}, f32[512,512]{1,0:T(8,128)}, ...), condition=%wide.region_30.31_spmd.clone, body=%wide.region_9.30_spmd.clone.sunk | while | flops 20458297344 | bytes 500580160 | solution.py:263
  170.3 5.2 constant_dynamic-slice_fusion.2
  175.5 8.8 fusion.217
  184.3 9.1 %fusion.218 = f32[4,1100]{1,0:T(4,128)S(1)} fusion(f32[4,1100,1000]{2,1,0:T(8,128)} %get-tuple-element.1143, f32[4,1100]{1,0:T(4,128)S(1)} %get-tuple-element.1144), kind=kLoop, calls=%fused_computation.11.clone.1 | loop fusion | flops 8795600 | bytes 17635200 | tf_op jit(solution)/shard_map/while/body/eval_jaxpr/reduce_sum | solution.py:64
  193.4 7.9 fusion.220
  219.8 10.3 %copy.186 = bf16[1,1100,512]{2,0,1:T(2,128)(2,1)} copy(bf16[1,1100,512]{2,1,0:T(8,128)(2,1)S(1)} %multiply_bitcast_fusion.2) | data formatting | bytes 2252800 | tf_op jit(solution)/shard_map/while/body/jit(dynamic_update_index_in_dim)/dynamic_update_slice | solution.py:263
  230.1 39.2 %dynamic_update_slice.23 = bf16[2,1100,512]{2,0,1:T(2,128)(2,1)} dynamic-update-slice(bf16[2,1100,512]{2,0,1:T(2,128)(2,1)} %get-tuple-element.1234, bf16[1,1100,512]{2,0,1:T(2,128)(2,1)} %copy.186, s32[]{:T(128)S(6)} %copy.207, s32[]{:T(128)} %constant.160.clone.1..sunk, s32[]{:T(128)} %constant.160.clone.1..sunk) | dynamic-update-slice | bytes 2252804 | tf_op jit(solution)/shard_map/while/body/jit(dynamic_update_index_in_dim)/dynamic_update_slice | solution.py:263
  271.4 5.7 select_add_fusion.19
  277.1 4.2 convert_reduce_fusion.11
  298.0 11.8 %convert_reduce_fusion.14 = (f32[4,128]{1,0:T(4,128)S(1)}, bf16[4,128,1000]{1,2,0:T(8,128)(2,1)}) fusion(f32[4,1100,1000]{2,1,0:T(8,128)} %get-tuple-element.1143, f32[4,1100]{1,0:T(4,128)S(1)} %log_add_fusion.2, bf16[1100,4,128]{2,1,0:T(4,128)(2,1)} %reshape.434), kind=kOutput, calls=%fused_computation.65.clone.1 | convolution fusion | flops 1136735488 | bytes 19770048 | tf_op jit(solution)/shard_map/while/body/eval_jaxpr/hsc,shd->chd/dot_general | solution.py:102
  312.2 3.4 convolution_add_fusion.20
  315.6 11.5 %multiply_reduce_fusion.18 = (f32[4,1100]{1,0:T(4,128)S(1)}, f32[4,1100,1000]{2,1,0:T(8,128)}) fusion(f32[4,1100,1000]{2,1,0:T(8,128)} %get-tuple-element.1143, f32[4,1100]{1,0:T(4,128)S(1)} %log_add_fusion.2, bf16[125,4,8,128]{3,2,1,0:T(8,128)(2,1)S(1)} %copy-done.12, bf16[1100,4,128]{2,1,0:T(4,128)(2,1)S(1)} %copy-done.3), kind=kOutput, calls=%fused_computation.7.clone.1 | convolution fusion | flops 1139595648 | bytes 37385600 | tf_op jit(solution)/shard_map/while/body/eval_jaxpr/shd,chd->hsc/dot_general | solution.py:106
  327.1 12.6 %multiply_convert_fusion.11 = bf16[4,1100,1000]{2,1,0:T(8,128)(2,1)S(1)} fusion(f32[4,1100,1000]{2,1,0:T(8,128)} %get-tuple-element.1159, f32[4,1100,1000]{2,1,0:T(8,128)} %get-tuple-element.1143, f32[4,1100]{1,0:T(4,128)S(1)} %get-tuple-element.1160, f32[4,1100]{1,0:T(4,128)S(1)} %log_add_fusion.2), kind=kLoop, calls=%fused_computation.6.clone.1 | loop fusion | flops 17600000 | bytes 44035200 | tf_op jit(solution)/shard_map/while/body/eval_jaxpr/convert_element_type | solution.py:107
  339.7 4.7 fusion.227
  344.4 3.5 convert_reduce_fusion.13
  370.9 5.2 constant_dynamic-slice_fusion.2
  376.1 8.8 fusion.217
  384.9 9.1 %fusion.218 = f32[4,1100]{1,0:T(4,128)S(1)} fusion(f32[4,1100,1000]{2,1,0:T(8,128)} %get-tuple-element.1143, f32[4,1100]{1,0:T(4,128)S(1)} %get-tuple-element.1144), kind=kLoop, calls=%fused_computation.11.clone.1 | loop fusion | flops 8795600 | bytes 17635200 | tf_op jit(solution)/shard_map/while/body/eval_jaxpr/reduce_sum | solution.py:64
  394.1 7.9 fusion.220
  420.4 10.3 %copy.186 = bf16[1,1100,512]{2,0,1:T(2,128)(2,1)} copy(bf16[1,1100,512]{2,1,0:T(8,128)(2,1)S(1)} %multiply_bitcast_fusion.2) | data formatting | bytes 2252800 | tf_op jit(solution)/shard_map/while/body/jit(dynamic_update_index_in_dim)/dynamic_update_slice | solution.py:263
  430.7 39.0 %dynamic_update_slice.23 = bf16[2,1100,512]{2,0,1:T(2,128)(2,1)} dynamic-update-slice(bf16[2,1100,512]{2,0,1:T(2,128)(2,1)} %get-tuple-element.1234, bf16[1,1100,512]{2,0,1:T(2,128)(2,1)} %copy.186, s32[]{:T(128)S(6)} %copy.207, s32[]{:T(128)} %constant.160.clone.1..sunk, s32[]{:T(128)} %constant.160.clone.1..sunk) | dynamic-update-slice | bytes 2252804 | tf_op jit(solution)/shard_map/while/body/jit(dynamic_update_index_in_dim)/dynamic_update_slice | solution.py:263
  471.8 6.3 select_add_fusion.19
  478.2 4.2 convert_reduce_fusion.11
  495.7 3.6 reshape.434
  499.3 11.8 %convert_reduce_fusion.14 = (f32[4,128]{1,0:T(4,128)S(1)}, bf16[4,128,1000]{1,2,0:T(8,128)(2,1)}) fusion(f32[4,1100,1000]{2,1,0:T(8,128)} %get-tuple-element.1143, f32[4,1100]{1,0:T(4,128)S(1)} %log_add_fusion.2, bf16[1100,4,128]{2,1,0:T(4,128)(2,1)} %reshape.434), kind=kOutput, calls=%fused_computation.65.clone.1 | convolution fusion | flops 1136735488 | bytes 19770048 | tf_op jit(solution)/shard_map/while/body/eval_jaxpr/hsc,shd->chd/dot_general | solution.py:102
  513.4 3.7 convolution_add_fusion.20
  517.2 11.5 %multiply_reduce_fusion.18 = (f32[4,1100]{1,0:T(4,128)S(1)}, f32[4,1100,1000]{2,1,0:T(8,128)}) fusion(f32[4,1100,1000]{2,1,0:T(8,128)} %get-tuple-element.1143, f32[4,1100]{1,0:T(4,128)S(1)} %log_add_fusion.2, bf16[125,4,8,128]{3,2,1,0:T(8,128)(2,1)S(1)} %copy-done.12, bf16[1100,4,128]{2,1,0:T(4,128)(2,1)S(1)} %copy-done.3), kind=kOutput, calls=%fused_computation.7.clone.1 | convolution fusion | flops 1139595648 | bytes 37385600 | tf_op jit(solution)/shard_map/while/body/eval_jaxpr/shd,chd->hsc/dot_general | solution.py:106
  528.7 12.5 %multiply_convert_fusion.11 = bf16[4,1100,1000]{2,1,0:T(8,128)(2,1)S(1)} fusion(f32[4,1100,1000]{2,1,0:T(8,128)} %get-tuple-element.1159, f32[4,1100,1000]{2,1,0:T(8,128)} %get-tuple-element.1143, f32[4,1100]{1,0:T(4,128)S(1)} %get-tuple-element.1160, f32[4,1100]{1,0:T(4,128)S(1)} %log_add_fusion.2), kind=kLoop, calls=%fused_computation.6.clone.1 | loop fusion | flops 17600000 | bytes 44035200 | tf_op jit(solution)/shard_map/while/body/eval_jaxpr/convert_element_type | solution.py:107
  541.3 4.7 fusion.227
  546.0 3.5 convert_reduce_fusion.13
  580.6 14.0 %scatter_custom_fusion.1 = bf16[2200,512]{1,0:T(8,128)(2,1)S(1)} fusion(s32[2200]{0:T(1024)} %copy-done.66, bf16[2200,512]{1,0:T(8,128)(2,1)} %reshape.402, bf16[]{:T(256)} %constant.177.clone.1), kind=kCustom, calls=%fused_computation.126 | custom fusion | bytes 2253312 | tf_op jit(solution)/shard_map/scatter | solution.py:273
  596.7 56.4 %all_to_all.20 = bf16[8,275,512]{2,1,0:T(8,128)(2,1)S(1)} all-to-all(bf16[8,275,512]{2,1,0:T(8,128)(2,1)} %reshape.370), channel_id=1, replica_groups=mesh['rows'=8,'feat'=4] {'rows'}, dimensions={0} | all-to-all | bytes 4505600 | tf_op jit(solution)/shard_map/all_to_all | solution.py:276
  655.7 16.5 %scatter_custom_fusion.2 = f32[512,512]{1,0:T(8,128)S(1)} fusion(s32[2200]{0:T(1024)} %copy-done.67, f32[2200,512]{1,0:T(8,128)} %reshape.410, f32[]{:T(128)} %constant.161.clone.1), kind=kCustom, calls=%fused_computation.130 | custom fusion | flops 1126400 | bytes 1049088 | tf_op jit(solution)/shard_map/scatter-add | solution.py:280
  673.1 22.2 %all-gather.2.cloned.1.call-done = bf16[2048,512]{1,0:T(8,128)(2,1)} async-done(((bf16[512,512]{1,0:T(8,128)(2,1)}), bf16[2048,512]{1,0:T(8,128)(2,1)}) %all-gather.2.cloned.1.call-update) | async-done | bytes 2097168 | tf_op jit(solution)/shard_map/all_gather | solution.py:284
  698.8 3.8 fusion.60
  702.7 42.0 %all-reduce.2 = (f32[512]{0:T(512)}, f32[10,512]{1,0:T(8,128)}, f32[512]{0:T(512)}, f32[512]{0:T(512)}, f32[512]{0:T(512)}, /*index=5*/f32[512]{0:T(512)}, f32[5...) all-reduce(f32[512]{0:T(512)S(1)} %get-tuple-element.880, ...), channel_id=1, replica_groups=mesh['rows'=8,'feat'=4] {'rows','feat'}, use_global_device_ids=true, to_apply=%region_39.40 | all-reduce | flops 10752 | bytes 86016 | tf_op jit(solution)/shard_map/psum | solution.py:298
  745.5 17.0 %all-reduce.4 = (f32[25]{0:T(128)S(1)}, f32[25]{0:T(128)S(1)}) all-reduce(f32[25]{0:T(128)S(1)} %get-tuple-element.752, f32[25]{0:T(128)S(1)} %get-tuple-element.751), channel_id=1, replica_groups=mesh['rows'=8,'feat'=4] {'rows'}, use_global_device_ids=true, to_apply=%region_36.37 | all-reduce | flops 50 | bytes 400 | tf_op jit(solution)/shard_map/psum | solution.py:294
  763.3 126.8 %all-reduce.8.cloned.1.call-done = (f32[100,512]{1,0:T(8,128)}, f32[512,512]{1,0:T(8,128)}, f32[512,512]{1,0:T(8,128)}, f32[512,512]{1,0:T(8,128)}, f32[512,512]...) async-done(((f32[100,512]{1,0:T(8,128)}, f32[512,512]{1,0:T(8,128)}, f32[512,512]{1,0:T(8,128)}, f32[512,512]{1,0:T(8,128)}, f32[512,512]{1,0:T(8,128)}, ...) | async-done | bytes 8593424 | tf_op jit(solution)/shard_map/psum | solution.py:298
  (466 shorter events, 163.7 us)
Async XLA Ops:
  7.2 20.4 %copy-start = (bf16[100,512]{1,0:T(8,128)(2,1)S(1)}, bf16[100,512]{1,0:T(8,128)(2,1)}, u32[]{:S(2)}) copy-start(bf16[100,512]{1,0:T(8,128)(2,1)} %param.26) | copy-start | bytes 307204
  7.2 69.9 %reduce-scatter.2.cloned.1.call-start = ((), (), s32[]{:S(2)}) async-start(), calls=%async_computation.4 | async-start | bytes 5242880 | tf_op jit(solution)/shard_map/reduce_scatter | solution.py:218
  27.1 4.3 copy-start.77
  31.4 45.8 %copy-start.76 = (f32[512]{0:T(512)S(1)}, f32[512]{0:T(512)}, u32[]{:S(2)}) copy-start(f32[512]{0:T(512)} %param.27) | copy-start | bytes 6148
  35.4 58.0 %copy-start.66 = (s32[2200]{0:T(1024)}, s32[2200]{0:T(1024)S(1)}, u32[]{:S(2)}) copy-start(s32[2200]{0:T(1024)S(1)} %fusion.76) | copy-start | bytes 26404
  87.7 5.7 copy-start.91
  87.7 57.2 %all-to-all-start.1 = ((bf16[8,275,512]{2,1,0:T(8,128)(2,1)}), bf16[8,275,512]{2,1,0:T(8,128)(2,1)}, u32[]{:S(2)}, u32[]{:S(2)}) async-start(bf16[8,275,512]{2,1,0:T(8,128)(2,1)} %reshape.368), calls=%async_computation.2 | async-start | bytes 4587520 | tf_op jit(solution)/shard_map/all_to_all | solution.py:221
  93.1 602.2 %all-gather.2.cloned.1.call-start = ((), (), s32[]{:S(2)}) async-start(), calls=%async_computation.5 | async-start | bytes 2621440 | tf_op jit(solution)/shard_map/all_gather | solution.py:284
  154.7 4.2 copy-start.69
  154.7 4.2 copy-start.71
  169.1 6.4 copy-start.5
  184.3 9.1 %copy-start.11 = (bf16[125,4,8,128]{3,2,1,0:T(8,128)(2,1)S(1)}, bf16[125,4,8,128]{3,2,1,0:T(8,128)(2,1)}, u32[]{:S(2)}) copy-start(bf16[125,4,8,128]{3,2,1,0:T(8,128)(2,1)} %fusion.219) | copy-start | bytes 3072004 | tf_op jit(solution)/shard_map/while
  206.0 77.7 %copy-start.1 = (f32[1100,512]{1,0:T(8,128)}, f32[1100,512]{1,0:T(8,128)S(1)}, u32[]{:S(2)}) copy-start(f32[1100,512]{1,0:T(8,128)S(1)} %get-tuple-element.1145) | copy-start | bytes 6758404 | tf_op jit(solution)/shard_map/while
  269.3 7.8 slice-start.1
  271.4 5.7 copy-start.82
  271.4 5.7 slice-start.2
  277.1 4.3 copy-start.4
  277.1 4.3 copy-start.62
  277.1 4.3 copy-start.80
  292.8 5.2 copy-start.50
  292.8 5.2 copy-start.53
  339.7 4.7 copy-start.6
  347.9 4.5 copy-start.56
  348.0 4.5 copy-start.59
  369.7 6.4 copy-start.5
  384.9 9.1 %copy-start.11 = (bf16[125,4,8,128]{3,2,1,0:T(8,128)(2,1)S(1)}, bf16[125,4,8,128]{3,2,1,0:T(8,128)(2,1)}, u32[]{:S(2)}) copy-start(bf16[125,4,8,128]{3,2,1,0:T(8,128)(2,1)} %fusion.219) | copy-start | bytes 3072004 | tf_op jit(solution)/shard_map/while
  406.6 78.1 %copy-start.1 = (f32[1100,512]{1,0:T(8,128)}, f32[1100,512]{1,0:T(8,128)S(1)}, u32[]{:S(2)}) copy-start(f32[1100,512]{1,0:T(8,128)S(1)} %get-tuple-element.1145) | copy-start | bytes 6758404 | tf_op jit(solution)/shard_map/while
  469.7 8.4 slice-start.1
  471.7 6.4 copy-start.82
  471.8 6.4 slice-start.2
  478.1 4.3 copy-start.4
  478.1 4.3 copy-start.62
  478.1 4.3 copy-start.80
  493.9 5.4 copy-start.50
  493.9 5.4 copy-start.53
  541.3 4.7 copy-start.6
  549.5 4.9 copy-start.56
  549.5 4.8 copy-start.59
  655.6 39.7 %copy-start.21 = (f32[2048,25]{0,1:T(8,128)S(1)}, f32[2048,25]{0,1:T(8,128)}, u32[]{:S(2)}) copy-start(f32[2048,25]{0,1:T(8,128)} %param.25) | copy-start | bytes 614404
  655.7 39.7 %copy-start.73 = (f32[25]{0:T(128)S(1)}, f32[25]{0:T(128)}, u32[]{:S(2)}) copy-start(f32[25]{0:T(128)} %copy-done.72) | copy-start | bytes 304
  655.7 39.7 %copy-start.75 = (f32[25]{0:T(128)S(1)}, f32[25]{0:T(128)}, u32[]{:S(2)}) copy-start(f32[25]{0:T(128)} %copy-done.74) | copy-start | bytes 304
  673.1 217.1 %all-reduce.8.cloned.1.call-start = ((), (), s32[]{:S(2)}) async-start(), calls=%async_computation.6 | async-start | bytes 17203200 | tf_op jit(solution)/shard_map/psum | solution.py:298
  698.7 3.9 copy-start.45
  698.8 3.9 copy-start.48
  698.8 45.9 %copy-start.20 = (bf16[2048,512]{1,0:T(8,128)(2,1)S(1)}, bf16[2048,512]{1,0:T(8,128)(2,1)}, u32[]{:S(2)}) copy-start(bf16[2048,512]{1,0:T(8,128)(2,1)} %all-gather.2.cloned.1.call-done) | copy-start | bytes 6291460
  702.6 59.9 %copy-start.78 = (f32[25]{0:T(128)S(1)}, f32[25]{0:T(128)}, u32[]{:S(2)}) copy-start(f32[25]{0:T(128)} %copy-done.77) | copy-start | bytes 304
  890.2 4.0 copy-start.28
  890.2 5.0 copy-start.27
  (109 other events, 270.7 us)
Sparse Core Ops, SparseCore 0:
  31.5 45.5 reduce-scatter.1
  673.2 22.0 all-gather.1
  704.6 185.5 all-reduce.7
where the time goes:
time: 925 us; the launch traced here: 908 us
  local copies, waits for them, and re-layouts  223 us (24%)
  waiting for transfers between devices  222 us (24%)
  matrix products  196 us (21%)
  blocking collectives  142 us (15%)
  other arithmetic  92.6 us (10%)
  between operations  14.8 us (2%)
  loops' own time  11.7 us (1%)
    psum x1, waiting for transfers between devices, body(): lax.psum((g_encoder, g_enc_bias, g_table, grad_sums[0], grad_sums[1], gra...  127 us
    dynamic_update_slice x4, local copies, waits for them, and re-layouts, body(): lax.scan(layer_step, start_sums, (stream_in, live_mask, cotangent))  98.8 us
    dot_general x37, matrix products, product(): return jnp.dot(left, right, preferred_element_type=jnp.float32)  89.9 us
    all_to_all x1, blocking collectives, body(): lax.all_to_all(sending, 'rows', split_axis=0, concat_axis=0, tiled=True)  56.4 us
    all_to_all x1, waiting for transfers between devices, body(): lax.all_to_all(outgoing, 'rows', split_axis=0, concat_axis=0, tiled=True)  51.4 us
    psum x1, blocking collectives, body(): lax.psum((g_encoder, g_enc_bias, g_table, grad_sums[0], grad_sums[1], gra...  42 us
    convert_element_type x2, other arithmetic, block_pass(): (prob_values * (d_probs - jnp.sum(d_probs * prob_values, -1, keepdims=Tru...  25.1 us
    dot_general x2, matrix products, block_pass(): jnp.einsum('hsc,shd->chd', prob_again, d_mixed, preferred_element_type=jn...  23.6 us
  transfers between devices with their start and end apart: 4, of which 4 were waited for; matrix products, arithmetic and copies ran while one was open for 2% of the time, Pallas kernels for 0%

commit v1 on v0

v1 whole, which is shorter than its diff:
```python
import functools
import math

import jax
import jax.numpy as jnp
from jax import lax
from jax.experimental import pallas as pl
from jax.experimental.pallas import tpu as pltpu
from jax.sharding import PartitionSpec as P

HEADS = 4
LANES = 128
epsilon = 1e-05
CHUNKS = 32
VMEM_LIMIT = 60 * 1024 * 1024
f32 = jnp.float32
bf16 = jnp.bfloat16


def dot(left, right):
    return jnp.dot(left, right, preferred_element_type=f32)


def dot_nt(left, right):
    return lax.dot_general(left, right, (((1,), (1,)), ((), ())), preferred_element_type=f32)


def dot_tn(left, right):
    return lax.dot_general(left, right, (((0,), (0,)), ((), ())), preferred_element_type=f32)


def round_up(value, unit):
    return -(-value // unit) * unit


def row_chunks(span):
    for parts in (3, 2, 1):
        if span % (16 * parts) == 0:
            return parts
    return 1


def params(*names):
    return pltpu.CompilerParams(vmem_limit_bytes=VMEM_LIMIT, dimension_semantics=("arbitrary",) * len(names))


def embed(feats, w_feat, w_mark, b_enc):
    slots = (dot(feats, w_feat[...]) + b_enc[...]).astype(bf16)
    return slots.astype(f32) + dot(feats, w_mark[...])


def attend_kernel(span, ctx_len, ctx_pad, feat_total, classes, parts,
                  ids, groups, mark, w_feat, w_mark, b_enc, w_query, b_query, w_key, w_value, b_value,
                  feats_o, low_o, q_o, k_o, v_o, e_o, inv_o, mix_o, table, rows_f):
    block = pl.program_id(0)
    head = pl.program_id(1)
    pad = feats_o.shape[1]
    step = pad // parts

    @pl.when((head == 0) & (block == 0))
    def _():
        count, deep, own = groups.shape

        def unfold(g, _):
            piece = jnp.concatenate([groups[g].astype(f32), jnp.zeros((LANES - deep, own), f32)], 0)
            table[pl.ds(pl.multiple_of(g * own, own), own), :] = piece.T
            return 0

        lax.fori_loop(0, count, unfold, 0)

    @pl.when(head == 0)
    def _():
        rows_f[pad - 16:, :] = jnp.zeros((16, LANES), f32)

        def fetch(i, _):
            for u in range(10):
                at = i * 10 + u
                rows_f[pl.ds(at, 1), :] = table[pl.ds(ids[block, at], 1), :]
            return 0

        lax.fori_loop(0, span // 10, fetch, 0)
        for at in range(span // 10 * 10, span):
            rows_f[pl.ds(at, 1), :] = table[pl.ds(ids[block, at], 1), :]

        def project(c, _):
            rows = pl.ds(pl.multiple_of(c * step, 16), step)
            lane = lax.broadcasted_iota(jnp.int32, (step, LANES), 1)
            hot = (lane == mark[0, rows, :] + feat_total) | (lane == feat_total + classes)
            feats = jnp.where(lane < feat_total, rows_f[rows, :], hot.astype(f32)).astype(bf16)
            feats_o[0, rows, :] = feats
            low = embed(feats, w_feat, w_mark, b_enc).astype(bf16)
            low_o[0, rows, :] = low
            q_o[0, rows, :] = (dot(low, w_query[...]) + b_query[...]).astype(bf16)
            k_o[0, rows, :] = dot(low, w_key[...]).astype(bf16)
            v_o[0, rows, :] = (dot(low, w_value[...]) + b_value[...]).astype(bf16)
            return 0

        lax.fori_loop(0, parts, project, 0)

    width = q_o.shape[2] // HEADS
    factor = math.log2(math.e) / math.sqrt(width)
    cols = pl.ds(pl.multiple_of(head * width, LANES), width)
    keys = k_o[0, :ctx_pad, cols]
    vals = jnp.concatenate([v_o[0, :ctx_pad, cols], jnp.ones((ctx_pad, width), bf16)], 1)
    edge = ctx_len // LANES * LANES
    for c in range(parts):
        rows = slice(c * step, (c + 1) * step)
        scores = dot_nt(q_o[0, rows, cols], keys)
        head_part = scores[:, :edge]
        most = jnp.max(head_part, 1, keepdims=True)
        if edge < ctx_pad:
            lane = lax.broadcasted_iota(jnp.int32, (step, ctx_pad - edge), 1)
            tail_part = jnp.where(lane < ctx_len - edge, scores[:, edge:], -1e30)
            most = jnp.maximum(most, jnp.max(tail_part, 1, keepdims=True))
            e_o[0, 0, rows, edge:] = jnp.exp2((tail_part - most) * factor).astype(bf16)
        e_o[0, 0, rows, :edge] = jnp.exp2((head_part - most) * factor).astype(bf16)
        summed = dot(e_o[0, 0, rows, :], vals)
        inverse = 1.0 / summed[:, width:]
        inv_o[0, rows, cols] = inverse
        mix_o[0, rows, cols] = (summed[:, :width] * inverse).astype(bf16)


def norm_parts(values):
    centre = jnp.mean(values, -1, keepdims=True)
    offset = values - centre
    second = jnp.mean(offset * offset, -1, keepdims=True)
    root = lax.rsqrt(second + epsilon)
    return offset * root, root


def norm_back(grad, unit, root):
    return root * (grad - jnp.mean(grad, -1, keepdims=True) - unit * jnp.mean(grad * unit, -1, keepdims=True))


def middle_kernel(ctx_len,
                  place, queries, feats, mixed, inv, cot, w_feat, w_mark, b_enc, w_out, b_out, gain_one, shift_one, w_in, b_in,
                  w_back, b_back, gain_two, shift_two,
                  out_o, first_o, dox_o, grads_o, wide_o, narrow_o,
                  g_out, g_in, g_back, wide, narrow):
    block = pl.program_id(0)
    part = pl.program_id(1)
    step = feats.shape[1]
    width = mixed.shape[2] // HEADS

    @pl.when((block == 0) & (part == 0))
    def _():
        g_out[...] = jnp.zeros_like(g_out)
        g_in[...] = jnp.zeros_like(g_in)
        g_back[...] = jnp.zeros_like(g_back)
        wide[...] = jnp.zeros_like(wide)
        narrow[...] = jnp.zeros_like(narrow)

    mixed_low = mixed[0]
    stream = embed(feats[0], w_feat, w_mark, b_enc)
    unit_one, root_one = norm_parts(stream + dot(mixed_low, w_out[...]) + b_out[...])
    normed = unit_one * gain_one[...] + shift_one[...]
    normed_low = normed.astype(bf16)
    hidden = dot(normed_low, w_in[...]) + b_in[...]
    inner = math.sqrt(2.0 / math.pi)
    square = hidden * hidden
    curve = jnp.tanh(hidden * (inner + (inner * 0.044715) * square))
    half = 0.5 * curve + 0.5
    active_low = (hidden * half).astype(bf16)
    slope = half + (0.5 * hidden) * (1.0 - curve * curve) * (inner + (3.0 * inner * 0.044715) * square)
    branch = dot(active_low, w_back[...]) + b_back[...]
    unit_two, root_two = norm_parts(normed + branch)
    row = part * step + lax.broadcasted_iota(jnp.int32, (step, 1), 0)
    alive = row < ctx_len + queries[block]
    out_o[0] = jnp.where(alive, unit_two * gain_two[...] + shift_two[...], 0.0).astype(bf16)
    grad = jnp.where(alive, cot[0], 0.0)
    second = norm_back(grad * gain_two[...], unit_two, root_two)
    branch_low = second.astype(bf16)
    g_back[...] += dot_tn(active_low, branch_low)
    hidden_low = (slope * dot_nt(branch_low, w_back[...])).astype(bf16)
    g_in[...] += dot_tn(normed_low, hidden_low)
    grad_one = second + dot_nt(hidden_low, w_in[...])
    first = norm_back(grad_one * gain_one[...], unit_one, root_one)
    first_o[0] = first
    first_low = first.astype(bf16)
    g_out[...] += dot_tn(mixed_low, first_low)
    back = dot_nt(first_low, w_out[...]).astype(bf16).astype(f32) * inv[0]
    lane = lax.broadcasted_iota(jnp.int32, (step, width), 1)
    for head in range(HEADS):
        cols = slice(head * width, (head + 1) * width)
        scaled = back[:, cols].astype(bf16)
        shift = -jnp.sum(scaled.astype(f32) * mixed_low[:, cols].astype(f32), 1, keepdims=True)
        top = shift.astype(bf16).astype(f32)
        extra = jnp.where(lane == 0, top, jnp.where(lane == 1, shift - top, 0.0))
        dox_o[0, head, :, :width] = scaled
        dox_o[0, head, :, width:] = extra.astype(bf16)
    total = lambda v: jnp.sum(v, 0, keepdims=True)
    wide[0:1, :] += total(hidden_low.astype(f32))
    narrow[0:1, :] += total(first_low.astype(f32))
    narrow[1:2, :] += total(grad_one * unit_one)
    narrow[2:3, :] += total(grad_one)
    narrow[3:4, :] += total(branch_low.astype(f32))
    narrow[4:5, :] += total(grad * unit_two)
    narrow[5:6, :] += total(grad)

    @pl.when((block == pl.num_programs(0) - 1) & (part == pl.num_programs(1) - 1))
    def _():
        model = g_out.shape[1]

        def lay(p, _):
            at = pl.multiple_of((p ^ place[0]) * 16, 16)
            grads_o[p, 0:16, :] = g_out[pl.ds(at, 16), :].astype(bf16)
            for j in range(2):
                grads_o[p, 16 + 16 * j:32 + 16 * j, :] = g_in[pl.ds(at, 16), j * model:(j + 1) * model].astype(bf16)
            grads_o[p, 48:80, :] = g_back[pl.ds(pl.multiple_of(at * 2, 32), 32), :].astype(bf16)
            return 0

        lax.fori_loop(0, CHUNKS, lay, 0)
        wide_o[...] = wide[...]
        narrow_o[...] = narrow[...]


def scores_kernel(ctx_pad, parts,
                  place, e, q, k, v, dox, low, d_o, g_o, bias_o, ds, g_scr, bias_scr):
    block = pl.program_id(0)
    pad = q.shape[1]
    step = pad // parts
    width = q.shape[2]
    root = 1.0 / math.sqrt(width)
    keys = k[0, :ctx_pad, :]
    vals = jnp.concatenate([v[0, :ctx_pad, :], jnp.ones((ctx_pad, width), bf16)], 1)
    for c in range(parts):
        rows = slice(c * step, (c + 1) * step)
        d_probs = dot_nt(dox[0, 0, rows, :], vals)
        ds[rows, :] = e[0, 0, rows, :] * d_probs.astype(bf16)
        d_o[0, 0, rows, :width] = (dot(ds[rows, :], keys) * root).astype(bf16)
    d_o[0, 0, :ctx_pad, width:2 * width] = (dot_tn(ds[...], q[0]) * root).astype(bf16)
    d_o[0, 0, :ctx_pad, 2 * width:] = dot_tn(e[0, 0], dox[0, 0, :, :width]).astype(bf16)
    d_o[0, 0, ctx_pad:, width:] = jnp.zeros((pad - ctx_pad, 2 * width), bf16)
    grads = dot_tn(low[0], d_o[0, 0])
    sums = jnp.sum(d_o[0, 0].astype(f32), 0, keepdims=True)

    @pl.when(block == 0)
    def _():
        g_scr[...] = grads
        bias_scr[...] = jnp.broadcast_to(sums, bias_scr.shape)

    @pl.when(block > 0)
    def _():
        g_scr[...] += grads
        bias_scr[...] += jnp.broadcast_to(sums, bias_scr.shape)

    @pl.when(block == pl.num_programs(0) - 1)
    def _():
        def lay(p, _):
            at = pl.multiple_of((p ^ place[0]) * 16, 16)
            g_o[p] = g_scr[pl.ds(at, 16), :].astype(bf16)
            return 0

        lax.fori_loop(0, CHUNKS, lay, 0)
        bias_o[...] = bias_scr[...]


def attend(ids, groups, mark, w_feat, w_mark, b_enc, w_query, b_query, w_key, w_value, b_value, ctx_len, feat_total, classes):
    blocks, span = ids.shape
    pad = mark.shape[1]
    model = w_query.shape[0]
    ctx_pad = round_up(ctx_len, LANES)
    parts = row_chunks(pad)
    whole = lambda a: pl.BlockSpec(a.shape, lambda *_: (0,) * a.ndim)
    per = lambda w: pl.BlockSpec((1, pad, w), lambda b, h, *_: (b, 0, 0))
    kernel = functools.partial(attend_kernel, span, ctx_len, ctx_pad, feat_total, classes, parts)
    shape = lambda *s: jax.ShapeDtypeStruct(s, bf16)
    return pl.pallas_call(
        kernel,
        grid_spec=pltpu.PrefetchScalarGridSpec(
            num_scalar_prefetch=1,
            grid=(blocks, HEADS),
            in_specs=[whole(groups), per(1)] + [whole(a) for a in (w_feat, w_mark, b_enc, w_query, b_query, w_key, w_value, b_value)],
            out_specs=[per(LANES), per(model), per(model), per(model), per(model),
                       pl.BlockSpec((1, 1, pad, ctx_pad), lambda b, h, *_: (b, h, 0, 0)), per(model), per(model)],
            scratch_shapes=[pltpu.VMEM((groups.shape[0] * groups.shape[2], LANES), f32), pltpu.VMEM((pad, LANES), f32)],
        ),
        out_shape=[shape(blocks, pad, LANES), shape(blocks, pad, model), shape(blocks, pad, model), shape(blocks, pad, model),
                   shape(blocks, pad, model), shape(blocks, HEADS, pad, ctx_pad),
                   jax.ShapeDtypeStruct((blocks, pad, model), f32), shape(blocks, pad, model)],
        compiler_params=params(0, 0),
        name="attend",
    )(ids, groups, mark, w_feat, w_mark, b_enc, w_query, b_query, w_key, w_value, b_value)


def middle(place, queries, feats, mixed, inv, cot, weights, ctx_len):
    blocks, pad, model = mixed.shape
    span = cot.shape[1]
    parts = row_chunks(pad)
    step = pad // parts
    inner = weights[7].shape[1]
    whole = lambda a: pl.BlockSpec(a.shape, lambda *_: (0,) * a.ndim)
    full = lambda *s: pl.BlockSpec(s, lambda *_: (0,) * len(s))
    per = lambda w: pl.BlockSpec((1, step, w), lambda b, c, *_: (b, c, 0))
    grads = [(model, model), (model, inner), (inner, model)]
    return pl.pallas_call(
        functools.partial(middle_kernel, ctx_len),
        grid_spec=pltpu.PrefetchScalarGridSpec(
            num_scalar_prefetch=2,
            grid=(blocks, parts),
            in_specs=[per(LANES), per(model), per(model), per(model)] + [whole(a) for a in weights],
            out_specs=[per(model), per(model),
                       pl.BlockSpec((1, HEADS, step, 2 * model // HEADS), lambda b, c, *_: (b, 0, c, 0))]
            + [full(CHUNKS, 80, model), full(8, inner), full(8, model)],
            scratch_shapes=[pltpu.VMEM(s, f32) for s in grads] + [pltpu.VMEM((8, inner), f32), pltpu.VMEM((8, model), f32)],
        ),
        out_shape=[jax.ShapeDtypeStruct((blocks, span, model), bf16), jax.ShapeDtypeStruct((blocks, pad, model), f32),
                   jax.ShapeDtypeStruct((blocks, HEADS, pad, 2 * model // HEADS), bf16)]
        + [jax.ShapeDtypeStruct((CHUNKS, 80, model), bf16)]
        + [jax.ShapeDtypeStruct((8, inner), f32), jax.ShapeDtypeStruct((8, model), f32)],
        compiler_params=params(0, 0),
        name="middle",
    )(place, queries, feats, mixed, inv, cot, *weights)


def score_grads(place, head, e, q, k, v, dox, low):
    blocks, pad, model = q.shape
    ctx_pad = e.shape[3]
    width = model // HEADS
    parts = row_chunks(pad)
    col = pl.BlockSpec((1, pad, width), lambda b, *_: (b, 0, head))
    return pl.pallas_call(
        functools.partial(scores_kernel, ctx_pad, parts),
        grid_spec=pltpu.PrefetchScalarGridSpec(
            num_scalar_prefetch=1,
            grid=(blocks,),
            in_specs=[pl.BlockSpec((1, 1, pad, ctx_pad), lambda b, *_: (b, head, 0, 0)), col, col, col,
                      pl.BlockSpec((1, 1, pad, 2 * width), lambda b, *_: (b, head, 0, 0)),
                      pl.BlockSpec((1, pad, model), lambda b, *_: (b, 0, 0))],
            out_specs=[pl.BlockSpec((1, 1, pad, 3 * width), lambda b, *_: (b, 0, 0, 0)),
                       pl.BlockSpec((CHUNKS, 16, 3 * width), lambda b, *_: (0, 0, 0)),
                       pl.BlockSpec((8, 3 * width), lambda b, *_: (0, 0))],
            scratch_shapes=[pltpu.VMEM((pad, ctx_pad), bf16), pltpu.VMEM((model, 3 * width), f32), pltpu.VMEM((8, 3 * width), f32)],
        ),
        out_shape=[jax.ShapeDtypeStruct((blocks, 1, pad, 3 * width), bf16),
                   jax.ShapeDtypeStruct((CHUNKS, 16, 3 * width), bf16), jax.ShapeDtypeStruct((8, 3 * width), f32)],
        compiler_params=params(0),
        name="score_grads",
    )(place, e, q, k, v, dox, low)


def stream_kernel(feat_total, place, first, *refs):
    d_refs, refs = refs[:HEADS], refs[HEADS:]
    wts, feats, w_aug_t, narrow, wide = refs[:5]
    biases, refs = refs[5:5 + HEADS], refs[5 + HEADS:]
    rows_o, tail_o, aug, sums = refs
    block = pl.program_id(0)
    part = pl.program_id(1)
    model = first.shape[2]
    width = model // HEADS

    total = first[0]
    for head in range(HEADS):
        total = total + dot(d_refs[head][0, 0], wts[head])
    low = total.astype(bf16)

    @pl.when((block == 0) & (part == 0))
    def _():
        aug[...] = jnp.zeros_like(aug)
        sums[...] = jnp.zeros_like(sums)

    aug[:LANES, :] += dot_tn(feats[0], low)
    d_feats = dot(low, w_aug_t[...])
    rows_o[0] = d_feats
    sums[0:1, :] += jnp.sum(d_feats, 0, keepdims=True)
    sums[1:2, :] += jnp.sum(d_feats * feats[0].astype(f32), 0, keepdims=True)

    @pl.when((block == pl.num_programs(0) - 1) & (part == pl.num_programs(1) - 1))
    def _():
        aug[LANES:LANES + 6, :] = narrow[0:6, :]
        aug[LANES + 6:LANES + 7, :] = wide[0:1, :model]
        aug[LANES + 7:LANES + 8, :] = wide[0:1, model:]
        for head in range(HEADS):
            cols = slice(head * width, (head + 1) * width)
            aug[LANES + 8:LANES + 9, cols] = biases[head][0:1, :width]
            aug[LANES + 9:LANES + 10, cols] = biases[head][0:1, 2 * width:]
        for j in range(2):
            aug[LANES + 10:LANES + 11, j * LANES:(j + 1) * LANES] = sums[j:j + 1, :]
        half = model // 2

        def lay(p, _):
            at = p ^ place[0]
            rows = pl.ds(pl.multiple_of(at // 2 * 16, 16), 16)
            tail_o[p] = aug[rows, pl.ds(pl.multiple_of(at % 2 * half, half), half)].astype(bf16)
            return 0

        lax.fori_loop(0, CHUNKS, lay, 0)


def stream_grads(place, first, d_parts, wts, feats, w_aug_t, narrow, wide, biases, feat_total):
    blocks, pad, model = first.shape
    parts = row_chunks(pad)
    step = pad // parts
    per = lambda w: pl.BlockSpec((1, step, w), lambda b, c, *_: (b, c, 0))
    d_spec = pl.BlockSpec((1, 1, step, d_parts[0].shape[3]), lambda b, c, *_: (b, 0, c, 0))
    whole = lambda a: pl.BlockSpec(a.shape, lambda *_: (0,) * a.ndim)
    return pl.pallas_call(
        functools.partial(stream_kernel, feat_total),
        grid_spec=pltpu.PrefetchScalarGridSpec(
            num_scalar_prefetch=1,
            grid=(blocks, parts),
            in_specs=[per(model)] + [d_spec] * HEADS + [whole(wts), per(LANES), whole(w_aug_t), whole(narrow), whole(wide)]
            + [whole(b) for b in biases],
            out_specs=[per(LANES), pl.BlockSpec((CHUNKS, 16, model // 2), lambda *_: (0, 0, 0))],
            scratch_shapes=[pltpu.VMEM((2 * LANES, model), f32), pltpu.VMEM((8, LANES), f32)],
        ),
        out_shape=[jax.ShapeDtypeStruct((blocks, pad, LANES), f32), jax.ShapeDtypeStruct((CHUNKS, 16, model // 2), bf16)],
        compiler_params=params(0, 0),
        name="stream_grads",
    )(place, first, *d_parts, wts, feats, w_aug_t, narrow, wide, *biases)


def spread_kernel(span, own, ids, rows, out_o, *tables):
    blocks = rows.shape[0]
    count = out_o.shape[0]
    deep = out_o.shape[1]
    for table in tables:
        table[...] = jnp.zeros_like(table)
    each = len(tables) // blocks if len(tables) > 1 else 1
    run = span // each
    unit = next(u for u in (10, 5, 2, 1) if run % u == 0)

    def add(i, _):
        for u in range(unit):
            for t in range(blocks * each):
                block, at = t // each, t % each * run + i * unit + u
                table = tables[t % len(tables)]
                spot = pl.ds(ids[block, at], 1)
                table[spot, :] += rows[block, pl.ds(at, 1), :]
        return 0

    lax.fori_loop(0, run // unit, add, 0)

    def fold(g, _):
        spot = pl.ds(pl.multiple_of(g * own, own), own)
        total = tables[0][spot, :]
        for table in tables[1:]:
            total = total + table[spot, :]
        out_o[g] = total.T[:deep].astype(bf16)
        return 0

    lax.fori_loop(0, count, fold, 0)


def spread(ids, rows, count, deep, own):
    span = ids.shape[1]
    tables = 4 if count <= 8 and span % 2 == 0 else 1
    return pl.pallas_call(
        functools.partial(spread_kernel, span, own),
        grid_spec=pltpu.PrefetchScalarGridSpec(
            num_scalar_prefetch=1,
            grid=(1,),
            in_specs=[pl.BlockSpec(rows.shape, lambda *_: (0, 0, 0))],
            out_specs=pl.BlockSpec((count, deep, own), lambda *_: (0, 0, 0)),
            scratch_shapes=[pltpu.VMEM((count * own, LANES), f32)] * tables,
        ),
        out_shape=jax.ShapeDtypeStruct((count, deep, own), bf16),
        compiler_params=params(0),
        name="spread",
    )(ids, rows)


def finish_kernel(place, grads, out_o, in_o, back_o):
    step = pl.program_id(0)
    model = out_o.shape[1]
    for u in range(out_o.shape[0] // 16):
        p = (step * (out_o.shape[0] // 16) + u) ^ place[0]
        rows = slice(u * 16, (u + 1) * 16)
        out_o[rows, :] = grads[p, 0:16, :].astype(f32)
        for j in range(2):
            in_o[rows, j * model:(j + 1) * model] = grads[p, 16 + 16 * j:32 + 16 * j, :].astype(f32)
        back_o[u * 32:(u + 1) * 32, :] = grads[p, 48:80, :].astype(f32)


def finish(place, grads):
    model = grads.shape[2]
    steps = 8
    shapes = [(model, model), (model, 2 * model), (2 * model, model)]
    return pl.pallas_call(
        finish_kernel,
        grid_spec=pltpu.PrefetchScalarGridSpec(
            num_scalar_prefetch=1,
            grid=(steps,),
            in_specs=[pl.BlockSpec(grads.shape, lambda *_: (0, 0, 0))],
            out_specs=[pl.BlockSpec((s[0] // steps, s[1]), lambda i, *_: (i, 0)) for s in shapes],
        ),
        out_shape=[jax.ShapeDtypeStruct(s, f32) for s in shapes],
        compiler_params=params(0),
        name="finish",
    )(place, grads)


def finish_tail_kernel(place, heads, tail, q_o, k_o, v_o, aug_o):
    step = pl.program_id(0)
    model = q_o.shape[1]
    width = model // HEADS
    half = model // 2
    for u in range(q_o.shape[0] // 16):
        p = (step * (q_o.shape[0] // 16) + u) ^ place[0]
        rows = slice(u * 16, (u + 1) * 16)
        for head in range(HEADS):
            cols = slice(head * width, (head + 1) * width)
            for j, ref in enumerate((q_o, k_o, v_o)):
                at = (head * 3 + j) * width
                ref[rows, cols] = heads[p, :, at:at + width].astype(f32)
        row = pl.ds(pl.multiple_of(u // 2 * 16, 16), 16)
        aug_o[row, (u % 2) * half:(u % 2 + 1) * half] = tail[p].astype(f32)


def finish_tail(place, heads, tail):
    model = tail.shape[2] * 2
    steps = 8
    shapes = [(model, model)] * 3 + [(2 * LANES, model)]
    return pl.pallas_call(
        finish_tail_kernel,
        grid_spec=pltpu.PrefetchScalarGridSpec(
            num_scalar_prefetch=1,
            grid=(steps,),
            in_specs=[pl.BlockSpec(heads.shape, lambda *_: (0, 0, 0)), pl.BlockSpec(tail.shape, lambda *_: (0, 0, 0))],
            out_specs=[pl.BlockSpec((s[0] // steps, s[1]), lambda i, *_: (i, 0)) for s in shapes],
        ),
        out_shape=[jax.ShapeDtypeStruct(s, f32) for s in shapes],
        compiler_params=params(0),
        name="finish_tail",
    )(place, heads, tail)


def swap(value, axis, bit):
    size = lax.axis_size(axis)
    return lax.ppermute(value, axis, [(i, i ^ bit) for i in range(size)])


def axis_bits(axis):
    return [(axis, 1 << b) for b in range(lax.axis_size(axis).bit_length() - 1)]


def sum_over(value, bits):
    for axis, bit in bits:
        value = value + swap(value, axis, bit)
    return value


def reduce_chunks(value, bits):
    split = CHUNKS.bit_length() - 1
    total = value
    for axis, bit in bits[:split]:
        half = total.shape[0] // 2
        came = swap(total[half:].astype(bf16), axis, bit)
        total = total[:half].astype(f32) + came.astype(f32)
    for axis, bit in bits[split:]:
        low = total.astype(bf16)
        total = low.astype(f32) + swap(low, axis, bit).astype(f32)
    return total.astype(bf16)


def gather_chunks(value, bits):
    for axis, bit in reversed(bits[:CHUNKS.bit_length() - 1]):
        value = jnp.concatenate([value, swap(value, axis, bit)], 0)
    return value


def body(
    raw_rows, enc_weight, enc_bias, label_table, w_query, b_query, w_key, w_value, b_value, w_out, b_out,
    gain_one, shift_one, w_in, b_in, w_back, b_back, gain_two, shift_two, members, labels, queries, cotangent,
):
    row_count = lax.axis_size("rows")
    feat_count = lax.axis_size("feat")
    row_index = lax.axis_index("rows")
    feat_index = lax.axis_index("feat")
    local_rows, col_width = raw_rows.shape
    own_rows = local_rows // feat_count
    feat_total = col_width * feat_count
    model = enc_weight.shape[1]
    classes = label_table.shape[0]
    blocks, span = members.shape
    ctx_len = labels.shape[1]
    pad = round_up(span, 16)
    row_total = float(local_rows * row_count)
    row_bits = axis_bits("rows")
    bits = axis_bits("feat") + row_bits
    place = jnp.int32(0)
    for at, (axis, bit) in enumerate(bits[:CHUNKS.bit_length() - 1]):
        has = (lax.axis_index(axis) // bit) % 2
        place = place + has * (CHUNKS >> (at + 1))
    place = place.reshape(1).astype(jnp.int32)
    row = lambda a: a.reshape(1, -1)

    columns = raw_rows.T
    sums = jnp.stack([jnp.sum(columns, 1), jnp.sum(columns * columns, 1)])
    sums = sum_over(sums, row_bits)
    col_mean = sums[0] / row_total
    factor = lax.rsqrt(sums[1] / row_total - col_mean * col_mean + epsilon)
    standard = ((columns - col_mean[:, None]) * factor[:, None]).astype(bf16)
    standard = standard.reshape(col_width, feat_count, own_rows).transpose(1, 0, 2)
    owned = lax.all_to_all(standard, "feat", split_axis=0, concat_axis=0, tiled=True).reshape(1, feat_total, own_rows)
    groups = owned
    for axis, bit in reversed(row_bits):
        groups = jnp.concatenate([groups, swap(groups, axis, bit)], 0)
    source = (members // local_rows) ^ row_index
    spot = jnp.zeros_like(source)
    for at in range(len(row_bits)):
        spot = spot + ((source >> at) & 1) * (row_count >> (at + 1))
    ids = spot * own_rows + members % own_rows

    w_feat = jnp.pad(enc_weight, ((0, LANES - feat_total), (0, 0)))
    w_mark = jnp.pad(label_table, ((feat_total, LANES - feat_total - classes), (0, 0)))
    b_enc = row(enc_bias)
    mark = jnp.pad(labels, ((0, 0), (0, pad - ctx_len)), constant_values=-2 * LANES)[:, :, None]
    feats, low, qry, key, val, expo, inv, mixed = attend(
        ids, groups, mark, w_feat, w_mark, b_enc, w_query, row(b_query), w_key, w_value, row(b_value), ctx_len, feat_total, classes)
    weights = (w_feat, w_mark, b_enc, w_out, row(b_out), row(gain_one), row(shift_one), w_in, row(b_in), w_back, row(b_back),
               row(gain_two), row(shift_two))
    layer_out, first, dox, grads, wide, narrow = middle(place, queries, feats, mixed, inv, cotangent, weights, ctx_len)
    grads = gather_chunks(reduce_chunks(grads, bits), bits)
    g_out, g_in, g_back = finish(place, grads)

    width = model // HEADS
    parts, heads, biases = [], [], []
    for head in range(HEADS):
        part, head_grads, bias = score_grads(place, head, expo, qry, key, val, dox, low)
        parts.append(part)
        heads.append(head_grads)
        biases.append(bias)
    cut = lambda w: w.T.reshape(HEADS, width, model)
    wts = jnp.concatenate([cut(w_query), cut(w_key), cut(w_value)], 1)
    d_rows, tail = stream_grads(place, first, parts, wts, feats, w_feat.T, narrow, wide, biases, feat_total)
    both = jnp.concatenate(heads + [tail], 2)
    both = gather_chunks(reduce_chunks(both, bits), bits)
    g_query, g_key, g_value, aug = finish_tail(place, both[:, :, :3 * model], both[:, :, 3 * model:])

    d_table = spread(ids, d_rows, row_count, feat_total, own_rows)
    d_table = d_table.astype(f32)
    for axis, bit in row_bits:
        half = d_table.shape[0] // 2
        d_table = d_table[:half] + swap(d_table[half:].astype(bf16), axis, bit).astype(f32)
    d_own = d_table.astype(bf16).reshape(feat_count, col_width, own_rows)
    d_columns = lax.all_to_all(d_own, "feat", split_axis=0, concat_axis=0, tiled=True)
    d_columns = d_columns.transpose(1, 0, 2).reshape(col_width, local_rows).astype(f32)
    smalls = aug[LANES:]
    stats = smalls[10, :2 * LANES].reshape(2, LANES)
    stats = lax.dynamic_slice_in_dim(stats, feat_index * col_width, col_width, 1)
    d_spread = -0.5 * (stats[1] / factor) * factor * factor * factor
    d_mean = -factor * stats[0] - 2.0 * d_spread * col_mean
    raw_grad = factor[:, None] * d_columns + (d_mean[:, None] + 2.0 * d_spread[:, None] * columns) / row_total
    return (
        layer_out, raw_grad.T, aug[:feat_total], aug[feat_total + classes], aug[feat_total:feat_total + classes],
        g_query, smalls[8], g_key, g_value, smalls[9], g_out, smalls[0], smalls[1], smalls[2], g_in,
        smalls[6:8].reshape(-1), g_back, smalls[3], smalls[4], smalls[5],
    )


def solution(mesh):
    both = ("rows", "feat")
    placed = (P("rows", "feat"),) + (P(),) * 18 + (P(both, None), P(both, None), P(both), P(both, None, None))
    results = (P(both, None, None), P("rows", "feat")) + (P(),) * 18
    return jax.shard_map(body, mesh=mesh, in_specs=placed, out_specs=results, check_vma=False)
```

time: 925 us -> 338 us (0.37); the launches traced: 908 us -> 337 us
  matrix products: 196 us -> 0 us
  waiting for transfers between devices: 222 us -> 52.4 us
  local copies, waits for them, and re-layouts: 223 us -> 58.9 us
  Pallas kernels: 0 us -> 152 us
  blocking collectives: 142 us -> 10.3 us
  other arithmetic: 92.6 us -> 15.4 us
  starting transfers between devices: 5.57 us -> 46.4 us
  between operations: 14.8 us -> 1.18 us
  loops' own time: 11.7 us -> 0 us
    dot_general x53 -> x0, matrix products: 196 us -> none  [the longest x37 89.9 us: product(): return jnp.dot(left, right, preferred_element_type=jnp.float32)]
    pallas_call x0 -> x10, Pallas kernels: none -> 152 us  [the longest x4 43.3 us: score_grads(): pl.pallas_call(functools.partial(scores_kernel, ctx_pad, parts), grid_spe...]
    psum x1 -> x0, waiting for transfers between devices: 127 us -> none  [body(): lax.psum((g_encoder, g_enc_bias, g_table, grad_sums[0], grad_sums[1], gra...]
    dynamic_update_slice x5 -> x0, local copies, waits for them, and re-layouts: 99.4 us -> none  [the longest x4 98.8 us: body(): lax.scan(layer_step, start_sums, (stream_in, live_mask, cotangent))]
    psum x3 -> x0, blocking collectives: 77.8 us -> none  [the longest x1 42 us: body(): lax.psum((g_encoder, g_enc_bias, g_table, grad_sums[0], grad_sums[1], gra...]
    all_to_all x2 -> x1, blocking collectives: 64.1 us -> 10.3 us  [body(): lax.all_to_all(standard, 'feat', split_axis=0, concat_axis=0, tiled=True)]
    ppermute x0 -> x29, waiting for transfers between devices: none -> 52.4 us  [swap(): return lax.ppermute(value, axis, [(i, i ^ bit) for i in range(size)])]
    all_to_all x1, waiting for transfers between devices: 51.4 us -> 0.01 us  [body(): lax.all_to_all(d_own, 'feat', split_axis=0, concat_axis=0, tiled=True)]
  transfers between devices with their start and end apart: 4 -> 30, of which waited for: 4 -> 13; matrix products, arithmetic and copies ran while one was open for 2% -> 19% of each run, Pallas kernels for 0% -> 4%
where the time goes in v1:
time: 338 us; the launch traced here: 337 us
  Pallas kernels  152 us (45%)
  local copies, waits for them, and re-layouts  58.9 us (17%)
  waiting for transfers between devices  52.4 us (16%)
  starting transfers between devices  46.4 us (14%)
  other arithmetic  15.4 us (5%)
  blocking collectives  10.3 us (3%)
    ppermute x29, waiting for transfers between devices, swap(): return lax.ppermute(value, axis, [(i, i ^ bit) for i in range(size)])  52.4 us
    pallas_call x4, Pallas kernels, score_grads(): pl.pallas_call(functools.partial(scores_kernel, ctx_pad, parts), grid_spe...  43.3 us
    ppermute x29, starting transfers between devices, swap(): return lax.ppermute(value, axis, [(i, i ^ bit) for i in range(size)])  41 us
    pallas_call x1, Pallas kernels, middle(): pl.pallas_call(functools.partial(middle_kernel, ctx_len), grid_spec=pltpu...  39.3 us
    pallas_call x1, Pallas kernels, attend(): pl.pallas_call(kernel, grid_spec=pltpu.PrefetchScalarGridSpec(num_scalar_...  38.6 us
    unnamed x48, local copies, waits for them, and re-layouts  31.9 us
    pallas_call x1, Pallas kernels, stream_grads(): pl.pallas_call(functools.partial(stream_kernel, feat_total), grid_spec=pl...  12.9 us
    all_to_all x1, blocking collectives, body(): lax.all_to_all(standard, 'feat', split_axis=0, concat_axis=0, tiled=True)  10.3 us
  transfers between devices with their start and end apart: 30, of which 13 were waited for; matrix products, arithmetic and copies ran while one was open for 19% of the time, Pallas kernels for 4%

profile of v1, /device:TPU:1, one launch (start us, length us, event | category | flops | bytes accessed | tf_op | source)
XLA Modules:
  0.0 336.6 jit_solution(4190361624139151576)
XLA Ops:
  1.8 2.1 collective-permute-start
  4.9 1.6 collective-permute-start.1
  7.4 2.5 collective-permute-start.2
  12.1 10.3 %all_to_all.10 = bf16[4,25,512]{2,1,0:T(8,128)(2,1)S(1)} all-to-all(bf16[4,25,512]{2,1,0:T(8,128)(2,1)S(1)} %bitcast.87), channel_id=1, replica_groups=mesh['rows'=8,'feat'=4] {'feat'}, dimensions={0} | all-to-all | bytes 204800 | tf_op jit(solution)/shard_map/all_to_all | solution.py:595
  22.5 2.4 collective-permute-start.3
  26.6 1.6 collective-permute-done.3
  28.1 2.6 collective-permute-start.4
  31.6 1.4 copy.65.mark
  34.3 5.4 %copy.67.cot = f32[2,1100,512]{2,1,0:T(8,128)} copy(f32[2,1100,512]{2,0,1:T(2,128)} %param.45) | data formatting | bytes 9011200 | tf_op args[22]
  44.3 8.3 %collective-permute-done.5 = bf16[4,100,512]{2,1,0:T(8,128)(2,1)S(1)} collective-permute-done((bf16[4,100,512]{2,1,0:T(8,128)(2,1)S(1)}, bf16[4,100,512]{2,1,0:T(8,128)(2,1)S(1)}, u32[]{:S(2)}, u32[]{:S(2)}) %collective-permute-start.5) | collective-permute-done | bytes 409632 | tf_op jit(solution)/shard_map/ppermute | solution.py:530
  53.6 38.6 %attend.1 = (bf16[2,1104,128]{2,1,0:T(8,128)(2,1)}, bf16[2,1104,512]{2,1,0:T(8,128)(2,1)}, bf16[2,1104,512]{2,1,0:T(8,128)(2,1)}, bf16[2,1104,512]{2,1,0:T(8,128...) custom-call(s32[2,1100]{1,0:T(2,128)} %fusion.5.ids, ...), custom_call_target="tpu_custom_call" | custom-call | tf_op jit(solution)/shard_map/attend/pallas_call | solution.py:268
  92.2 39.3 %middle.1 = (bf16[2,1100,512]{2,1,0:T(8,128)(2,1)}, f32[2,1104,512]{2,1,0:T(8,128)}, bf16[2,4,1104,256]{3,2,1,0:T(8,128)(2,1)}, bf16[32,80,512]{2,1,0:T(8,128)(2...) custom-call(s32[1]{0:T(128)} %bitcast.place, s32[2]{0:T(128)} %queries.1, ...), custom_call_target="tpu_custom_call" | custom-call | tf_op jit(solution)/shard_map/middle/pallas_call | solution.py:296
  131.5 10.9 %score_grads.4 = (bf16[2,1,1104,384]{3,2,1,0:T(8,128)(2,1)}, bf16[32,16,384]{2,1,0:T(8,128)(2,1)}, f32[8,384]{1,0:T(8,128)}) custom-call(s32[1]{0:T(128)} %bitcast.place, bf16[2,4,1104,1024]{3,2,1,0:T(8,128)(2,1)} %get-tuple-element.60.e, bf16[2,1104,512]{2,1,0:T(8,128)(2,1)} %get-tuple-element.61.q, bf16[2,1104,512]{2,1,0:T(8,128)(2,1)} %get-tuple-element.62.k, ...), custom_call_target="tpu_custom_call" | custom-call | tf_op jit(solution)/shard_map/score_grads/pallas_call | solution.py:322
  142.4 10.7 %score_grads.5 = (bf16[2,1,1104,384]{3,2,1,0:T(8,128)(2,1)}, bf16[32,16,384]{2,1,0:T(8,128)(2,1)}, f32[8,384]{1,0:T(8,128)}) custom-call(s32[1]{0:T(128)} %bitcast.place, bf16[2,4,1104,1024]{3,2,1,0:T(8,128)(2,1)} %get-tuple-element.60.e, bf16[2,1104,512]{2,1,0:T(8,128)(2,1)} %get-tuple-element.61.q, bf16[2,1104,512]{2,1,0:T(8,128)(2,1)} %get-tuple-element.62.k, ...), custom_call_target="tpu_custom_call" | custom-call | tf_op jit(solution)/shard_map/score_grads/pallas_call | solution.py:322
  153.1 10.7 %score_grads.6 = (bf16[2,1,1104,384]{3,2,1,0:T(8,128)(2,1)}, bf16[32,16,384]{2,1,0:T(8,128)(2,1)}, f32[8,384]{1,0:T(8,128)}) custom-call(s32[1]{0:T(128)} %bitcast.place, bf16[2,4,1104,1024]{3,2,1,0:T(8,128)(2,1)} %get-tuple-element.60.e, bf16[2,1104,512]{2,1,0:T(8,128)(2,1)} %get-tuple-element.61.q, bf16[2,1104,512]{2,1,0:T(8,128)(2,1)} %get-tuple-element.62.k, ...), custom_call_target="tpu_custom_call" | custom-call | tf_op jit(solution)/shard_map/score_grads/pallas_call | solution.py:322
  163.9 11.0 %score_grads.7 = (bf16[2,1,1104,384]{3,2,1,0:T(8,128)(2,1)}, bf16[32,16,384]{2,1,0:T(8,128)(2,1)}, f32[8,384]{1,0:T(8,128)}) custom-call(s32[1]{0:T(128)} %bitcast.place, bf16[2,4,1104,1024]{3,2,1,0:T(8,128)(2,1)} %get-tuple-element.60.e, bf16[2,1104,512]{2,1,0:T(8,128)(2,1)} %get-tuple-element.61.q, bf16[2,1104,512]{2,1,0:T(8,128)(2,1)} %get-tuple-element.62.k, ...), custom_call_target="tpu_custom_call" | custom-call | tf_op jit(solution)/shard_map/score_grads/pallas_call | solution.py:322
  176.0 12.9 %stream_grads.1 = (f32[2,1104,128]{2,1,0:T(8,128)}, bf16[32,16,256]{2,1,0:T(8,128)(2,1)}) custom-call(s32[1]{0:T(128)} %bitcast.place, f32[2,1104,512]{2,1,0:T(8,128)} %get-tuple-element.59.first, bf16[2,1,1104,384]{3,2,1,0:T(8,128)(2,1)} %get-tuple-element.66.refs_0_, bf16[2,1,1104,384]{3,2,1,0:T(8,128)(2,1)} %get-tuple-element.67.refs_1_, ...), custom_call_target="tpu_custom_call" | custom-call | tf_op jit(solution)/shard_map/stream_grads/pallas_call | solution.py:397
  191.0 2.0 collective-permute-start.9
  193.0 7.9 %spread.1 = bf16[8,100,512]{2,1,0:T(8,128)(2,1)} custom-call(s32[2,1100]{1,0:T(2,128)} %fusion.5.ids, f32[2,1104,128]{2,1,0:T(8,128)} %get-tuple-element.76.rows), custom_call_target="tpu_custom_call" | custom-call | tf_op jit(solution)/shard_map/spread/pallas_call | solution.py:448
  203.3 1.4 convert_add_fusion.1
  205.7 15.4 %copy.73 = bf16[2,1100,512]{2,0,1:T(2,128)(2,1)} copy(bf16[2,1100,512]{2,1,0:T(8,128)(2,1)} %get-tuple-element.130) | data formatting | bytes 4505600
  224.0 5.7 %collective-permute-done.7 = bf16[2,100,512]{2,1,0:T(8,128)(2,1)S(1)} collective-permute-done((bf16[2,100,512]{2,1,0:T(8,128)(2,1)S(1)}, bf16[2,100,512]{2,1,0:T(8,128)(2,1)S(1)}, u32[]{:S(2)}, u32[]{:S(2)}) %collective-permute-start.7) | collective-permute-done | bytes 204832 | tf_op jit(solution)/shard_map/ppermute | solution.py:530
  229.8 3.2 collective-permute-start.8
  234.3 4.5 %collective-permute-done.12 = bf16[2,16,1792]{2,1,0:T(8,128)(2,1)S(1)} collective-permute-done((bf16[2,16,1792]{2,1,0:T(8,128)(2,1)S(1)}, bf16[2,16,1792]{2,1,0:T(8,128)(2,1)S(1)}, u32[]{:S(2)}, u32[]{:S(2)}) %collective-permute-start.12) | collective-permute-done | bytes 114720 | tf_op jit(solution)/shard_map/ppermute | solution.py:530
  240.2 1.6 reshape.168
  241.8 5.4 %all-to-all-start.1 = ((bf16[4,25,512]{2,1,0:T(8,128)(2,1)}), bf16[4,25,512]{2,1,0:T(8,128)(2,1)}, u32[]{:S(2)}, u32[]{:S(2)}) async-start(bf16[4,25,512]{2,1,0:T(8,128)(2,1)} %reshape.168), calls=%async_computation.1 | async-start | bytes 262144 | tf_op jit(solution)/shard_map/all_to_all | solution.py:637
  247.2 1.5 constant_dynamic-update-slice_fusion.9
  248.7 2.6 collective-permute-start.14
  254.4 7.0 %collective-permute-done.21 = bf16[4,80,512]{2,1,0:T(8,128)(2,1)S(1)} collective-permute-done((bf16[4,80,512]{2,1,0:T(8,128)(2,1)S(1)}, bf16[4,80,512]{2,1,0:T(8,128)(2,1)S(1)}, u32[]{:S(2)}, u32[]{:S(2)}) %collective-permute-start.21) | collective-permute-done | bytes 327712 | tf_op jit(solution)/shard_map/ppermute | solution.py:530
  262.4 3.4 %collective-permute-done.22 = bf16[2,80,512]{2,1,0:T(8,128)(2,1)S(1)} collective-permute-done((bf16[2,80,512]{2,1,0:T(8,128)(2,1)S(1)}, bf16[2,80,512]{2,1,0:T(8,128)(2,1)S(1)}, u32[]{:S(2)}, u32[]{:S(2)}) %collective-permute-start.22) | collective-permute-done | bytes 163872 | tf_op jit(solution)/shard_map/ppermute | solution.py:530
  266.2 4.5 %collective-permute-done.23 = bf16[1,80,512]{2,1,0:T(8,128)(2,1)S(1)} collective-permute-done((bf16[1,80,512]{2,1,0:T(8,128)(2,1)S(1)}, bf16[1,80,512]{2,1,0:T(8,128)(2,1)S(1)}, u32[]{:S(2)}, u32[]{:S(2)}) %collective-permute-start.23) | collective-permute-done | bytes 81952 | tf_op jit(solution)/shard_map/ppermute | solution.py:530
  271.5 1.6 collective-permute-start.17
  273.1 2.7 collective-permute-done.24
  276.6 4.6 %collective-permute-done.25 = bf16[2,80,512]{2,1,0:T(8,128)(2,1)S(1)} collective-permute-done((bf16[2,80,512]{2,1,0:T(8,128)(2,1)S(1)}, bf16[2,80,512]{2,1,0:T(8,128)(2,1)S(1)}, u32[]{:S(2)}, u32[]{:S(2)}) %collective-permute-start.25) | collective-permute-done | bytes 163872 | tf_op jit(solution)/shard_map/ppermute | solution.py:530
  283.3 5.9 %collective-permute-start.18 = (bf16[16,16,1792]{2,1,0:T(8,128)(2,1)}, bf16[16,16,1792]{2,1,0:T(8,128)(2,1)}, u32[]{:S(2)}, u32[]{:S(2)}) collective-permute-start(bf16[16,16,1792]{2,1,0:T(8,128)(2,1)} %get-tuple-element.169), channel_id=1, source_target_pairs={{0,1},{1,0},{2,3},{3,2},{4,5},{5,4},{6,7},{7,6},{8,9},{9,8},{10,11... | collective-permute-start | bytes 2752520 | tf_op jit(solution)/shard_map/ppermute | solution.py:530
  294.8 7.1 %collective-permute-done.27 = bf16[8,80,512]{2,1,0:T(8,128)(2,1)} collective-permute-done((bf16[8,80,512]{2,1,0:T(8,128)(2,1)}, bf16[8,80,512]{2,1,0:T(8,128)(2,1)}, u32[]{:S(2)}, u32[]{:S(2)}) %collective-permute-start.27) | collective-permute-done | bytes 655392 | tf_op jit(solution)/shard_map/ppermute | solution.py:530
  301.9 2.1 constant_dynamic-update-slice_fusion.16
  303.9 5.7 %collective-permute-start.28 = (bf16[16,80,512]{2,1,0:T(8,128)(2,1)}, bf16[16,80,512]{2,1,0:T(8,128)(2,1)}, u32[]{:S(2)}, u32[]{:S(2)}) collective-permute-start(bf16[16,80,512]{2,1,0:T(8,128)(2,1)} %get-tuple-element.158), channel_id=1, source_target_pairs={{0,1},{1,0},{2,3},{3,2},{4,5},{5,4},{6,7},{7,6},{8,9},{9,8},{10,11... | collective-permute-start | bytes 3932168 | tf_op jit(solution)/shard_map/ppermute | solution.py:530
  309.6 2.2 constant_dynamic-update-slice_fusion.10
  311.8 2.7 slice.222.heads
  314.4 1.7 slice.223.tail
  316.1 4.7 %finish_tail.1 = (f32[512,512]{1,0:T(8,128)}, f32[512,512]{1,0:T(8,128)}, f32[512,512]{1,0:T(8,128)}, f32[256,512]{1,0:T(8,128)}) custom-call(s32[1]{0:T(128)} %bitcast.place, bf16[32,16,1536]{2,1,0:T(8,128)(2,1)} %slice.222.heads, bf16[32,16,256]{2,1,0:T(8,128)(2,1)} %slice.223.tail), custom_call_target="tpu_custom_call" | custom-call | tf_op jit(solution)/shard_map/finish_tail/pallas_call | solution.py:514
  321.5 1.6 slice.184
  323.2 1.4 slice.186
  326.0 1.6 fusion.15
  328.4 1.4 constant_dynamic-update-slice_fusion.21.grads
  329.8 1.5 copy-done.1
  331.3 5.4 %finish.1 = (f32[512,512]{1,0:T(8,128)}, f32[512,1024]{1,0:T(8,128)}, f32[1024,512]{1,0:T(8,128)}) custom-call(s32[1]{0:T(128)} %bitcast.place, bf16[32,80,512]{2,1,0:T(8,128)(2,1)} %copy-done.1), custom_call_target="tpu_custom_call" | custom-call | tf_op jit(solution)/shard_map/finish/pallas_call | solution.py:479
  (144 shorter events, 43.3 us)
Async XLA Ops:
  1.8 3.1 collective-permute-start
  4.9 2.5 collective-permute-start.1
  7.4 3.5 %collective-permute-start.2 = (f32[2,25]{1,0:T(2,128)S(1)}, f32[2,25]{1,0:T(2,128)S(1)}, u32[]{:S(2)}, u32[]{:S(2)}) collective-permute-start(f32[2,25]{1,0:T(2,128)S(1)} %fusion.16), channel_id=1, source_target_pairs={{0,16},{4,20},{8,24},{12,28},{16,0},{20,4},{24,8},{28,12},{1,17},{... | collective-permute-start | bytes 608 | tf_op jit(solution)/shard_map/ppermute | solution.py:530
  12.0 21.6 %copy-start.12 = (bf16[10,512]{1,0:T(8,128)(2,1)S(1)}, bf16[10,512]{1,0:T(8,128)(2,1)}, u32[]{:S(2)}) copy-start(bf16[10,512]{1,0:T(8,128)(2,1)} %param.26) | copy-start | bytes 30724
  22.5 5.7 %collective-permute-start.3 = (bf16[1,100,512]{2,1,0:T(8,128)(2,1)S(1)}, bf16[1,100,512]{2,1,0:T(8,128)(2,1)S(1)}, u32[]{:S(2)}, u32[]{:S(2)}) collective-permute-start(bf16[1,100,512]{2,1,0:T(8,128)(2,1)S(1)} %reshape.154), channel_id=1, source_target_pairs={{0,16},{4,20},{8,24},{12,28},{16,0},{20,4},{24,8},{28,12},{1,17},{... | collective-permute-start | bytes 307208 | tf_op jit(solution)/shard_map/ppermute | solution.py:530
  28.1 14.1 %collective-permute-start.4 = (bf16[2,100,512]{2,1,0:T(8,128)(2,1)S(1)}, bf16[2,100,512]{2,1,0:T(8,128)(2,1)S(1)}, u32[]{:S(2)}, u32[]{:S(2)}) collective-permute-start(bf16[2,100,512]{2,1,0:T(8,128)(2,1)S(1)} %pad_maximum_fusion.7), channel_id=1, source_target_pairs={{0,8},{4,12},{8,0},{12,4},{16,24},{20,28},{24,16},{28,20},{1,9},{5... | collective-permute-start | bytes 614408 | tf_op jit(solution)/shard_map/ppermute | solution.py:530
  34.3 5.4 %copy-start.7 = (bf16[512,512]{1,0:T(8,128)(2,1)S(1)}, bf16[512,512]{1,0:T(8,128)(2,1)}, u32[]{:S(2)}) copy-start(bf16[512,512]{1,0:T(8,128)(2,1)} %w_value.1) | copy-start | bytes 1572868
  34.3 5.6 %copy-start.6 = (bf16[512,512]{1,0:T(8,128)(2,1)S(1)}, bf16[512,512]{1,0:T(8,128)(2,1)}, u32[]{:S(2)}) copy-start(bf16[512,512]{1,0:T(8,128)(2,1)} %w_key.1) | copy-start | bytes 1572868
  39.7 1.0 copy-start.5
  40.9 2.7 copy-start.13
  42.3 10.3 %collective-permute-start.5 = (bf16[4,100,512]{2,1,0:T(8,128)(2,1)S(1)}, bf16[4,100,512]{2,1,0:T(8,128)(2,1)S(1)}, u32[]{:S(2)}, u32[]{:S(2)}) collective-permute-start(bf16[4,100,512]{2,1,0:T(8,128)(2,1)S(1)} %pad_maximum_fusion.4), channel_id=1, source_target_pairs={{0,4},{4,0},{8,12},{12,8},{16,20},{20,16},{24,28},{28,24},{1,5},{5... | collective-permute-start | bytes 1228808 | tf_op jit(solution)/shard_map/ppermute | solution.py:530
  163.8 11.0 %copy-start.8 = (bf16[32,16,384]{2,1,0:T(8,128)(2,1)S(1)}, bf16[32,16,384]{2,1,0:T(8,128)(2,1)}, u32[]{:S(2)}) copy-start(bf16[32,16,384]{2,1,0:T(8,128)(2,1)} %get-tuple-element.77) | copy-start | bytes 1179652
  163.8 11.0 %copy-start.9 = (bf16[32,16,384]{2,1,0:T(8,128)(2,1)S(1)}, bf16[32,16,384]{2,1,0:T(8,128)(2,1)}, u32[]{:S(2)}) copy-start(bf16[32,16,384]{2,1,0:T(8,128)(2,1)} %get-tuple-element.78) | copy-start | bytes 1179652
  174.8 1.0 copy-start.10
  174.8 1.1 copy-start.11
  189.9 11.0 %copy-start.2 = (bf16[32,16,1792]{2,1,0:T(8,128)(2,1)}, bf16[32,16,1792]{2,1,0:T(8,128)(2,1)S(1)}, u32[]{:S(2)}) copy-start(bf16[32,16,1792]{2,1,0:T(8,128)(2,1)S(1)} %constant_dynamic-update-slice_fusion) | copy-start | bytes 5505028
  191.0 12.3 %collective-permute-start.9 = (bf16[16,16,1792]{2,1,0:T(8,128)(2,1)}, bf16[16,16,1792]{2,1,0:T(8,128)(2,1)S(1)}, u32[]{:S(2)}, u32[]{:S(2)}) collective-permute-start(bf16[16,16,1792]{2,1,0:T(8,128)(2,1)} %slice.213), channel_id=1, source_target_pairs={{0,1},{1,0},{2,3},{3,2},{4,5},{5,4},{6,7},{7,6},{8,9},{9,8},{10,11... | collective-permute-start | bytes 2752520 | tf_op jit(solution)/shard_map/ppermute | solution.py:530
  202.0 19.8 %collective-permute-start.6 = (bf16[4,100,512]{2,1,0:T(8,128)(2,1)S(1)}, bf16[4,100,512]{2,1,0:T(8,128)(2,1)}, u32[]{:S(2)}, u32[]{:S(2)}) collective-permute-start(bf16[4,100,512]{2,1,0:T(8,128)(2,1)S(1)} %slice.207), channel_id=1, source_target_pairs={{0,4},{4,0},{8,12},{12,8},{16,20},{20,16},{24,28},{28,24},{1,5},{5... | collective-permute-start | bytes 1228808 | tf_op jit(solution)/shard_map/ppermute | solution.py:530
  204.7 18.9 %collective-permute-start.10 = (bf16[8,16,1792]{2,1,0:T(8,128)(2,1)S(1)}, bf16[8,16,1792]{2,1,0:T(8,128)(2,1)S(1)}, u32[]{:S(2)}, u32[]{:S(2)}) collective-permute-start(bf16[8,16,1792]{2,1,0:T(8,128)(2,1)S(1)} %slice.276), channel_id=1, source_target_pairs={{0,2},{1,3},{2,0},{3,1},{4,6},{5,7},{6,4},{7,5},{8,10},{9,11},{10,... | collective-permute-start | bytes 1376264 | tf_op jit(solution)/shard_map/ppermute | solution.py:530
  205.7 15.4 %copy-start.3 = (bf16[32,80,512]{2,1,0:T(8,128)(2,1)S(1)}, bf16[32,80,512]{2,1,0:T(8,128)(2,1)}, u32[]{:S(2)}) copy-start(bf16[32,80,512]{2,1,0:T(8,128)(2,1)} %get-tuple-element.86) | copy-start | bytes 7864324
  221.1 1.2 copy-start
  221.2 12.0 %collective-permute-start.19 = (bf16[16,80,512]{2,1,0:T(8,128)(2,1)S(1)}, bf16[16,80,512]{2,1,0:T(8,128)(2,1)S(1)}, u32[]{:S(2)}, u32[]{:S(2)}) collective-permute-start(bf16[16,80,512]{2,1,0:T(8,128)(2,1)S(1)} %slice.190), channel_id=1, source_target_pairs={{0,1},{1,0},{2,3},{3,2},{4,5},{5,4},{6,7},{7,6},{8,9},{9,8},{10,11... | collective-permute-start | bytes 3932168 | tf_op jit(solution)/shard_map/ppermute | solution.py:530
  223.4 6.3 %collective-permute-start.7 = (bf16[2,100,512]{2,1,0:T(8,128)(2,1)S(1)}, bf16[2,100,512]{2,1,0:T(8,128)(2,1)S(1)}, u32[]{:S(2)}, u32[]{:S(2)}) collective-permute-start(bf16[2,100,512]{2,1,0:T(8,128)(2,1)S(1)} %slice.279), channel_id=1, source_target_pairs={{0,8},{4,12},{8,0},{12,4},{16,24},{20,28},{24,16},{28,20},{1,9},{5... | collective-permute-start | bytes 614408 | tf_op jit(solution)/shard_map/ppermute | solution.py:530
  223.7 9.2 %collective-permute-start.11 = (bf16[4,16,1792]{2,1,0:T(8,128)(2,1)S(1)}, bf16[4,16,1792]{2,1,0:T(8,128)(2,1)S(1)}, u32[]{:S(2)}, u32[]{:S(2)}) collective-permute-start(bf16[4,16,1792]{2,1,0:T(8,128)(2,1)S(1)} %slice.278), channel_id=1, source_target_pairs={{0,4},{4,0},{8,12},{12,8},{16,20},{20,16},{24,28},{28,24},{1,5},{5... | collective-permute-start | bytes 688136 | tf_op jit(solution)/shard_map/ppermute | solution.py:530
  229.8 9.7 %collective-permute-start.8 = (bf16[1,100,512]{2,1,0:T(8,128)(2,1)S(1)}, bf16[1,100,512]{2,1,0:T(8,128)(2,1)S(1)}, u32[]{:S(2)}, u32[]{:S(2)}) collective-permute-start(bf16[1,100,512]{2,1,0:T(8,128)(2,1)S(1)} %slice.282), channel_id=1, source_target_pairs={{0,16},{4,20},{8,24},{12,28},{16,0},{20,4},{24,8},{28,12},{1,17},{... | collective-permute-start | bytes 307208 | tf_op jit(solution)/shard_map/ppermute | solution.py:530
  233.1 5.8 %collective-permute-start.12 = (bf16[2,16,1792]{2,1,0:T(8,128)(2,1)S(1)}, bf16[2,16,1792]{2,1,0:T(8,128)(2,1)S(1)}, u32[]{:S(2)}, u32[]{:S(2)}) collective-permute-start(bf16[2,16,1792]{2,1,0:T(8,128)(2,1)S(1)} %slice.281), channel_id=1, source_target_pairs={{0,8},{4,12},{8,0},{12,4},{16,24},{20,28},{24,16},{28,20},{1,9},{5... | collective-permute-start | bytes 344072 | tf_op jit(solution)/shard_map/ppermute | solution.py:530
  233.7 17.7 %collective-permute-start.20 = (bf16[8,80,512]{2,1,0:T(8,128)(2,1)S(1)}, bf16[8,80,512]{2,1,0:T(8,128)(2,1)}, u32[]{:S(2)}, u32[]{:S(2)}) collective-permute-start(bf16[8,80,512]{2,1,0:T(8,128)(2,1)S(1)} %slice.275), channel_id=1, source_target_pairs={{0,2},{1,3},{2,0},{3,1},{4,6},{5,7},{6,4},{7,5},{8,10},{9,11},{10,... | collective-permute-start | bytes 1966088 | tf_op jit(solution)/shard_map/ppermute | solution.py:530
  239.5 7.7 %collective-permute-start.13 = (bf16[1,16,1792]{2,1,0:T(8,128)(2,1)}, bf16[1,16,1792]{2,1,0:T(8,128)(2,1)}, u32[]{:S(2)}, u32[]{:S(2)}) collective-permute-start(bf16[1,16,1792]{2,1,0:T(8,128)(2,1)} %slice.284), channel_id=1, source_target_pairs={{0,16},{4,20},{8,24},{12,28},{16,0},{20,4},{24,8},{28,12},{1,17},{... | collective-permute-start | bytes 172040 | tf_op jit(solution)/shard_map/ppermute | solution.py:530
  241.8 49.7 %all-to-all-start.1 = ((bf16[4,25,512]{2,1,0:T(8,128)(2,1)}), bf16[4,25,512]{2,1,0:T(8,128)(2,1)}, u32[]{:S(2)}, u32[]{:S(2)}) async-start(bf16[4,25,512]{2,1,0:T(8,128)(2,1)} %reshape.168), calls=%async_computation.1 | async-start | bytes 262144 | tf_op jit(solution)/shard_map/all_to_all | solution.py:637
  248.7 4.9 %collective-permute-start.14 = (bf16[1,16,1792]{2,1,0:T(8,128)(2,1)S(1)}, bf16[1,16,1792]{2,1,0:T(8,128)(2,1)S(1)}, u32[]{:S(2)}, u32[]{:S(2)}) collective-permute-start(bf16[1,16,1792]{2,1,0:T(8,128)(2,1)S(1)} %get-tuple-element.157), channel_id=1, source_target_pairs={{0,16},{4,20},{8,24},{12,28},{16,0},{20,4},{24,8},{28,12},{1,17},{... | collective-permute-start | bytes 172040 | tf_op jit(solution)/shard_map/ppermute | solution.py:530
  252.7 8.7 %collective-permute-start.21 = (bf16[4,80,512]{2,1,0:T(8,128)(2,1)S(1)}, bf16[4,80,512]{2,1,0:T(8,128)(2,1)S(1)}, u32[]{:S(2)}, u32[]{:S(2)}) collective-permute-start(bf16[4,80,512]{2,1,0:T(8,128)(2,1)S(1)} %slice.277), channel_id=1, source_target_pairs={{0,4},{4,0},{8,12},{12,8},{16,20},{20,16},{24,28},{28,24},{1,5},{5... | collective-permute-start | bytes 983048 | tf_op jit(solution)/shard_map/ppermute | solution.py:530
  253.6 12.3 %collective-permute-start.15 = (bf16[2,16,1792]{2,1,0:T(8,128)(2,1)S(1)}, bf16[2,16,1792]{2,1,0:T(8,128)(2,1)S(1)}, u32[]{:S(2)}, u32[]{:S(2)}) collective-permute-start(bf16[2,16,1792]{2,1,0:T(8,128)(2,1)S(1)} %pad_maximum_fusion.9), channel_id=1, source_target_pairs={{0,8},{4,12},{8,0},{12,4},{16,24},{20,28},{24,16},{28,20},{1,9},{5... | collective-permute-start | bytes 344072 | tf_op jit(solution)/shard_map/ppermute | solution.py:530
  261.5 4.2 %collective-permute-start.22 = (bf16[2,80,512]{2,1,0:T(8,128)(2,1)S(1)}, bf16[2,80,512]{2,1,0:T(8,128)(2,1)S(1)}, u32[]{:S(2)}, u32[]{:S(2)}) collective-permute-start(bf16[2,80,512]{2,1,0:T(8,128)(2,1)S(1)} %slice.280), channel_id=1, source_target_pairs={{0,8},{4,12},{8,0},{12,4},{16,24},{20,28},{24,16},{28,20},{1,9},{5... | collective-permute-start | bytes 491528 | tf_op jit(solution)/shard_map/ppermute | solution.py:530
  265.8 5.0 %collective-permute-start.23 = (bf16[1,80,512]{2,1,0:T(8,128)(2,1)S(1)}, bf16[1,80,512]{2,1,0:T(8,128)(2,1)S(1)}, u32[]{:S(2)}, u32[]{:S(2)}) collective-permute-start(bf16[1,80,512]{2,1,0:T(8,128)(2,1)S(1)} %slice.283), channel_id=1, source_target_pairs={{0,16},{4,20},{8,24},{12,28},{16,0},{20,4},{24,8},{28,12},{1,17},{... | collective-permute-start | bytes 245768 | tf_op jit(solution)/shard_map/ppermute | solution.py:530
  266.0 5.5 %collective-permute-start.16 = (bf16[4,16,1792]{2,1,0:T(8,128)(2,1)S(1)}, bf16[4,16,1792]{2,1,0:T(8,128)(2,1)S(1)}, u32[]{:S(2)}, u32[]{:S(2)}) collective-permute-start(bf16[4,16,1792]{2,1,0:T(8,128)(2,1)S(1)} %pad_maximum_fusion.6), channel_id=1, source_target_pairs={{0,4},{4,0},{8,12},{12,8},{16,20},{20,16},{24,28},{28,24},{1,5},{5... | collective-permute-start | bytes 688136 | tf_op jit(solution)/shard_map/ppermute | solution.py:530
  271.5 4.3 %collective-permute-start.24 = (bf16[1,80,512]{2,1,0:T(8,128)(2,1)S(1)}, bf16[1,80,512]{2,1,0:T(8,128)(2,1)S(1)}, u32[]{:S(2)}, u32[]{:S(2)}) collective-permute-start(bf16[1,80,512]{2,1,0:T(8,128)(2,1)S(1)} %get-tuple-element.153), channel_id=1, source_target_pairs={{0,16},{4,20},{8,24},{12,28},{16,0},{20,4},{24,8},{28,12},{1,17},{... | collective-permute-start | bytes 245768 | tf_op jit(solution)/shard_map/ppermute | solution.py:530
  271.5 10.8 %collective-permute-start.17 = (bf16[8,16,1792]{2,1,0:T(8,128)(2,1)S(1)}, bf16[8,16,1792]{2,1,0:T(8,128)(2,1)S(1)}, u32[]{:S(2)}, u32[]{:S(2)}) collective-permute-start(bf16[8,16,1792]{2,1,0:T(8,128)(2,1)S(1)} %pad_maximum_fusion.3), channel_id=1, source_target_pairs={{0,2},{1,3},{2,0},{3,1},{4,6},{5,7},{6,4},{7,5},{8,10},{9,11},{10,... | collective-permute-start | bytes 1376264 | tf_op jit(solution)/shard_map/ppermute | solution.py:530
  275.8 5.4 %collective-permute-start.25 = (bf16[2,80,512]{2,1,0:T(8,128)(2,1)S(1)}, bf16[2,80,512]{2,1,0:T(8,128)(2,1)S(1)}, u32[]{:S(2)}, u32[]{:S(2)}) collective-permute-start(bf16[2,80,512]{2,1,0:T(8,128)(2,1)S(1)} %pad_maximum_fusion.8), channel_id=1, source_target_pairs={{0,8},{4,12},{8,0},{12,4},{16,24},{20,28},{24,16},{28,20},{1,9},{5... | collective-permute-start | bytes 491528 | tf_op jit(solution)/shard_map/ppermute | solution.py:530
  281.3 7.9 %collective-permute-start.26 = (bf16[4,80,512]{2,1,0:T(8,128)(2,1)S(1)}, bf16[4,80,512]{2,1,0:T(8,128)(2,1)S(1)}, u32[]{:S(2)}, u32[]{:S(2)}) collective-permute-start(bf16[4,80,512]{2,1,0:T(8,128)(2,1)S(1)} %pad_maximum_fusion.5), channel_id=1, source_target_pairs={{0,4},{4,0},{8,12},{12,8},{16,20},{20,16},{24,28},{28,24},{1,5},{5... | collective-permute-start | bytes 983048 | tf_op jit(solution)/shard_map/ppermute | solution.py:530
  283.3 26.3 %collective-permute-start.18 = (bf16[16,16,1792]{2,1,0:T(8,128)(2,1)}, bf16[16,16,1792]{2,1,0:T(8,128)(2,1)}, u32[]{:S(2)}, u32[]{:S(2)}) collective-permute-start(bf16[16,16,1792]{2,1,0:T(8,128)(2,1)} %get-tuple-element.169), channel_id=1, source_target_pairs={{0,1},{1,0},{2,3},{3,2},{4,5},{5,4},{6,7},{7,6},{8,9},{9,8},{10,11... | collective-permute-start | bytes 2752520 | tf_op jit(solution)/shard_map/ppermute | solution.py:530
  290.1 11.8 %collective-permute-start.27 = (bf16[8,80,512]{2,1,0:T(8,128)(2,1)}, bf16[8,80,512]{2,1,0:T(8,128)(2,1)}, u32[]{:S(2)}, u32[]{:S(2)}) collective-permute-start(bf16[8,80,512]{2,1,0:T(8,128)(2,1)} %pad_maximum_fusion.2), channel_id=1, source_target_pairs={{0,2},{1,3},{2,0},{3,1},{4,6},{5,7},{6,4},{7,5},{8,10},{9,11},{10,... | collective-permute-start | bytes 1966088 | tf_op jit(solution)/shard_map/ppermute | solution.py:530
  303.9 24.5 %collective-permute-start.28 = (bf16[16,80,512]{2,1,0:T(8,128)(2,1)}, bf16[16,80,512]{2,1,0:T(8,128)(2,1)}, u32[]{:S(2)}, u32[]{:S(2)}) collective-permute-start(bf16[16,80,512]{2,1,0:T(8,128)(2,1)} %get-tuple-element.158), channel_id=1, source_target_pairs={{0,1},{1,0},{2,3},{3,2},{4,5},{5,4},{6,7},{7,6},{8,9},{9,8},{10,11... | collective-permute-start | bytes 3932168 | tf_op jit(solution)/shard_map/ppermute | solution.py:530
  314.4 13.1 %copy-start.4 = (f32[2048,25]{0,1:T(8,128)S(1)}, f32[2048,25]{0,1:T(8,128)}, u32[]{:S(2)}) copy-start(f32[2048,25]{0,1:T(8,128)} %param.23) | copy-start | bytes 614404
  329.8 1.5 copy-start.1

commit v2 on v1

v2 whole, which is shorter than its diff:
```python
import functools
import math

import jax
import jax.numpy as jnp
from jax import lax
from jax.experimental import pallas as pl
from jax.experimental.pallas import tpu as pltpu
from jax.sharding import PartitionSpec as P

HEADS = 4
LANES = 128
epsilon = 1e-05
CHUNKS = 32
VMEM_LIMIT = 60 * 1024 * 1024
f32 = jnp.float32
bf16 = jnp.bfloat16


def dot(left, right):
    return jnp.dot(left, right, preferred_element_type=f32)


def dot_nt(left, right):
    return lax.dot_general(left, right, (((1,), (1,)), ((), ())), preferred_element_type=f32)


def dot_tn(left, right):
    return lax.dot_general(left, right, (((0,), (0,)), ((), ())), preferred_element_type=f32)


def round_up(value, unit):
    return -(-value // unit) * unit


def row_chunks(span):
    for parts in (3, 2, 1):
        if span % (16 * parts) == 0:
            return parts
    return 1


def cost(gigaflops, megabytes):
    return pl.CostEstimate(flops=int(gigaflops * 1e9), bytes_accessed=int(megabytes * 1e6), transcendentals=0)


def params(*names):
    return pltpu.CompilerParams(vmem_limit_bytes=VMEM_LIMIT, dimension_semantics=("arbitrary",) * len(names))


def fetch_kernel(span, feat_total, classes, ids, near, far, mark, feats_o, table, rows_f):
    count, deep, own = near.shape
    blocks, pad, _ = feats_o.shape
    unit = next(u for u in (20, 10, 5, 2, 1) if span % u == 0)

    for half, ref in enumerate((near, far)):
        def unfold(g, _):
            piece = jnp.concatenate([ref[g].astype(f32), jnp.zeros((LANES - deep, own), f32)], 0).T
            at = half * count + g
            table[pl.ds(pl.multiple_of(at * own, own), own), :] = piece
            return 0

        lax.fori_loop(0, count, unfold, 0)
    rows_f[pad - 16:, :] = jnp.zeros((16, LANES), f32)
    for block in range(blocks):
        def fetch(i, _):
            for u in range(unit):
                at = i * unit + u
                rows_f[pl.ds(at, 1), :] = table[pl.ds(ids[block * span + at], 1), :]
            return 0

        lax.fori_loop(0, span // unit, fetch, 0)
        lane = lax.broadcasted_iota(jnp.int32, (pad, LANES), 1)
        hot = (lane == mark[block] + feat_total) | (lane == feat_total + classes)
        feats_o[block] = jnp.where(lane < feat_total, rows_f[...], hot.astype(f32)).astype(bf16)


def fetch(ids, near, far, mark, feat_total, classes):
    blocks, pad, _ = mark.shape
    full = lambda *s: pl.BlockSpec(s, lambda *_: (0,) * len(s), pipeline_mode=pl.Buffered(1))
    return pl.pallas_call(
        functools.partial(fetch_kernel, ids.shape[0] // blocks, feat_total, classes),
        grid_spec=pltpu.PrefetchScalarGridSpec(
            num_scalar_prefetch=1,
            grid=(1,),
            in_specs=[full(*near.shape), full(*far.shape), full(*mark.shape)],
            out_specs=pl.BlockSpec((blocks, pad, LANES), lambda *_: (0, 0, 0)),
            scratch_shapes=[pltpu.VMEM((2 * near.shape[0] * near.shape[2], LANES), f32), pltpu.VMEM((pad, LANES), f32)],
        ),
        out_shape=jax.ShapeDtypeStruct((blocks, pad, LANES), bf16),
        compiler_params=params(0),
        cost_estimate=cost(6, 1),
        name="fetch",
    )(ids, near, far, mark)


def embed(feats, w_feat, w_mark, b_enc):
    slots = (dot(feats, w_feat[...]) + b_enc[...]).astype(bf16)
    return slots.astype(f32) + dot(feats, w_mark[...])


def norm_parts(values):
    centre = jnp.mean(values, -1, keepdims=True)
    offset = values - centre
    second = jnp.mean(offset * offset, -1, keepdims=True)
    root = lax.rsqrt(second + epsilon)
    return offset * root, root


def norm_back(grad, unit, root):
    return root * (grad - jnp.mean(grad, -1, keepdims=True) - unit * jnp.mean(grad * unit, -1, keepdims=True))


def forward_kernel(blocks, ctx_len, ctx_pad, parts,
                   place, queries, feats, cot, w_feat, w_mark, b_enc, w_qkv, b_qkv, w_out, b_out, gain_one, shift_one,
                   w_in, b_in, w_back, b_back, gain_two, shift_two, w_feat_t,
                   low_o, qkv_o, e_o, out_o, rows_o, back_o, shift_o, keep_o, give_o, aug_o,
                   mixed, inv, out_f, act_s, norm_s, d_hid_s, d_bra_s, d_att_s, g_out, g_in, g_back, wide, narrow):
    tick = pl.program_id(0)
    pad = low_o.shape[1]
    model = back_o.shape[2]
    step = pad // parts
    width = model // HEADS

    @pl.when(tick < blocks * HEADS)
    def _():
        block = tick // HEADS
        head = tick % HEADS

        @pl.when(head == 0)
        def _():
            def project(c, _):
                rows = pl.ds(pl.multiple_of(c * step, 16), step)
                low = embed(feats[block, rows, :], w_feat, w_mark, b_enc).astype(bf16)
                low_o[0, rows, :model] = low
                low_o[0, rows, model:] = feats[block, rows, :]
                made = (dot(low, w_qkv[...]) + b_qkv[...]).astype(bf16)
                for h in range(HEADS):
                    qkv_o[0, h, rows, :] = made[:, h * 3 * width:(h + 1) * 3 * width]
                return 0

            lax.fori_loop(0, parts, project, 0)

        factor = math.log2(math.e) / math.sqrt(width)
        keys = qkv_o[0, head, :ctx_pad, width:2 * width]
        vals = jnp.concatenate([qkv_o[0, head, :ctx_pad, 2 * width:], jnp.ones((ctx_pad, width), bf16)], 1)
        edge = ctx_len // LANES * LANES
        cols = pl.ds(pl.multiple_of(head * width, LANES), width)
        spans = [slice(c * step, (c + 1) * step) for c in range(parts)]

        def score(c):
            return dot_nt(qkv_o[0, head, spans[c], :width], keys)

        def weigh(c, scores):
            front = scores[:, :edge]
            most = jnp.max(front, 1, keepdims=True)
            if edge < ctx_pad:
                lane = lax.broadcasted_iota(jnp.int32, (step, ctx_pad - edge), 1)
                rear = jnp.where(lane < ctx_len - edge, scores[:, edge:], -1e30)
                most = jnp.maximum(most, jnp.max(rear, 1, keepdims=True))
                e_o[0, 0, spans[c], edge:] = jnp.exp2((rear - most) * factor).astype(bf16)
            e_o[0, 0, spans[c], :edge] = jnp.exp2((front - most) * factor).astype(bf16)

        def mix(c):
            summed = dot(e_o[0, 0, spans[c], :], vals)
            inverse = 1.0 / summed[:, width:]
            lane = lax.broadcasted_iota(jnp.int32, (step, LANES), 1)
            inv[block, spans[c], :] = jnp.where(lane == head, inverse[:, :LANES], inv[block, spans[c], :])
            mixed[block, spans[c], cols] = (summed[:, :width] * inverse).astype(bf16)

        ready = score(0)
        for c in range(parts):
            coming = score(c + 1) if c + 1 < parts else None
            weigh(c, ready)
            mix(c)
            ready = coming

    @pl.when(tick >= blocks * HEADS)
    def _():
        part = tick - blocks * HEADS

        @pl.when(part == 0)
        def _():
            for ref in (g_out, g_in, g_back, wide, narrow):
                ref[...] = jnp.zeros_like(ref)

        tiles = model // LANES
        rows = pl.ds(pl.multiple_of(part * step, 16), step)
        total = lambda v: jnp.sum(v, 0, keepdims=True)
        wide_t, narrow_t = [], [[] for _ in range(6)]

        def flow(block):
            here = slice(block * step, (block + 1) * step)
            mixed_low = mixed[block, rows, :]
            reached = embed(feats[block, rows, :], w_feat, w_mark, b_enc) + dot(mixed_low, w_out[...])
            yield
            unit_one, root_one = norm_parts(reached + b_out[...])
            normed = unit_one * gain_one[...] + shift_one[...]
            norm_s[here, :] = normed.astype(bf16)
            yield
            hidden = dot(norm_s[here, :], w_in[...])
            yield
            hidden = hidden + b_in[...]
            slant = math.sqrt(2.0 / math.pi)
            square = hidden * hidden
            half = 0.5 * jnp.tanh(hidden * (slant + (slant * 0.044715) * square)) + 0.5
            active = hidden * half
            act_s[here, :] = active.astype(bf16)
            slope = half + active * (1.0 - half) * (2.0 * slant + (6.0 * slant * 0.044715) * square)
            yield
            branch = dot(act_s[here, :], w_back[...])
            yield
            unit_two, root_two = norm_parts(normed + (branch + b_back[...]))
            row = part * step + lax.broadcasted_iota(jnp.int32, (step, 1), 0)
            alive = row < ctx_len + queries[block]
            result = jnp.where(alive, unit_two * gain_two[...] + shift_two[...], 0.0)
            given = []
            for j in range(tiles):
                lanes = pl.ds(j * blocks + block, step, stride=tiles * blocks)
                out_f[lanes, :] = result[:, j * LANES:(j + 1) * LANES]
                given.append(cot[lanes, :])
            grad = jnp.where(alive, jnp.concatenate(given, 1), 0.0)
            second = norm_back(grad * gain_two[...], unit_two, root_two)
            d_bra_s[here, :] = second.astype(bf16)
            narrow_t[3].append(total(d_bra_s[here, :].astype(f32)))
            narrow_t[4].append(total(grad * unit_two))
            narrow_t[5].append(total(grad))
            yield
            d_act = dot_nt(d_bra_s[here, :], w_back[...])
            yield
            d_hid = (slope * d_act).astype(bf16)
            d_hid_s[here, :] = d_hid
            wide_t.append(total(d_hid.astype(f32)))
            yield
            d_norm = dot_nt(d_hid_s[here, :], w_in[...])
            yield
            grad_one = second + d_norm
            narrow_t[1].append(total(grad_one * unit_one))
            narrow_t[2].append(total(grad_one))
            first = norm_back(grad_one * gain_one[...], unit_one, root_one)
            d_att_s[here, :] = first.astype(bf16)
            narrow_t[0].append(total(d_att_s[here, :].astype(f32)))
            yield
            back = dot_nt(d_att_s[here, :], w_out[...])
            rows_o[block] = dot(d_att_s[here, :], w_feat_t[...])
            yield
            back = back.astype(bf16).astype(f32)
            lane = lax.broadcasted_iota(jnp.int32, (step, LANES), 1)
            shifts = jnp.zeros((step, LANES), f32)
            for h in range(HEADS):
                cols = slice(h * width, (h + 1) * width)
                scaled = (back[:, cols] * inv[block, rows, h:h + 1]).astype(bf16)
                back_o[block, :, cols] = scaled
                moved = jnp.sum(scaled.astype(f32) * mixed_low[:, cols].astype(f32), 1, keepdims=True)
                shifts = jnp.where(lane == h, -moved, shifts)
            shift_o[block] = shifts
            yield

        flows = [flow(block) for block in range(blocks)]
        for item in flows:
            next(item)
        for turn in range(6):
            for item in flows:
                next(item)
                next(item, None)
            if turn == 2:
                g_back[...] += dot_tn(act_s[...], d_bra_s[...])
            if turn == 3:
                g_in[...] += dot_tn(norm_s[...], d_hid_s[...])
            if turn == 4:
                both = jnp.concatenate([jnp.concatenate([mixed[block, rows, :], feats[block, rows, :]], 1) for block in range(blocks)], 0)
                g_out[...] += dot_tn(both, d_att_s[...])
        out_o[...] = out_f[...].astype(bf16)
        wide[0:1, :] += sum(wide_t[1:], wide_t[0])
        for at in range(6):
            narrow[at:at + 1, :] += sum(narrow_t[at][1:], narrow_t[at][0])

        @pl.when(part == parts - 1)
        def _():
            def lay(start, ref, p, _):
                at = pl.multiple_of((p ^ place[0]) * 16, 16)
                ref[p - start, 0:16, :] = g_out[pl.ds(at, 16), :].astype(bf16)
                for j in range(2):
                    ref[p - start, 16 + 16 * j:32 + 16 * j, :] = g_in[pl.ds(at, 16), j * model:(j + 1) * model].astype(bf16)
                ref[p - start, 48:80, :] = g_back[pl.ds(pl.multiple_of(at * 2, 32), 32), :].astype(bf16)
                return 0

            for start, ref in ((0, keep_o), (CHUNKS // 2, give_o)):
                lax.fori_loop(start, start + CHUNKS // 2, functools.partial(lay, start, ref), 0)
            aug_o[:LANES, :] = g_out[model:, :]
            aug_o[LANES:, :] = jnp.zeros((LANES, model), f32)
            aug_o[LANES:LANES + 6, :] = narrow[0:6, :]
            for j in range(2):
                aug_o[LANES + 6 + j:LANES + 7 + j, :] = wide[0:1, j * model:(j + 1) * model]


def forward(place, queries, feats, cot, weights, ctx_len):
    blocks, pad, _ = feats.shape
    model = weights[3].shape[0]
    inner = weights[9].shape[1]
    width = model // HEADS
    ctx_pad = round_up(ctx_len, LANES)
    parts = row_chunks(pad)
    step = pad // parts
    early = blocks * HEADS
    flat = blocks * model // LANES
    attending = lambda t: jnp.minimum(t, early - 1)
    later = lambda t: jnp.maximum(t - early, 0)
    once = lambda a: pl.BlockSpec(a.shape, lambda *_: (0,) * a.ndim, pipeline_mode=pl.Buffered(1))
    full = lambda *s: pl.BlockSpec(s, lambda *_: (0,) * len(s))
    rowed = lambda w: pl.BlockSpec((blocks, step, w), lambda t, *_: (0, later(t), 0))
    shape = jax.ShapeDtypeStruct
    return pl.pallas_call(
        functools.partial(forward_kernel, blocks, ctx_len, ctx_pad, parts),
        grid_spec=pltpu.PrefetchScalarGridSpec(
            num_scalar_prefetch=2,
            grid=(early + parts,),
            in_specs=[once(feats), pl.BlockSpec((step * flat, LANES), lambda t, *_: (later(t), 0))] + [once(a) for a in weights],
            out_specs=[
                pl.BlockSpec((1, pad, model + LANES), lambda t, *_: (attending(t) // HEADS, 0, 0)),
                pl.BlockSpec((1, HEADS, pad, 3 * width), lambda t, *_: (attending(t) // HEADS, 0, 0, 0)),
                pl.BlockSpec((1, 1, pad, ctx_pad), lambda t, *_: (attending(t) // HEADS, attending(t) % HEADS, 0, 0)),
                pl.BlockSpec((step * flat, LANES), lambda t, *_: (later(t), 0)),
                rowed(LANES), rowed(model), rowed(LANES),
                full(CHUNKS // 2, 80, model), full(CHUNKS // 2, 80, model), full(2 * LANES, model)],
            scratch_shapes=[
                pltpu.VMEM((blocks, pad, model), bf16), pltpu.VMEM((blocks, pad, LANES), f32), pltpu.VMEM((step * flat, LANES), f32),
                pltpu.VMEM((blocks * step, inner), bf16), pltpu.VMEM((blocks * step, model), bf16),
                pltpu.VMEM((blocks * step, inner), bf16), pltpu.VMEM((blocks * step, model), bf16),
                pltpu.VMEM((blocks * step, model), bf16), pltpu.VMEM((model + LANES, model), f32), pltpu.VMEM((model, inner), f32),
                pltpu.VMEM((inner, model), f32), pltpu.VMEM((8, inner), f32), pltpu.VMEM((8, model), f32)],
        ),
        out_shape=[
            shape((blocks, pad, model + LANES), bf16), shape((blocks, HEADS, pad, 3 * width), bf16),
            shape((blocks, HEADS, pad, ctx_pad), bf16), shape(cot.shape, bf16), shape((blocks, pad, LANES), f32),
            shape((blocks, pad, model), bf16), shape((blocks, pad, LANES), f32), shape((CHUNKS // 2, 80, model), bf16),
            shape((CHUNKS // 2, 80, model), bf16), shape((2 * LANES, model), f32)],
        compiler_params=params(0),
        cost_estimate=cost(60, 1),
        name="forward",
    )(place, queries, feats, cot, *weights)


def scores_kernel(head, ctx_pad, parts, place, e, qkv, back, shift, low, w_head, w_rows, d_rows, aug, *refs):
    last = head == HEADS - 1
    done, refs = (refs[:head], refs[head:]) if last else ((), refs)
    if last:
        keep_o, give_o, rows_o, ds, dox, d_all, g_scr, aug_s = refs
    else:
        g_o, rows_o, aug_o, ds, dox, d_all, g_scr, aug_s = refs
    block = pl.program_id(0)
    pad = back.shape[1]
    model = aug.shape[1]
    step = pad // parts
    width = back.shape[2]
    root = 1.0 / math.sqrt(width)
    keys = qkv[0, 0, :ctx_pad, width:2 * width]
    vals = jnp.concatenate([qkv[0, 0, :ctx_pad, 2 * width:], jnp.ones((ctx_pad, width), bf16)], 1)
    lane = lax.broadcasted_iota(jnp.int32, (pad, width), 1)
    moved = shift[0, :, head:head + 1]
    top = moved.astype(bf16).astype(f32)
    dox[:, :width] = back[0]
    dox[:, width:] = jnp.where(lane == 0, top, jnp.where(lane == 1, moved - top, 0.0)).astype(bf16)
    spans = [slice(c * step, (c + 1) * step) for c in range(parts)]

    def score(c):
        return dot_nt(dox[spans[c], :], vals)

    ready = score(0)
    for c in range(parts):
        coming = score(c + 1) if c + 1 < parts else None
        ds[spans[c], :] = e[0, 0, spans[c], :] * ready.astype(bf16)
        d_all[spans[c], :width] = (dot(ds[spans[c], :], keys) * root).astype(bf16)
        ready = coming
    d_all[:ctx_pad, 2 * width:] = dot_tn(back[0], e[0, 0]).T.astype(bf16)
    d_all[:ctx_pad, width:2 * width] = (dot_tn(qkv[0, 0, :, :width], ds[...]) * root).T.astype(bf16)
    d_all[ctx_pad:, width:] = jnp.zeros((pad - ctx_pad, 2 * width), bf16)
    grads = dot_tn(low[0], d_all[...])
    sums = jnp.sum(d_all[...].astype(f32), 0, keepdims=True)
    pair = dot(d_all[...], w_rows[0])
    rows_o[0] = d_rows[0] + (pair[:, :LANES] + pair[:, LANES:])
    cols = slice(head * width, (head + 1) * width)

    @pl.when(block == 0)
    def _():
        g_scr[...] = grads
        aug_s[...] = aug[...]

    @pl.when(block > 0)
    def _():
        g_scr[...] += grads

    aug_s[LANES + 8:LANES + 9, cols] += sums[:, :width]
    aug_s[LANES + 9:LANES + 10, cols] += sums[:, 2 * width:]

    @pl.when(block == pl.num_programs(0) - 1)
    def _():
        feat_part = g_scr[model:, :]
        high = feat_part.astype(bf16)
        both = jnp.concatenate([high, (feat_part - high.astype(f32)).astype(bf16)], 0)
        fitted = dot(both, w_head[0])
        aug_s[:LANES, :] += fitted[:LANES] + fitted[LANES:]
        half = model // 2

        def lay(start, ref, p, _):
            at = p ^ place[0]
            rows = pl.ds(pl.multiple_of(at * 16, 16), 16)
            if not last:
                ref[p - start] = g_scr[rows, :].astype(bf16)
                return 0
            for h in range(head):
                ref[p - start, :, h * 3 * width:(h + 1) * 3 * width] = done[h][p]
            ref[p - start, :, head * 3 * width:3 * model] = g_scr[rows, :].astype(bf16)
            spot = pl.ds(pl.multiple_of(at // 2 * 16, 16), 16)
            ref[p - start, :, 3 * model:] = aug_s[spot, pl.ds(pl.multiple_of(at % 2 * half, half), half)].astype(bf16)
            return 0

        if last:
            for start, ref in ((0, keep_o), (CHUNKS // 2, give_o)):
                lax.fori_loop(start, start + CHUNKS // 2, functools.partial(lay, start, ref), 0)
        else:
            lax.fori_loop(0, CHUNKS, functools.partial(lay, 0, g_o), 0)
            aug_o[...] = aug_s[...]


def score_grads(place, head, e, qkv, back, shift, low, w_head, w_rows, d_rows, aug, done):
    blocks, pad, model = back.shape
    ctx_pad = e.shape[3]
    width = model // HEADS
    parts = row_chunks(pad)
    last = head == HEADS - 1
    full = lambda *s: pl.BlockSpec(s, lambda *_: (0,) * len(s))
    rowed = pl.BlockSpec((1, pad, LANES), lambda b, *_: (b, 0, 0))
    shape = jax.ShapeDtypeStruct
    ends = [(CHUNKS // 2, 16, 3 * model + model // 2)] * 2 if last else [(CHUNKS, 16, 3 * width)]
    out_specs = [full(*s) for s in ends] + [rowed]
    out_shape = [shape(s, bf16) for s in ends] + [shape((blocks, pad, LANES), f32)]
    if not last:
        out_specs.append(full(2 * LANES, model))
        out_shape.append(shape((2 * LANES, model), f32))
    return pl.pallas_call(
        functools.partial(scores_kernel, head, ctx_pad, parts),
        grid_spec=pltpu.PrefetchScalarGridSpec(
            num_scalar_prefetch=1,
            grid=(blocks,),
            in_specs=[pl.BlockSpec((1, 1, pad, ctx_pad), lambda b, *_: (b, head, 0, 0)),
                      pl.BlockSpec((1, 1, pad, 3 * width), lambda b, *_: (b, head, 0, 0)),
                      pl.BlockSpec((1, pad, width), lambda b, *_: (b, 0, head)),
                      rowed,
                      pl.BlockSpec((1, pad, model + LANES), lambda b, *_: (b, 0, 0)),
                      pl.BlockSpec((1, 3 * width, model), lambda b, *_: (head, 0, 0)),
                      pl.BlockSpec((1, 3 * width, 2 * LANES), lambda b, *_: (head, 0, 0)),
                      rowed, full(2 * LANES, model)] + [full(*d.shape) for d in done if last],
            out_specs=out_specs,
            scratch_shapes=[pltpu.VMEM((pad, ctx_pad), bf16), pltpu.VMEM((pad, 2 * width), bf16), pltpu.VMEM((pad, 3 * width), bf16),
                            pltpu.VMEM((model + LANES, 3 * width), f32), pltpu.VMEM((2 * LANES, model), f32)],
        ),
        out_shape=out_shape,
        compiler_params=params(0),
        cost_estimate=cost(10, 1),
        name="score_grads",
    )(place, e, qkv, back, shift, low, w_head, w_rows, d_rows, aug, *(done if last else ()))


def spread_kernel(span, own, ids, rows, out_o, *tables):
    blocks = rows.shape[0]
    count, feats, col_width, _ = out_o.shape
    for table in tables:
        table[...] = jnp.zeros_like(table)
    each = len(tables) // blocks if len(tables) > 1 else 1
    run = span // each
    unit = next(u for u in (10, 5, 2, 1) if run % u == 0)

    def add(i, _):
        for u in range(unit):
            for t in range(blocks * each):
                block, at = t // each, t % each * run + i * unit + u
                table = tables[t % len(tables)]
                spot = pl.ds(ids[block * span + at], 1)
                table[spot, :] += rows[block, pl.ds(at, 1), :]
        return 0

    lax.fori_loop(0, run // unit, add, 0)

    def fold(g, _):
        spot = pl.ds(pl.multiple_of(g * own, own), own)
        total = tables[0][spot, :]
        for table in tables[1:]:
            total = total + table[spot, :]
        total = total.T
        for f in range(feats):
            at = f * (col_width + 1)
            out_o[g, f] = total[at:at + col_width].astype(bf16)
        return 0

    lax.fori_loop(0, count, fold, 0)


def spread(ids, rows, count, feats, col_width, own):
    span = ids.shape[0] // rows.shape[0]
    tables = 4 if count <= 8 and span % 2 == 0 else 1
    return pl.pallas_call(
        functools.partial(spread_kernel, span, own),
        grid_spec=pltpu.PrefetchScalarGridSpec(
            num_scalar_prefetch=1,
            grid=(1,),
            in_specs=[pl.BlockSpec(rows.shape, lambda *_: (0, 0, 0))],
            out_specs=pl.BlockSpec((count, feats, col_width, own), lambda *_: (0, 0, 0, 0)),
            scratch_shapes=[pltpu.VMEM((count * own, LANES), f32)] * tables,
        ),
        out_shape=jax.ShapeDtypeStruct((count, feats, col_width, own), bf16),
        compiler_params=params(0),
        cost_estimate=cost(7, 1),
        name="spread",
    )(ids, rows)


def chosen(p, near, far):
    half = CHUNKS // 2
    at = p % half
    return lambda *spot: jnp.where(p < half, near[(at, *spot)].astype(f32), far[(at, *spot)].astype(f32))


def finish_kernel(place, near, far, out_o, in_o, back_o):
    step = pl.program_id(0)
    model = out_o.shape[1]
    each = out_o.shape[0] // 16
    for u in range(each):
        take = chosen((step * each + u) ^ place[0], near, far)
        rows = slice(u * 16, (u + 1) * 16)
        out_o[rows, :] = take(slice(0, 16))
        for j in range(2):
            in_o[rows, j * model:(j + 1) * model] = take(slice(16 + 16 * j, 32 + 16 * j))
        back_o[u * 32:(u + 1) * 32, :] = take(slice(48, 80))


def finish(place, near, far):
    model = near.shape[2]
    steps = 8
    shapes = [(model, model), (model, 2 * model), (2 * model, model)]
    return pl.pallas_call(
        finish_kernel,
        grid_spec=pltpu.PrefetchScalarGridSpec(
            num_scalar_prefetch=1,
            grid=(steps,),
            in_specs=[pl.BlockSpec(a.shape, lambda *_: (0, 0, 0)) for a in (near, far)],
            out_specs=[pl.BlockSpec((s[0] // steps, s[1]), lambda i, *_: (i, 0)) for s in shapes],
        ),
        out_shape=[jax.ShapeDtypeStruct(s, f32) for s in shapes],
        compiler_params=params(0),
        cost_estimate=cost(5, 1),
        name="finish",
    )(place, near, far)


def finish_tail_kernel(col_width, classes, place, near, far, q_o, k_o, v_o, enc_o, bias_o, mark_o, wide_o, *refs):
    lines, aug = refs[:-1], refs[-1]
    step = pl.program_id(0)
    model = q_o.shape[1]
    width = model // HEADS
    half = model // 2
    each = q_o.shape[0] // 16
    for u in range(each):
        take = chosen((step * each + u) ^ place[0], near, far)
        rows = slice(u * 16, (u + 1) * 16)
        for head in range(HEADS):
            cols = slice(head * width, (head + 1) * width)
            for j, ref in enumerate((q_o, k_o, v_o)):
                at = (head * 3 + j) * width
                ref[rows, cols] = take(slice(None), slice(at, at + width))

    @pl.when(step == 0)
    def _():
        for c in range(CHUNKS):
            take = chosen(c ^ place[0], near, far)
            aug[c // 2 * 16:c // 2 * 16 + 16, c % 2 * half:(c % 2 + 1) * half] = take(slice(None), slice(3 * model, None))
        feats = enc_o.shape[0] // col_width
        for f in range(feats):
            enc_o[f * col_width:(f + 1) * col_width, :] = aug[f * (col_width + 1):f * (col_width + 1) + col_width, :]
        at = feats * (col_width + 1)
        mark_o[...] = aug[at:at + classes, :]
        bias_o[...] = aug[at + classes:at + classes + 1, :]
        for j in range(2):
            wide_o[:, j * model:(j + 1) * model] = aug[LANES + 6 + j:LANES + 7 + j, :]
        for line, row in zip(lines, (0, 1, 2, 3, 4, 5, 8, 9)):
            line[...] = aug[LANES + row:LANES + row + 1, :]


def finish_tail(place, near, far, model, feat_total, col_width, classes):
    steps = 8
    shapes = [(model, model)] * 3
    singles = [(feat_total, model), (1, model), (classes, model), (1, 2 * model)] + [(1, model)] * 8
    full = lambda *s: pl.BlockSpec(s, lambda *_: (0,) * len(s))
    return pl.pallas_call(
        functools.partial(finish_tail_kernel, col_width, classes),
        grid_spec=pltpu.PrefetchScalarGridSpec(
            num_scalar_prefetch=1,
            grid=(steps,),
            in_specs=[full(*a.shape) for a in (near, far)],
            out_specs=[pl.BlockSpec((s[0] // steps, s[1]), lambda i, *_: (i, 0)) for s in shapes] + [full(*s) for s in singles],
            scratch_shapes=[pltpu.VMEM((2 * LANES, model), f32)],
        ),
        out_shape=[jax.ShapeDtypeStruct(s, f32) for s in shapes + singles],
        compiler_params=params(0),
        cost_estimate=cost(5, 1),
        name="finish_tail",
    )(place, near, far)


SLOTS = (0, 1, 0, 1, 1)
SPAN = 64.0


def swap(value, axis, bit):
    size = lax.axis_size(axis)
    return lax.ppermute(value, axis, [(i, i ^ bit) for i in range(size)])


def rounded(value):
    return lax.reduce_precision(value, 8, 7)


def exchange(value, axis):
    return lax.all_to_all(value, axis, split_axis=0, concat_axis=0, tiled=True)


def chunk_steps(keep, give, bits):
    split = CHUNKS.bit_length() - 1
    for at, (axis, bit) in enumerate(bits):
        came = swap(give, axis, bit)
        if at + 1 < split:
            half = keep.shape[0] // 2
            give = (keep[half:].astype(f32) + came[half:].astype(f32)).astype(bf16)
            keep = keep[:half].astype(f32) + came[:half].astype(f32)
        else:
            give = keep = (keep.astype(f32) + came.astype(f32)).astype(bf16)
        fixed = yield give
        if fixed is not None:
            give = fixed
    for axis, bit in reversed(bits[1:split]):
        keep = jnp.concatenate([keep, swap(keep, axis, bit)], 0)
        yield keep
    yield keep, swap(keep, *bits[0])


def body(
    raw_rows, enc_weight, enc_bias, label_table, w_query, b_query, w_key, w_value, b_value, w_out, b_out,
    gain_one, shift_one, w_in, b_in, w_back, b_back, gain_two, shift_two, members, labels, queries, cotangent,
):
    row_count = lax.axis_size("rows")
    feat_count = lax.axis_size("feat")
    row_index = lax.axis_index("rows")
    feat_index = lax.axis_index("feat")
    local_rows, col_width = raw_rows.shape
    own_rows = local_rows // feat_count
    feat_total = col_width * feat_count
    feat_span = feat_total + feat_count
    model = enc_weight.shape[1]
    width = model // HEADS
    classes = label_table.shape[0]
    blocks, span = members.shape
    ctx_len = labels.shape[1]
    pad = round_up(span, 16)
    row_total = float(local_rows * row_count)
    bits = [(axis, 1 << b) for axis in ("feat", "rows") for b in range(lax.axis_size(axis).bit_length() - 1)]
    place = jnp.int32(0)
    for at, (axis, bit) in enumerate(bits[:CHUNKS.bit_length() - 1]):
        place = place + lax.axis_index(axis) // bit % 2 * (CHUNKS >> (at + 1))
    place = place.reshape(1).astype(jnp.int32)
    row = lambda a: a.reshape(1, -1)

    columns = raw_rows.T
    origin = rounded(jnp.mean(columns, 1, keepdims=True))
    moved = columns - origin
    sums = [origin[:, 0]]
    for value, scales in ((jnp.mean(moved, 1), (1.0, 1024.0, 1048576.0)), (jnp.mean(moved * moved, 1), (0.0625, 64.0, 65536.0))):
        for scale in scales:
            top = lax.reduce_precision(value * scale, 5, 10)
            sums.append(top)
            value = value - top / scale
    moved = moved * SPAN
    notes = jnp.pad(jnp.stack(sums), ((0, 1), (0, 32 - col_width))).reshape(1, 1, 2 * LANES)
    notes = jnp.broadcast_to(jnp.pad(notes, ((0, 0), (0, 0), (0, own_rows - 2 * LANES))), (feat_count, 1, own_rows))
    moved = moved.reshape(col_width, feat_count, own_rows).transpose(1, 0, 2)
    sent = jnp.concatenate([moved, notes], 1).astype(jnp.float16)
    owned = exchange(sent, "feat").reshape(1, feat_span, own_rows)
    near = jnp.concatenate([owned] + [swap(owned, "rows", bits) for bits in (2, 4, 6)], 0)
    for bit in range(3, row_count.bit_length() - 1):
        near = jnp.concatenate([near, swap(near, "rows", 1 << bit)], 0)
    far = swap(near, "rows", 1)
    groups = jnp.concatenate([near[:, col_width::col_width + 1, :2 * LANES], far[:, col_width::col_width + 1, :2 * LANES]], 0)
    notes = groups.astype(f32).reshape(row_count, feat_count, 8, 32)[:, :, :, :col_width]
    origins = notes[:, :, 0]
    first_means = notes[:, :, 1] + notes[:, :, 2] / 1024.0 + notes[:, :, 3] / 1048576.0
    square_means = notes[:, :, 4] * 16.0 + notes[:, :, 5] / 64.0 + notes[:, :, 6] / 65536.0
    col_mean = jnp.mean(origins + first_means, 0)
    apart = origins - col_mean
    factor = lax.rsqrt(jnp.mean(square_means + apart * (2.0 * first_means + apart), 0) + epsilon)
    wider = lambda v: jnp.pad(v, ((0, 0), (0, 0), (0, 1))).reshape(v.shape[0], feat_span, 1)
    apart, slope = wider(apart), wider(factor[None])
    standard = lambda part, off: ((part.astype(f32) * (1.0 / SPAN) + off) * slope).astype(bf16)
    near, far = standard(near, apart[:row_count // 2]), standard(far, apart[row_count // 2:])
    source = members // local_rows
    ids_back = (source * own_rows + members % own_rows).reshape(-1)
    source = source ^ row_index
    source = ((source >> 1) & 3) + 4 * (source >> 3) + (source & 1) * (row_count // 2)
    ids = (source * own_rows + members % own_rows).reshape(-1)

    spaced = jnp.pad(enc_weight.reshape(feat_count, col_width, model), ((0, 0), (0, 1), (0, 0))).reshape(feat_span, model)
    w_feat = jnp.pad(spaced, ((0, LANES - feat_span), (0, 0)))
    w_mark = jnp.pad(label_table, ((feat_span, LANES - feat_span - classes), (0, 0)))
    b_enc = row(enc_bias)
    mark = jnp.pad(labels, ((0, 0), (0, pad - ctx_len)), constant_values=-2 * LANES)[:, :, None]
    cut = lambda w: w.reshape(model, HEADS, 1, width)
    w_qkv = jnp.concatenate([cut(w_query), cut(w_key), cut(w_value)], 2).reshape(model, 3 * model)
    edge = lambda b: b.reshape(1, HEADS, 1, width)
    b_qkv = jnp.concatenate([edge(b_query), edge(jnp.zeros_like(b_query)), edge(b_value)], 2).reshape(1, 3 * model)
    w_heads = w_qkv.T.reshape(HEADS, 3 * width, model)
    w_feat_t = w_feat.T
    w_rows = jnp.einsum("hkd,df->hkf", w_heads, w_feat_t, preferred_element_type=f32)
    high = rounded(w_rows)
    w_rows = jnp.concatenate([high, w_rows - high], 2).astype(bf16)
    tiles = model // LANES
    flat = cotangent.transpose(1, 0, 2).reshape(span, blocks, tiles, LANES).transpose(0, 2, 1, 3).reshape(-1, LANES)

    feats = fetch(ids, near, far, mark, feat_span, classes)
    weights = (w_feat, w_mark, b_enc, w_qkv, b_qkv, w_out, row(b_out), row(gain_one), row(shift_one), w_in, row(b_in),
               w_back, row(b_back), row(gain_two), row(shift_two), w_feat_t)
    low, qkv, expo, layer_out, d_rows, back, shift, keep, give, aug = forward(place, queries, feats, flat, weights, ctx_len)
    layer_out = layer_out.reshape(span, tiles, blocks, LANES).transpose(0, 2, 1, 3).reshape(span, blocks, model).transpose(1, 0, 2)

    steps = chunk_steps(keep, give, bits)
    done = []
    for head in range(HEADS):
        for _ in range(SLOTS[head]):
            held, back = lax.optimization_barrier((next(steps), back))
        made = score_grads(place, head, expo, qkv, back, shift, low, w_heads, w_rows, d_rows, aug, done)
        if head < HEADS - 1:
            head_grads, d_rows, aug = made
            done.append(head_grads)
        else:
            keep, give, d_rows = made
    tail = chunk_steps(keep, give, bits)
    for _ in range(SLOTS[HEADS]):
        held, d_rows = lax.optimization_barrier((next(steps), d_rows))

    d_table = spread(ids_back, d_rows, row_count, feat_count, col_width, own_rows)
    held, d_table = lax.optimization_barrier((next(tail), d_table))
    tail.send(held)
    d_table = exchange(d_table.reshape(row_count * feat_count, col_width, own_rows), ("rows", "feat"))
    d_columns = jnp.sum(d_table.reshape(row_count, feat_count, col_width, own_rows).astype(f32), 0)
    d_columns = d_columns.transpose(1, 0, 2).reshape(col_width, local_rows)
    for ends in tail:
        pass
    (g_query, g_key, g_value, g_enc, g_enc_bias, g_table, g_b_in, g_b_out, g_gain_one, g_shift_one, g_b_back, g_gain_two,
     g_shift_two, g_b_query, g_b_value) = finish_tail(place, *ends, model, feat_total, col_width, classes)
    for ends in steps:
        pass
    g_out, g_in, g_back = finish(place, *ends)

    at = feat_index * col_width
    weight = lax.dynamic_slice_in_dim(enc_weight, at, col_width, 0).astype(f32)
    stat_one = jnp.sum(weight * g_enc_bias, 1)
    stat_two = jnp.sum(weight * lax.dynamic_slice_in_dim(g_enc, at, col_width, 0), 1)
    col_mean = lax.dynamic_slice_in_dim(col_mean, feat_index, 1, 0)[0]
    factor = lax.dynamic_slice_in_dim(factor, feat_index, 1, 0)[0]
    d_spread = -0.5 * stat_two * factor * factor
    d_mean = -factor * stat_one - 2.0 * d_spread * col_mean
    raw_grad = factor[:, None] * d_columns + (d_mean[:, None] + 2.0 * d_spread[:, None] * columns) / row_total
    flatten = lambda a: a.reshape(-1)
    return (
        layer_out, raw_grad.T, g_enc, flatten(g_enc_bias), g_table, g_query, flatten(g_b_query), g_key, g_value,
        flatten(g_b_value), g_out, flatten(g_b_out), flatten(g_gain_one), flatten(g_shift_one), g_in, flatten(g_b_in), g_back,
        flatten(g_b_back), flatten(g_gain_two), flatten(g_shift_two),
    )


def solution(mesh):
    both = ("rows", "feat")
    placed = (P("rows", "feat"),) + (P(),) * 18 + (P(both, None), P(both, None), P(both), P(both, None, None))
    results = (P(both, None, None), P("rows", "feat")) + (P(),) * 18
    return jax.shard_map(body, mesh=mesh, in_specs=placed, out_specs=results, check_vma=False)
```

time: 338 us -> 267 us (0.79)
  local copies, waits for them, and re-layouts: 58.9 us -> 20.6 us
  waiting for transfers between devices: 52.4 us -> 33 us
  Pallas kernels: 152 us -> 136 us
  starting transfers between devices: 46.4 us -> 59.2 us
  blocking collectives: 10.3 us -> 0 us
    unnamed x48 -> x43, local copies, waits for them, and re-layouts: 31.9 us -> 8.08 us
    ppermute x29 -> x24, waiting for transfers between devices: 52.4 us -> 33 us  [swap(): return lax.ppermute(value, axis, [(i, i ^ bit) for i in range(size)])]
    pallas_call x8 -> x7, Pallas kernels: 139 us -> 123 us  [the longest x1 61.2 us: forward(): pl.pallas_call(functools.partial(forward_kernel, blocks, ctx_len, ctx_pad...]
    slice x19 -> x3, local copies, waits for them, and re-layouts: 12.8 us -> 1.95 us  [the longest x1 0.97 us: body(): far[:, col_width::col_width + 1, :2 * LANES]]
    all_to_all x1 -> x0, blocking collectives: 10.3 us -> none  [body(): lax.all_to_all(standard, 'feat', split_axis=0, concat_axis=0, tiled=True)]
    all_to_all x1 -> x2, starting transfers between devices: 5.43 us -> 12.8 us  [exchange(): return lax.all_to_all(value, axis, split_axis=0, concat_axis=0, tiled=True)]
    ppermute x29 -> x24, starting transfers between devices: 41 us -> 46.4 us  [swap(): return lax.ppermute(value, axis, [(i, i ^ bit) for i in range(size)])]
    concatenate x5 -> x6, local copies, waits for them, and re-layouts: 7.57 us -> 2.67 us  [the longest x2 1.74 us: chunk_steps(): keep = jnp.concatenate([keep, swap(keep, axis, bit)], 0)]
  transfers between devices with their start and end apart: 30 -> 26, of which waited for: 13 -> 13; matrix products, arithmetic and copies ran while one was open for 19% -> 8% of each run, Pallas kernels for 4% -> 24%
where the time goes in v2:
time: 267 us; the launch traced here: 263 us
  Pallas kernels  136 us (51%)
  starting transfers between devices  59.2 us (22%)
  waiting for transfers between devices  33 us (12%)
  local copies, waits for them, and re-layouts  20.6 us (8%)
  other arithmetic  12.3 us (5%)
    pallas_call x1, Pallas kernels, forward(): pl.pallas_call(functools.partial(forward_kernel, blocks, ctx_len, ctx_pad...  61.2 us
    pallas_call x4, Pallas kernels, score_grads(): pl.pallas_call(functools.partial(scores_kernel, head, ctx_pad, parts), gr...  49.8 us
    ppermute x24, starting transfers between devices, swap(): return lax.ppermute(value, axis, [(i, i ^ bit) for i in range(size)])  46.4 us
    ppermute x24, waiting for transfers between devices, swap(): return lax.ppermute(value, axis, [(i, i ^ bit) for i in range(size)])  33 us
    all_to_all x2, starting transfers between devices, exchange(): return lax.all_to_all(value, axis, split_axis=0, concat_axis=0, tiled=True)  12.8 us
    unnamed x43, local copies, waits for them, and re-layouts  8.08 us
    pallas_call x1, Pallas kernels, spread(): pl.pallas_call(functools.partial(spread_kernel, span, own), grid_spec=plt...  7.56 us
    pallas_call x1, Pallas kernels, fetch(): pl.pallas_call(functools.partial(fetch_kernel, ids.shape[0] // blocks, fe...  6.6 us
  transfers between devices with their start and end apart: 26, of which 13 were waited for; matrix products, arithmetic and copies ran while one was open for 8% of the time, Pallas kernels for 24%

profile of v2, /device:TPU:1, one launch (start us, length us, event | category | flops | bytes accessed | tf_op | source)
XLA Modules:
  0.0 262.8 jit_solution(5770400898917471940)
XLA Ops:
  0.7 1.1 reduce_sum.72
  1.8 1.2 multiply_reduce_fusion
  4.0 4.3 %all-to-all-start = ((f16[4,26,512]{2,1,0:T(8,128)(2,1)}), f16[4,26,512]{2,1,0:T(8,128)(2,1)S(1)}, u32[]{:S(2)}, u32[]{:S(2)}) async-start(f16[4,26,512]{2,1,0:T(8,128)(2,1)} %pad_maximum_fusion.7), calls=%async_computation | async-start | bytes 262144 | tf_op jit(solution)/shard_map/all_to_all | solution.py:624
  9.2 1.4 copy.92.mark
  13.0 1.9 collective-permute-start
  14.9 2.3 collective-permute-start.1
  18.9 1.2 collective-permute-done.1
  20.7 4.1 %collective-permute-done.2 = f16[1,104,512]{2,1,0:T(8,128)(2,1)S(1)} collective-permute-done((f16[1,104,512]{2,1,0:T(8,128)(2,1)S(1)}, f16[1,104,512]{2,1,0:T(8,128)(2,1)S(1)}, u32[]{:S(2)}, u32[]{:S(2)}) %collective-permute-start.2) | collective-permute-done | bytes 106528 | tf_op jit(solution)/shard_map/ppermute | solution.py:616
  25.5 1.2 collective-permute-start.3
  26.9 1.7 copy.99.w_qkv
  30.0 1.0 slice.139
  31.1 3.6 %collective-permute-done.3 = f16[4,104,512]{2,1,0:T(8,128)(2,1)} collective-permute-done((f16[4,104,512]{2,1,0:T(8,128)(2,1)}, f16[4,104,512]{2,1,0:T(8,128)(2,1)}, u32[]{:S(2)}, u32[]{:S(2)}) %collective-permute-start.3) | collective-permute-done | bytes 426016 | tf_op jit(solution)/shard_map/ppermute | solution.py:616
  34.7 1.0 slice.140
  36.2 2.3 multiply_convert_fusion
  38.6 6.6 %fetch.1.feats = bf16[2,1104,128]{2,1,0:T(8,128)(2,1)} custom-call(s32[2200]{0:T(1024)} %reshape.358.ids, bf16[4,104,512]{2,1,0:T(8,128)(2,1)} %get-tuple-element.148.near, bf16[4,104,512]{2,1,0:T(8,128)(2,1)} %get-tuple-element.147.far, s32[2,1104,1]{2,1,0:T(8,128)} %copy.92.mark), custom_call_target="tpu_custom_call" | custom-call | flops 6000000000 | bytes 1000000 | tf_op jit(solution)/shard_map/fetch/pallas_call | solution.py:81
  45.2 61.2 %forward.1 = (bf16[2,1104,640]{2,1,0:T(8,128)(2,1)}, bf16[2,4,1104,384]{3,2,1,0:T(8,128)(2,1)}, bf16[2,4,1104,1024]{3,2,1,0:T(8,128)(2,1)}, bf16[8800,128]{1,0:T...) custom-call(s32[1]{0:T(128)} %bitcast.place, ...), custom_call_target="tpu_custom_call" | custom-call | flops 60000002048 | bytes 1000000 | tf_op jit(solution)/shard_map/forward/pallas_call | solution.py:313
  106.4 3.4 %collective-permute-start.4 = (bf16[16,80,512]{2,1,0:T(8,128)(2,1)}, bf16[16,80,512]{2,1,0:T(8,128)(2,1)S(1)}, u32[]{:S(2)}, u32[]{:S(2)}) collective-permute-start(bf16[16,80,512]{2,1,0:T(8,128)(2,1)} %get-tuple-element.69), channel_id=1, source_target_pairs={{0,1},{1,0},{2,3},{3,2},{4,5},{5,4},{6,7},{7,6},{8,9},{9,8},{10,11... | collective-permute-start | bytes 3932168 | tf_op jit(solution)/shard_map/ppermute | solution.py:616
  110.4 1.0 pad_maximum_fusion.1.w_rows
  111.3 12.2 %score_grads.4 = (bf16[32,16,384]{2,1,0:T(8,128)(2,1)}, f32[2,1104,128]{2,1,0:T(8,128)}, f32[256,512]{1,0:T(8,128)}) custom-call(s32[1]{0:T(128)} %bitcast.place, bf16[2,4,1104,1024]{3,2,1,0:T(8,128)(2,1)} %get-tuple-element.66.e, bf16[2,4,1104,384]{3,2,1,0:T(8,128)(2,1)} %get-tuple-element.67.qkv, bf16[2,1104,512]{2,1,0:T(8,128)(2,1)} %get-tuple-element.72.back, ...), custom_call_target="tpu_custom_call" | custom-call | flops 10000000000 | bytes 1000000 | tf_op jit(solution)/shard_map/score_grads/pallas_call | solution.py:441
  123.5 1.2 add_convert_fusion
  124.8 1.0 collective-permute-start.5
  125.8 12.1 %score_grads.5 = (bf16[32,16,384]{2,1,0:T(8,128)(2,1)}, f32[2,1104,128]{2,1,0:T(8,128)}, f32[256,512]{1,0:T(8,128)}) custom-call(s32[1]{0:T(128)} %bitcast.place, bf16[2,4,1104,1024]{3,2,1,0:T(8,128)(2,1)} %get-tuple-element.66.e, bf16[2,4,1104,384]{3,2,1,0:T(8,128)(2,1)} %get-tuple-element.67.qkv, bf16[2,1104,512]{2,1,0:T(8,128)(2,1)} %get-tuple-element.72.back, ...), custom_call_target="tpu_custom_call" | custom-call | flops 10000000000 | bytes 1000000 | tf_op jit(solution)/shard_map/score_grads/pallas_call | solution.py:441
  138.0 12.1 %score_grads.6 = (bf16[32,16,384]{2,1,0:T(8,128)(2,1)}, f32[2,1104,128]{2,1,0:T(8,128)}, f32[256,512]{1,0:T(8,128)}) custom-call(s32[1]{0:T(128)} %bitcast.place, bf16[2,4,1104,1024]{3,2,1,0:T(8,128)(2,1)} %get-tuple-element.66.e, bf16[2,4,1104,384]{3,2,1,0:T(8,128)(2,1)} %get-tuple-element.67.qkv, bf16[2,1104,512]{2,1,0:T(8,128)(2,1)} %get-tuple-element.72.back, ...), custom_call_target="tpu_custom_call" | custom-call | flops 10000000000 | bytes 1000000 | tf_op jit(solution)/shard_map/score_grads/pallas_call | solution.py:441
  150.3 1.3 collective-permute-start.7
  151.6 13.3 %score_grads.7 = (bf16[16,16,1792]{2,1,0:T(8,128)(2,1)}, bf16[16,16,1792]{2,1,0:T(8,128)(2,1)}, f32[2,1104,128]{2,1,0:T(8,128)}) custom-call(s32[1]{0:T(128)} %bitcast.place, bf16[2,4,1104,1024]{3,2,1,0:T(8,128)(2,1)} %get-tuple-element.66.e, bf16[2,4,1104,384]{3,2,1,0:T(8,128)(2,1)} %get-tuple-element.67.qkv, bf16[2,1104,512]{2,1,0:T(8,128)(2,1)} %get-tuple-element.72.back, ...), custom_call_target="tpu_custom_call" | custom-call | flops 10000000000 | bytes 1000000 | tf_op jit(solution)/shard_map/score_grads/pallas_call | solution.py:441
  166.4 7.6 %spread.1 = bf16[8,4,25,512]{3,2,1,0:T(8,128)(2,1)} custom-call(s32[2200]{0:T(1024)} %reshape.385.ids, f32[2,1104,128]{2,1,0:T(8,128)} %get-tuple-element.89.rows), custom_call_target="tpu_custom_call" | custom-call | flops 7000000000 | bytes 1000000 | tf_op jit(solution)/shard_map/spread/pallas_call | solution.py:502
  174.6 2.4 collective-permute-start.17
  177.0 4.4 %collective-permute-done.17 = bf16[2,80,512]{2,1,0:T(8,128)(2,1)S(1)} collective-permute-done((bf16[2,80,512]{2,1,0:T(8,128)(2,1)S(1)}, bf16[2,80,512]{2,1,0:T(8,128)(2,1)S(1)}, u32[]{:S(2)}, u32[]{:S(2)}) %collective-permute-start.17) | collective-permute-done | bytes 163872 | tf_op jit(solution)/shard_map/ppermute | solution.py:616
  181.4 2.2 collective-permute-start.18
  183.6 2.7 %collective-permute-done.8 = bf16[8,16,1792]{2,1,0:T(8,128)(2,1)S(1)} collective-permute-done((bf16[8,16,1792]{2,1,0:T(8,128)(2,1)S(1)}, bf16[8,16,1792]{2,1,0:T(8,128)(2,1)S(1)}, u32[]{:S(2)}, u32[]{:S(2)}) %collective-permute-start.8) | collective-permute-done | bytes 458784 | tf_op jit(solution)/shard_map/ppermute | solution.py:616
  187.4 3.5 %collective-permute-start.19 = (bf16[1,80,512]{2,1,0:T(8,128)(2,1)S(1)}, bf16[1,80,512]{2,1,0:T(8,128)(2,1)S(1)}, u32[]{:S(2)}, u32[]{:S(2)}) collective-permute-start(bf16[1,80,512]{2,1,0:T(8,128)(2,1)S(1)} %get-tuple-element.115), channel_id=1, source_target_pairs={{0,16},{4,20},{8,24},{12,28},{16,0},{20,4},{24,8},{28,12},{1,17},{... | collective-permute-start | bytes 245768 | tf_op jit(solution)/shard_map/ppermute | solution.py:616
  190.9 2.0 collective-permute-done.9
  192.9 2.5 collective-permute-start.10
  196.2 1.4 collective-permute-done.10
  197.6 2.5 collective-permute-start.11
  200.1 1.3 collective-permute-done.20
  202.6 2.8 %collective-permute-start.12 = (bf16[1,16,1792]{2,1,0:T(8,128)(2,1)S(1)}, bf16[1,16,1792]{2,1,0:T(8,128)(2,1)S(1)}, u32[]{:S(2)}, u32[]{:S(2)}) collective-permute-start(bf16[1,16,1792]{2,1,0:T(8,128)(2,1)S(1)} %get-tuple-element.119), channel_id=1, source_target_pairs={{0,16},{4,20},{8,24},{12,28},{16,0},{20,4},{24,8},{28,12},{1,17},{... | collective-permute-start | bytes 172040 | tf_op jit(solution)/shard_map/ppermute | solution.py:616
  205.4 2.1 collective-permute-done.21
  209.2 8.6 %all-to-all-start.1 = ((bf16[32,25,512]{2,1,0:T(8,128)(2,1)}), bf16[32,25,512]{2,1,0:T(8,128)(2,1)S(1)}, u32[]{:S(2)}, u32[]{:S(2)}) async-start(bf16[32,25,512]{2,1,0:T(8,128)(2,1)} %bitcast.41), calls=%async_computation.1 | async-start | bytes 2097152 | tf_op jit(solution)/shard_map/all_to_all | solution.py:624
  217.8 1.5 collective-permute-start.14
  221.0 11.1 %collective-permute-start.23 = (bf16[16,80,512]{2,1,0:T(8,128)(2,1)}, bf16[16,80,512]{2,1,0:T(8,128)(2,1)S(1)}, u32[]{:S(2)}, u32[]{:S(2)}) collective-permute-start(bf16[16,80,512]{2,1,0:T(8,128)(2,1)} %constant_dynamic-update-slice_fusion.9.near), channel_id=1, source_target_pairs={{0,1},{1,0},{2,3},{3,2},{4,5},{5,4},{6,7},{7,6},{8,9},{9,8},{10,11... | collective-permute-start | bytes 3932168 | tf_op jit(solution)/shard_map/ppermute | solution.py:616
  233.0 1.8 collective-permute-start.15
  236.9 8.9 %collective-permute-done.15 = bf16[8,16,1792]{2,1,0:T(8,128)(2,1)S(1)} collective-permute-done((bf16[8,16,1792]{2,1,0:T(8,128)(2,1)S(1)}, bf16[8,16,1792]{2,1,0:T(8,128)(2,1)S(1)}, u32[]{:S(2)}, u32[]{:S(2)}) %collective-permute-start.15) | collective-permute-done | bytes 458784 | tf_op jit(solution)/shard_map/ppermute | solution.py:616
  246.5 2.0 collective-permute-start.16
  249.0 1.1 copy-done.13
  250.1 5.4 %finish.1 = (f32[512,512]{1,0:T(8,128)}, f32[512,1024]{1,0:T(8,128)}, f32[1024,512]{1,0:T(8,128)}) custom-call(s32[1]{0:T(128)} %bitcast.place, bf16[16,80,512]{2,1,0:T(8,128)(2,1)} %constant_dynamic-update-slice_fusion.9.near, bf16[16,80,512]{2,1,0:T(8,128)(2,1)} %copy-done.13), custom_call_target="tpu_custom_call" | custom-call | flops 5000000000 | bytes 1000000 | tf_op jit(solution)/shard_map/finish/pallas_call | solution.py:541
  255.5 5.0 %finish_tail.1 = (f32[512,512]{1,0:T(8,128)}, f32[512,512]{1,0:T(8,128)}, f32[512,512]{1,0:T(8,128)}, f32[100,512]{1,0:T(8,128)}, f32[1,512]{1,0:T(1,128)}, /*in...) custom-call(s32[1]{0:T(128)} %bitcast.place, ...), custom_call_target="tpu_custom_call" | custom-call | flops 5000000000 | bytes 1000000 | tf_op jit(solution)/shard_map/finish_tail/pallas_call | solution.py:594
  260.5 1.0 fusion.15
  (131 shorter events, 23.7 us)
Async XLA Ops:
  0.7 7.6 %copy-start.8 = (s32[2,1100]{1,0:T(2,128)S(1)}, s32[2,1100]{1,0:T(2,128)}, u32[]{:S(2)}) copy-start(s32[2,1100]{1,0:T(2,128)} %param.42) | copy-start | bytes 26404
  0.7 7.7 %copy-start.10 = (s32[2,1000]{1,0:T(2,128)S(1)}, s32[2,1000]{1,0:T(2,128)}, u32[]{:S(2)}) copy-start(s32[2,1000]{1,0:T(2,128)} %param.43) | copy-start | bytes 24004
  3.0 7.6 %copy-start.7 = (bf16[100,512]{1,0:T(8,128)(2,1)S(1)}, bf16[100,512]{1,0:T(8,128)(2,1)}, u32[]{:S(2)}) copy-start(bf16[100,512]{1,0:T(8,128)(2,1)} %param.24) | copy-start | bytes 307204
  4.0 8.9 %all-to-all-start = ((f16[4,26,512]{2,1,0:T(8,128)(2,1)}), f16[4,26,512]{2,1,0:T(8,128)(2,1)S(1)}, u32[]{:S(2)}, u32[]{:S(2)}) async-start(f16[4,26,512]{2,1,0:T(8,128)(2,1)} %pad_maximum_fusion.7), calls=%async_computation | async-start | bytes 262144 | tf_op jit(solution)/shard_map/all_to_all | solution.py:624
  8.5 3.1 %copy-start.9 = (bf16[10,512]{1,0:T(8,128)(2,1)S(1)}, bf16[10,512]{1,0:T(8,128)(2,1)}, u32[]{:S(2)}) copy-start(bf16[10,512]{1,0:T(8,128)(2,1)} %param.26) | copy-start | bytes 30724
  9.2 3.1 %copy-start.4 = (bf16[512,512]{1,0:T(8,128)(2,1)S(1)}, bf16[512,512]{1,0:T(8,128)(2,1)}, u32[]{:S(2)}) copy-start(bf16[512,512]{1,0:T(8,128)(2,1)} %param.30) | copy-start | bytes 1572868
  10.6 1.9 copy-start.5
  10.8 1.9 copy-start.6
  13.0 5.2 %collective-permute-start = (f16[1,104,512]{2,1,0:T(8,128)(2,1)S(1)}, f16[1,104,512]{2,1,0:T(8,128)(2,1)S(1)}, u32[]{:S(2)}, u32[]{:S(2)}) collective-permute-start(f16[1,104,512]{2,1,0:T(8,128)(2,1)S(1)} %reshape.361), channel_id=1, source_target_pairs={{0,8},{4,12},{8,0},{12,4},{16,24},{20,28},{24,16},{28,20},{1,9},{5... | collective-permute-start | bytes 319496 | tf_op jit(solution)/shard_map/ppermute | solution.py:616
  14.9 5.1 %collective-permute-start.1 = (f16[1,104,512]{2,1,0:T(8,128)(2,1)S(1)}, f16[1,104,512]{2,1,0:T(8,128)(2,1)S(1)}, u32[]{:S(2)}, u32[]{:S(2)}) collective-permute-start(f16[1,104,512]{2,1,0:T(8,128)(2,1)S(1)} %reshape.361), channel_id=1, source_target_pairs={{0,16},{4,20},{8,24},{12,28},{16,0},{20,4},{24,8},{28,12},{1,17},{... | collective-permute-start | bytes 319496 | tf_op jit(solution)/shard_map/ppermute | solution.py:616
  17.2 7.6 %collective-permute-start.2 = (f16[1,104,512]{2,1,0:T(8,128)(2,1)S(1)}, f16[1,104,512]{2,1,0:T(8,128)(2,1)S(1)}, u32[]{:S(2)}, u32[]{:S(2)}) collective-permute-start(f16[1,104,512]{2,1,0:T(8,128)(2,1)S(1)} %reshape.361), channel_id=1, source_target_pairs={{0,24},{4,28},{8,16},{12,20},{16,8},{20,12},{24,0},{28,4},{1,25},{... | collective-permute-start | bytes 319496 | tf_op jit(solution)/shard_map/ppermute | solution.py:616
  25.5 9.2 %collective-permute-start.3 = (f16[4,104,512]{2,1,0:T(8,128)(2,1)}, f16[4,104,512]{2,1,0:T(8,128)(2,1)}, u32[]{:S(2)}, u32[]{:S(2)}) collective-permute-start(f16[4,104,512]{2,1,0:T(8,128)(2,1)} %constant_dynamic-update-slice_fusion), channel_id=1, source_target_pairs={{0,4},{4,0},{8,12},{12,8},{16,20},{20,16},{24,28},{28,24},{1,5},{5... | collective-permute-start | bytes 1277960 | tf_op jit(solution)/shard_map/ppermute | solution.py:616
  26.9 82.9 %copy-start = (bf16[512,4,3,128]{0,3,2,1:T(8,128)(2,1)}, bf16[512,4,3,128]{0,3,2,1:T(8,128)(2,1)S(1)}, u32[]{:S(2)}) copy-start(bf16[512,4,3,128]{0,3,2,1:T(8,128)(2,1)S(1)} %pad_maximum_fusion) | copy-start | bytes 4718596
  26.9 1.8 copy-start.11
  26.9 1.8 copy-start.12
  106.4 17.1 %collective-permute-start.4 = (bf16[16,80,512]{2,1,0:T(8,128)(2,1)}, bf16[16,80,512]{2,1,0:T(8,128)(2,1)S(1)}, u32[]{:S(2)}, u32[]{:S(2)}) collective-permute-start(bf16[16,80,512]{2,1,0:T(8,128)(2,1)} %get-tuple-element.69), channel_id=1, source_target_pairs={{0,1},{1,0},{2,3},{3,2},{4,5},{5,4},{6,7},{7,6},{8,9},{9,8},{10,11... | collective-permute-start | bytes 3932168 | tf_op jit(solution)/shard_map/ppermute | solution.py:616
  111.3 12.2 %copy-start.2 = (bf16[16,80,512]{2,1,0:T(8,128)(2,1)S(1)}, bf16[16,80,512]{2,1,0:T(8,128)(2,1)}, u32[]{:S(2)}) copy-start(bf16[16,80,512]{2,1,0:T(8,128)(2,1)} %get-tuple-element.68) | copy-start | bytes 3932164
  124.8 25.3 %collective-permute-start.5 = (bf16[8,80,512]{2,1,0:T(8,128)(2,1)}, bf16[8,80,512]{2,1,0:T(8,128)(2,1)S(1)}, u32[]{:S(2)}, u32[]{:S(2)}) collective-permute-start(bf16[8,80,512]{2,1,0:T(8,128)(2,1)} %get-tuple-element.124), channel_id=1, source_target_pairs={{0,2},{1,3},{2,0},{3,1},{4,6},{5,7},{6,4},{7,5},{8,10},{9,11},{10,... | collective-permute-start | bytes 1966088 | tf_op jit(solution)/shard_map/ppermute | solution.py:616
  150.3 15.9 %collective-permute-start.7 = (bf16[4,80,512]{2,1,0:T(8,128)(2,1)S(1)}, bf16[4,80,512]{2,1,0:T(8,128)(2,1)S(1)}, u32[]{:S(2)}, u32[]{:S(2)}) collective-permute-start(bf16[4,80,512]{2,1,0:T(8,128)(2,1)S(1)} %get-tuple-element.127), channel_id=1, source_target_pairs={{0,4},{4,0},{8,12},{12,8},{16,20},{20,16},{24,28},{28,24},{1,5},{5... | collective-permute-start | bytes 983048 | tf_op jit(solution)/shard_map/ppermute | solution.py:616
  164.9 9.0 %collective-permute-start.6 = (bf16[16,16,1792]{2,1,0:T(8,128)(2,1)}, bf16[16,16,1792]{2,1,0:T(8,128)(2,1)S(1)}, u32[]{:S(2)}, u32[]{:S(2)}) collective-permute-start(bf16[16,16,1792]{2,1,0:T(8,128)(2,1)} %get-tuple-element.87), channel_id=1, source_target_pairs={{0,1},{1,0},{2,3},{3,2},{4,5},{5,4},{6,7},{7,6},{8,9},{9,8},{10,11... | collective-permute-start | bytes 2752520 | tf_op jit(solution)/shard_map/ppermute | solution.py:616
  166.4 7.6 %copy-start.3 = (bf16[16,16,1792]{2,1,0:T(8,128)(2,1)S(1)}, bf16[16,16,1792]{2,1,0:T(8,128)(2,1)}, u32[]{:S(2)}) copy-start(bf16[16,16,1792]{2,1,0:T(8,128)(2,1)} %get-tuple-element.86) | copy-start | bytes 2752516
  174.1 12.2 %collective-permute-start.8 = (bf16[8,16,1792]{2,1,0:T(8,128)(2,1)S(1)}, bf16[8,16,1792]{2,1,0:T(8,128)(2,1)S(1)}, u32[]{:S(2)}, u32[]{:S(2)}) collective-permute-start(bf16[8,16,1792]{2,1,0:T(8,128)(2,1)S(1)} %get-tuple-element.91), channel_id=1, source_target_pairs={{0,2},{1,3},{2,0},{3,1},{4,6},{5,7},{6,4},{7,5},{8,10},{9,11},{10,... | collective-permute-start | bytes 1376264 | tf_op jit(solution)/shard_map/ppermute | solution.py:616
  174.6 6.8 %collective-permute-start.17 = (bf16[2,80,512]{2,1,0:T(8,128)(2,1)S(1)}, bf16[2,80,512]{2,1,0:T(8,128)(2,1)S(1)}, u32[]{:S(2)}, u32[]{:S(2)}) collective-permute-start(bf16[2,80,512]{2,1,0:T(8,128)(2,1)S(1)} %get-tuple-element.133), channel_id=1, source_target_pairs={{0,8},{4,12},{8,0},{12,4},{16,24},{20,28},{24,16},{28,20},{1,9},{5... | collective-permute-start | bytes 491528 | tf_op jit(solution)/shard_map/ppermute | solution.py:616
  181.4 5.3 %collective-permute-start.18 = (bf16[1,80,512]{2,1,0:T(8,128)(2,1)S(1)}, bf16[1,80,512]{2,1,0:T(8,128)(2,1)S(1)}, u32[]{:S(2)}, u32[]{:S(2)}) collective-permute-start(bf16[1,80,512]{2,1,0:T(8,128)(2,1)S(1)} %fusion.6), channel_id=1, source_target_pairs={{0,16},{4,20},{8,24},{12,28},{16,0},{20,4},{24,8},{28,12},{1,17},{... | collective-permute-start | bytes 245768 | tf_op jit(solution)/shard_map/ppermute | solution.py:616
  186.4 6.4 %collective-permute-start.9 = (bf16[4,16,1792]{2,1,0:T(8,128)(2,1)S(1)}, bf16[4,16,1792]{2,1,0:T(8,128)(2,1)S(1)}, u32[]{:S(2)}, u32[]{:S(2)}) collective-permute-start(bf16[4,16,1792]{2,1,0:T(8,128)(2,1)S(1)} %get-tuple-element.130), channel_id=1, source_target_pairs={{0,4},{4,0},{8,12},{12,8},{16,20},{20,16},{24,28},{28,24},{1,5},{5... | collective-permute-start | bytes 688136 | tf_op jit(solution)/shard_map/ppermute | solution.py:616
  187.4 8.1 %collective-permute-start.19 = (bf16[1,80,512]{2,1,0:T(8,128)(2,1)S(1)}, bf16[1,80,512]{2,1,0:T(8,128)(2,1)S(1)}, u32[]{:S(2)}, u32[]{:S(2)}) collective-permute-start(bf16[1,80,512]{2,1,0:T(8,128)(2,1)S(1)} %get-tuple-element.115), channel_id=1, source_target_pairs={{0,16},{4,20},{8,24},{12,28},{16,0},{20,4},{24,8},{28,12},{1,17},{... | collective-permute-start | bytes 245768 | tf_op jit(solution)/shard_map/ppermute | solution.py:616
  192.9 4.7 %collective-permute-start.10 = (bf16[2,16,1792]{2,1,0:T(8,128)(2,1)S(1)}, bf16[2,16,1792]{2,1,0:T(8,128)(2,1)S(1)}, u32[]{:S(2)}, u32[]{:S(2)}) collective-permute-start(bf16[2,16,1792]{2,1,0:T(8,128)(2,1)S(1)} %get-tuple-element.136), channel_id=1, source_target_pairs={{0,8},{4,12},{8,0},{12,4},{16,24},{20,28},{24,16},{28,20},{1,9},{5... | collective-permute-start | bytes 344072 | tf_op jit(solution)/shard_map/ppermute | solution.py:616
  195.4 6.0 %collective-permute-start.20 = (bf16[2,80,512]{2,1,0:T(8,128)(2,1)S(1)}, bf16[2,80,512]{2,1,0:T(8,128)(2,1)S(1)}, u32[]{:S(2)}, u32[]{:S(2)}) collective-permute-start(bf16[2,80,512]{2,1,0:T(8,128)(2,1)S(1)} %pad_maximum_fusion.6), channel_id=1, source_target_pairs={{0,8},{4,12},{8,0},{12,4},{16,24},{20,28},{24,16},{28,20},{1,9},{5... | collective-permute-start | bytes 491528 | tf_op jit(solution)/shard_map/ppermute | solution.py:616
  197.6 4.3 %collective-permute-start.11 = (bf16[1,16,1792]{2,1,0:T(8,128)(2,1)S(1)}, bf16[1,16,1792]{2,1,0:T(8,128)(2,1)S(1)}, u32[]{:S(2)}, u32[]{:S(2)}) collective-permute-start(bf16[1,16,1792]{2,1,0:T(8,128)(2,1)S(1)} %fusion.12), channel_id=1, source_target_pairs={{0,16},{4,20},{8,24},{12,28},{16,0},{20,4},{24,8},{28,12},{1,17},{... | collective-permute-start | bytes 172040 | tf_op jit(solution)/shard_map/ppermute | solution.py:616
  201.5 6.0 %collective-permute-start.21 = (bf16[4,80,512]{2,1,0:T(8,128)(2,1)S(1)}, bf16[4,80,512]{2,1,0:T(8,128)(2,1)S(1)}, u32[]{:S(2)}, u32[]{:S(2)}) collective-permute-start(bf16[4,80,512]{2,1,0:T(8,128)(2,1)S(1)} %pad_maximum_fusion.4), channel_id=1, source_target_pairs={{0,4},{4,0},{8,12},{12,8},{16,20},{20,16},{24,28},{28,24},{1,5},{5... | collective-permute-start | bytes 983048 | tf_op jit(solution)/shard_map/ppermute | solution.py:616
  202.6 5.3 %collective-permute-start.12 = (bf16[1,16,1792]{2,1,0:T(8,128)(2,1)S(1)}, bf16[1,16,1792]{2,1,0:T(8,128)(2,1)S(1)}, u32[]{:S(2)}, u32[]{:S(2)}) collective-permute-start(bf16[1,16,1792]{2,1,0:T(8,128)(2,1)S(1)} %get-tuple-element.119), channel_id=1, source_target_pairs={{0,16},{4,20},{8,24},{12,28},{16,0},{20,4},{24,8},{28,12},{1,17},{... | collective-permute-start | bytes 172040 | tf_op jit(solution)/shard_map/ppermute | solution.py:616
  207.5 12.5 %collective-permute-start.22 = (bf16[8,80,512]{2,1,0:T(8,128)(2,1)S(1)}, bf16[8,80,512]{2,1,0:T(8,128)(2,1)S(1)}, u32[]{:S(2)}, u32[]{:S(2)}) collective-permute-start(bf16[8,80,512]{2,1,0:T(8,128)(2,1)S(1)} %pad_maximum_fusion.2), channel_id=1, source_target_pairs={{0,2},{1,3},{2,0},{3,1},{4,6},{5,7},{6,4},{7,5},{8,10},{9,11},{10,... | collective-permute-start | bytes 1966088 | tf_op jit(solution)/shard_map/ppermute | solution.py:616
  207.9 9.9 %collective-permute-start.13 = (bf16[2,16,1792]{2,1,0:T(8,128)(2,1)S(1)}, bf16[2,16,1792]{2,1,0:T(8,128)(2,1)S(1)}, u32[]{:S(2)}, u32[]{:S(2)}) collective-permute-start(bf16[2,16,1792]{2,1,0:T(8,128)(2,1)S(1)} %pad_maximum_fusion.8), channel_id=1, source_target_pairs={{0,8},{4,12},{8,0},{12,4},{16,24},{20,28},{24,16},{28,20},{1,9},{5... | collective-permute-start | bytes 344072 | tf_op jit(solution)/shard_map/ppermute | solution.py:616
  209.2 39.4 %all-to-all-start.1 = ((bf16[32,25,512]{2,1,0:T(8,128)(2,1)}), bf16[32,25,512]{2,1,0:T(8,128)(2,1)S(1)}, u32[]{:S(2)}, u32[]{:S(2)}) async-start(bf16[32,25,512]{2,1,0:T(8,128)(2,1)} %bitcast.41), calls=%async_computation.1 | async-start | bytes 2097152 | tf_op jit(solution)/shard_map/all_to_all | solution.py:624
  217.8 15.2 %collective-permute-start.14 = (bf16[4,16,1792]{2,1,0:T(8,128)(2,1)S(1)}, bf16[4,16,1792]{2,1,0:T(8,128)(2,1)S(1)}, u32[]{:S(2)}, u32[]{:S(2)}) collective-permute-start(bf16[4,16,1792]{2,1,0:T(8,128)(2,1)S(1)} %pad_maximum_fusion.5), channel_id=1, source_target_pairs={{0,4},{4,0},{8,12},{12,8},{16,20},{20,16},{24,28},{28,24},{1,5},{5... | collective-permute-start | bytes 688136 | tf_op jit(solution)/shard_map/ppermute | solution.py:616
  221.0 28.0 %collective-permute-start.23 = (bf16[16,80,512]{2,1,0:T(8,128)(2,1)}, bf16[16,80,512]{2,1,0:T(8,128)(2,1)S(1)}, u32[]{:S(2)}, u32[]{:S(2)}) collective-permute-start(bf16[16,80,512]{2,1,0:T(8,128)(2,1)} %constant_dynamic-update-slice_fusion.9.near), channel_id=1, source_target_pairs={{0,1},{1,0},{2,3},{3,2},{4,5},{5,4},{6,7},{7,6},{8,9},{9,8},{10,11... | collective-permute-start | bytes 3932168 | tf_op jit(solution)/shard_map/ppermute | solution.py:616
  233.0 12.7 %collective-permute-start.15 = (bf16[8,16,1792]{2,1,0:T(8,128)(2,1)S(1)}, bf16[8,16,1792]{2,1,0:T(8,128)(2,1)S(1)}, u32[]{:S(2)}, u32[]{:S(2)}) collective-permute-start(bf16[8,16,1792]{2,1,0:T(8,128)(2,1)S(1)} %pad_maximum_fusion.3), channel_id=1, source_target_pairs={{0,2},{1,3},{2,0},{3,1},{4,6},{5,7},{6,4},{7,5},{8,10},{9,11},{10,... | collective-permute-start | bytes 1376264 | tf_op jit(solution)/shard_map/ppermute | solution.py:616
  246.5 8.9 %collective-permute-start.16 = (bf16[16,16,1792]{2,1,0:T(8,128)(2,1)}, bf16[16,16,1792]{2,1,0:T(8,128)(2,1)}, u32[]{:S(2)}, u32[]{:S(2)}) collective-permute-start(bf16[16,16,1792]{2,1,0:T(8,128)(2,1)} %constant_dynamic-update-slice_fusion.4.near), channel_id=1, source_target_pairs={{0,1},{1,0},{2,3},{3,2},{4,5},{5,4},{6,7},{7,6},{8,9},{9,8},{10,11... | collective-permute-start | bytes 2752520 | tf_op jit(solution)/shard_map/ppermute | solution.py:616
  249.0 1.1 copy-start.13
  255.5 6.1 %copy-start.1 = (f32[2048,25]{0,1:T(8,128)S(1)}, f32[2048,25]{0,1:T(8,128)}, u32[]{:S(2)}) copy-start(f32[2048,25]{0,1:T(8,128)} %param.23) | copy-start | bytes 614404

commit v3 on v2

v3 whole, which is shorter than its diff:
```python
import functools
import math

import jax
import jax.numpy as jnp
from jax import lax
from jax.experimental import pallas as pl
from jax.experimental.pallas import tpu as pltpu
from jax.sharding import PartitionSpec as P

HEADS = 4
LANES = 128
epsilon = 1e-05
CHUNKS = 32
SMALLS = 120
SPAN = 64.0
VMEM_LIMIT = 60 * 1024 * 1024
f32 = jnp.float32
bf16 = jnp.bfloat16


def dot(left, right):
    return jnp.dot(left, right, preferred_element_type=f32)


def dot_nt(left, right):
    return lax.dot_general(left, right, (((1,), (1,)), ((), ())), preferred_element_type=f32)


def dot_tn(left, right):
    return lax.dot_general(left, right, (((0,), (0,)), ((), ())), preferred_element_type=f32)


def round_up(value, unit):
    return -(-value // unit) * unit


def row_chunks(span):
    for parts in (3, 2, 1):
        if span % (16 * parts) == 0:
            return parts
    return 1


def cost(gigaflops, megabytes):
    return pl.CostEstimate(flops=int(gigaflops * 1e9), bytes_accessed=int(megabytes * 1e6), transcendentals=0)


def params(*names, room=VMEM_LIMIT):
    room = min(room, VMEM_LIMIT)
    return pltpu.CompilerParams(vmem_limit_bytes=room, dimension_semantics=("arbitrary",) * len(names))


def fetch_kernel(span, feats, classes, ids, near, far, labels, feats_o, stats_o, table, rows_f, notes, origins):
    count, deep, own = near.shape
    each = deep // feats
    blocks, pad, _ = feats_o.shape
    unit = next(u for u in (50, 20, 10, 5, 2, 1) if span % u == 0)
    total = 2 * count
    lane = lax.broadcasted_iota(jnp.int32, (total, LANES), 1)
    mean_row, factor_row, origin_rows = 0.0, 0.0, 0.0
    for f in range(feats):
        for half, ref in enumerate((near, far)):
            def collect(g, _):
                notes[pl.ds(half * count + g, 1), :] = ref[g, (f + 1) * each - 1:(f + 1) * each, :2 * LANES]
                return 0

            lax.fori_loop(0, count, collect, 0)
        start, other = notes[:, :LANES], notes[:, LANES:]
        back = lambda v, by: pltpu.roll(v, LANES - by, 1)
        place = lambda v: pltpu.roll(jnp.where(lane < each - 1, v, 0.0), f * each, 1) if f else jnp.where(lane < each - 1, v, 0.0)
        first = back(start, 32) + back(start, 64) * (1.0 / 1024.0) + back(start, 96) * (1.0 / 1048576.0)
        square = other * 16.0 + back(other, 32) * (1.0 / 64.0) + back(other, 64) * (1.0 / 65536.0)
        middle_of = jnp.sum(start + first, 0, keepdims=True) * (1.0 / total)
        apart = start - middle_of
        spread_of = jnp.sum(square + apart * (2.0 * first + apart), 0, keepdims=True) * (1.0 / total)
        spread_of = jnp.where(lane[:1] < each - 1, spread_of, 1.0)
        full = lambda v: jnp.broadcast_to(v, (total, LANES))
        mean_row = mean_row + place(full(middle_of))
        factor_row = factor_row + place(full(lax.rsqrt(spread_of + epsilon)))
        origin_rows = origin_rows + place(start)
    origins[...] = origin_rows
    stats_o[0:1, :] = mean_row[0:1]
    stats_o[1:2, :] = factor_row[0:1]

    for half, ref in enumerate((near, far)):
        def unfold(g, _):
            piece = jnp.concatenate([ref[g], jnp.zeros((LANES - deep, own), f32)], 0).T
            at = half * count + g
            table[pl.ds(pl.multiple_of(at * own, own), own), :] = piece * (1.0 / SPAN) + origins[pl.ds(at, 1), :]
            return 0

        lax.fori_loop(0, count, unfold, 0)
    rows_f[pad - 16:, :] = jnp.zeros((16, LANES), f32)
    kind = lax.broadcasted_iota(jnp.int32, (16, pad), 0)
    pick = (lax.broadcasted_iota(jnp.int32, (16, LANES), 0) + deep == lax.broadcasted_iota(jnp.int32, (16, LANES), 1))
    pick = pick.astype(f32).astype(bf16)
    lane = lax.broadcasted_iota(jnp.int32, (pad, LANES), 1)
    for block in range(blocks):
        def fetch(i, _):
            for u in range(unit):
                at = i * unit + u
                rows_f[pl.ds(at, 1), :] = table[pl.ds(ids[block * span + at], 1), :]
            return 0

        lax.fori_loop(0, span // unit, fetch, 0)
        hot = ((kind == labels[block:block + 1, :]) | (kind == classes)).astype(f32).astype(bf16)
        scaled = (rows_f[...] - mean_row[0:1]) * factor_row[0:1]
        feats_o[block] = jnp.where(lane < deep, scaled, dot_tn(hot, pick)).astype(bf16)


def fetch(ids, near, far, labels, feats, classes):
    blocks, pad = labels.shape
    whole = lambda *s: pl.BlockSpec(s, lambda *_: (0,) * len(s), pipeline_mode=pl.Buffered(1))
    full = lambda *s: pl.BlockSpec(s, lambda *_: (0,) * len(s))
    total = 2 * near.shape[0]
    return pl.pallas_call(
        functools.partial(fetch_kernel, ids.shape[0] // blocks, feats, classes),
        grid_spec=pltpu.PrefetchScalarGridSpec(
            num_scalar_prefetch=1,
            grid=(1,),
            in_specs=[whole(*near.shape), whole(*far.shape), whole(*labels.shape)],
            out_specs=[full(blocks, pad, LANES), full(8, LANES)],
            scratch_shapes=[pltpu.VMEM((total * near.shape[2], LANES), f32), pltpu.VMEM((pad, LANES), f32),
                            pltpu.VMEM((total, 2 * LANES), f32), pltpu.VMEM((total, LANES), f32)],
        ),
        out_shape=[jax.ShapeDtypeStruct((blocks, pad, LANES), bf16), jax.ShapeDtypeStruct((8, LANES), f32)],
        compiler_params=params(0, room=(12 << 20) + 16 * total * near.shape[2] * LANES),
        cost_estimate=cost(6, 1),
        name="fetch",
    )(ids, near, far, labels)


def embed(feats, w_embed, b_enc):
    both = dot(feats, w_embed[...])
    model = both.shape[1] // 2
    slots = (both[:, :model] + b_enc[...]).astype(bf16)
    return slots.astype(f32) + both[:, model:]


def norm_parts(values):
    centre = jnp.mean(values, -1, keepdims=True)
    offset = values - centre
    second = jnp.mean(offset * offset, -1, keepdims=True)
    root = lax.rsqrt(second + epsilon)
    return offset * root, root


def norm_back(grad, unit, root):
    return root * (grad - jnp.mean(grad, -1, keepdims=True) - unit * jnp.mean(grad * unit, -1, keepdims=True))


def forward_kernel(blocks, ctx_len, ctx_pad, parts,
                   place, queries, feats, cot, w_embed, b_enc, w_qkv, b_qkv, w_out, b_out, gain_one, shift_one,
                   w_in, b_in, w_back, b_back, gain_two, shift_two, w_out_t,
                   qkv_o, e_o, out_o, rows_o, back_o, shift_o, keep_o, give_o, aug_o,
                   mixed, inv, out_f, act_s, norm_s, d_hid_s, d_bra_s, d_att_s, g_out, g_in, g_back, wide, narrow):
    tick = pl.program_id(0)
    pad = qkv_o.shape[2]
    model = back_o.shape[2]
    step = pad // parts
    width = model // HEADS

    @pl.when(tick < blocks * HEADS)
    def _():
        block = tick // HEADS
        head = tick % HEADS

        @pl.when(head == 0)
        def _():
            def project(c, _):
                rows = pl.ds(pl.multiple_of(c * step, 16), step)
                low = embed(feats[block, rows, :], w_embed, b_enc).astype(bf16)
                made = (dot(low, w_qkv[...]) + b_qkv[...]).astype(bf16)
                for h in range(HEADS):
                    qkv_o[0, h, rows, :] = made[:, h * 3 * width:(h + 1) * 3 * width]
                return 0

            lax.fori_loop(0, parts, project, 0)

        factor = math.log2(math.e) / math.sqrt(width)
        keys = qkv_o[0, head, :ctx_pad, width:2 * width]
        vals = jnp.concatenate([qkv_o[0, head, :ctx_pad, 2 * width:], jnp.ones((ctx_pad, width), bf16)], 1)
        edge = ctx_len // LANES * LANES
        cols = pl.ds(pl.multiple_of(head * width, LANES), width)
        spans = [slice(c * step, (c + 1) * step) for c in range(parts)]

        def score(c):
            return dot_nt(qkv_o[0, head, spans[c], :width], keys)

        def weigh(c, scores):
            front = scores[:, :edge]
            most = jnp.max(front, 1, keepdims=True)
            if edge < ctx_pad:
                lane = lax.broadcasted_iota(jnp.int32, (step, ctx_pad - edge), 1)
                rear = jnp.where(lane < ctx_len - edge, scores[:, edge:], -1e30)
                most = jnp.maximum(most, jnp.max(rear, 1, keepdims=True))
                e_o[0, 0, spans[c], edge:] = jnp.exp2((rear - most) * factor).astype(bf16)
            e_o[0, 0, spans[c], :edge] = jnp.exp2((front - most) * factor).astype(bf16)

        def mix(c):
            summed = dot(e_o[0, 0, spans[c], :], vals)
            inverse = 1.0 / summed[:, width:]
            lane = lax.broadcasted_iota(jnp.int32, (step, LANES), 1)
            inv[block, spans[c], :] = jnp.where(lane == head, inverse[:, :LANES], inv[block, spans[c], :])
            mixed[block, spans[c], cols] = (summed[:, :width] * inverse).astype(bf16)

        ready = score(0)
        for c in range(parts):
            coming = score(c + 1) if c + 1 < parts else None
            weigh(c, ready)
            mix(c)
            ready = coming

    @pl.when(tick >= blocks * HEADS)
    def _():
        part = tick - blocks * HEADS

        @pl.when(part == 0)
        def _():
            for ref in (g_out, g_in, g_back, wide, narrow):
                ref[...] = jnp.zeros_like(ref)

        tiles = model // LANES
        rows = pl.ds(pl.multiple_of(part * step, 16), step)
        total = lambda v: jnp.sum(v, 0, keepdims=True)
        wide_t, narrow_t = [], [[] for _ in range(6)]

        def flow(block):
            here = slice(block * step, (block + 1) * step)
            mixed_low = mixed[block, rows, :]
            reached = embed(feats[block, rows, :], w_embed, b_enc) + dot(mixed_low, w_out[...])
            yield
            unit_one, root_one = norm_parts(reached + b_out[...])
            normed = unit_one * gain_one[...] + shift_one[...]
            norm_s[here, :] = normed.astype(bf16)
            yield
            hidden = dot(norm_s[here, :], w_in[...])
            yield
            hidden = hidden + b_in[...]
            slant = math.sqrt(2.0 / math.pi)
            square = hidden * hidden
            half = 0.5 * jnp.tanh(hidden * (slant + (slant * 0.044715) * square)) + 0.5
            active = hidden * half
            act_s[here, :] = active.astype(bf16)
            slope = half + active * (1.0 - half) * (2.0 * slant + (6.0 * slant * 0.044715) * square)
            yield
            branch = dot(act_s[here, :], w_back[...])
            yield
            unit_two, root_two = norm_parts(normed + (branch + b_back[...]))
            row = part * step + lax.broadcasted_iota(jnp.int32, (step, 1), 0)
            alive = row < ctx_len + queries[block]
            result = jnp.where(alive, unit_two * gain_two[...] + shift_two[...], 0.0)
            given = []
            for j in range(tiles):
                lanes = pl.ds(j * blocks + block, step, stride=tiles * blocks)
                out_f[lanes, :] = result[:, j * LANES:(j + 1) * LANES]
                given.append(cot[lanes, :])
            grad = jnp.where(alive, jnp.concatenate(given, 1), 0.0)
            second = norm_back(grad * gain_two[...], unit_two, root_two)
            d_bra_s[here, :] = second.astype(bf16)
            narrow_t[3].append(total(d_bra_s[here, :].astype(f32)))
            narrow_t[4].append(total(grad * unit_two))
            narrow_t[5].append(total(grad))
            yield
            d_act = dot_nt(d_bra_s[here, :], w_back[...])
            yield
            d_hid = (slope * d_act).astype(bf16)
            d_hid_s[here, :] = d_hid
            wide_t.append(total(d_hid.astype(f32)))
            yield
            d_norm = dot_nt(d_hid_s[here, :], w_in[...])
            yield
            grad_one = second + d_norm
            narrow_t[1].append(total(grad_one * unit_one))
            narrow_t[2].append(total(grad_one))
            first = norm_back(grad_one * gain_one[...], unit_one, root_one)
            d_att_s[here, :] = first.astype(bf16)
            narrow_t[0].append(total(d_att_s[here, :].astype(f32)))
            yield
            both = dot(d_att_s[here, :], w_out_t[...])
            yield
            rows_o[block] = both[:, model:]
            back = both[:, :model].astype(bf16).astype(f32)
            lane = lax.broadcasted_iota(jnp.int32, (step, LANES), 1)
            shifts = jnp.zeros((step, LANES), f32)
            for h in range(HEADS):
                cols = slice(h * width, (h + 1) * width)
                scaled = (back[:, cols] * inv[block, rows, h:h + 1]).astype(bf16)
                back_o[block, :, cols] = scaled
                moved = jnp.sum(scaled.astype(f32) * mixed_low[:, cols].astype(f32), 1, keepdims=True)
                shifts = jnp.where(lane == h, -moved, shifts)
            shift_o[block] = shifts
            yield

        flows = [flow(block) for block in range(blocks)]
        for item in flows:
            next(item)
        for turn in range(6):
            for item in flows:
                next(item)
                next(item, None)
            if turn == 2:
                g_back[...] += dot_tn(act_s[...], d_bra_s[...])
            if turn == 3:
                g_in[...] += dot_tn(norm_s[...], d_hid_s[...])
            if turn == 4:
                both = jnp.concatenate([jnp.concatenate([mixed[block, rows, :], feats[block, rows, :]], 1) for block in range(blocks)], 0)
                g_out[...] += dot_tn(both, d_att_s[...])
        out_o[...] = out_f[...].astype(bf16)
        wide[0:1, :] += sum(wide_t[1:], wide_t[0])
        for at in range(6):
            narrow[at:at + 1, :] += sum(narrow_t[at][1:], narrow_t[at][0])

        @pl.when(part == parts - 1)
        def _():
            def lay(start, ref, p, _):
                at = pl.multiple_of((p ^ place[0]) * 16, 16)
                other = pl.multiple_of((p ^ place[1]) * 32, 32)
                ref[p - start, 0:16, :] = g_out[pl.ds(at, 16), :].astype(bf16)
                for j in range(2):
                    ref[p - start, 16 + 16 * j:32 + 16 * j, :] = g_in[pl.ds(at, 16), j * model:(j + 1) * model].astype(bf16)
                ref[p - start, 48:80, :] = g_back[pl.ds(other, 32), :].astype(bf16)
                return 0

            for start, ref in ((0, keep_o), (CHUNKS // 2, give_o)):
                lax.fori_loop(start, start + CHUNKS // 2, functools.partial(lay, start, ref), 0)
            aug_o[...] = g_out[model:, :]
            aug_o[SMALLS:SMALLS + 6, :] = narrow[0:6, :]
            for j in range(2):
                aug_o[SMALLS + 6 + j:SMALLS + 7 + j, :] = wide[0:1, j * model:(j + 1) * model]


def forward(place, queries, feats, cot, weights, ctx_len):
    blocks, pad, _ = feats.shape
    model = weights[2].shape[0]
    inner = weights[8].shape[1]
    width = model // HEADS
    ctx_pad = round_up(ctx_len, LANES)
    parts = row_chunks(pad)
    step = pad // parts
    early = blocks * HEADS
    flat = blocks * model // LANES
    attending = lambda t: jnp.minimum(t, early - 1)
    later = lambda t: jnp.maximum(t - early, 0)
    once = lambda a: pl.BlockSpec(a.shape, lambda *_: (0,) * a.ndim, pipeline_mode=pl.Buffered(1))
    full = lambda *s: pl.BlockSpec(s, lambda *_: (0,) * len(s))
    rowed = lambda w: pl.BlockSpec((blocks, step, w), lambda t, *_: (0, later(t), 0))
    shape = jax.ShapeDtypeStruct
    return pl.pallas_call(
        functools.partial(forward_kernel, blocks, ctx_len, ctx_pad, parts),
        grid_spec=pltpu.PrefetchScalarGridSpec(
            num_scalar_prefetch=2,
            grid=(early + parts,),
            in_specs=[once(feats), pl.BlockSpec((step * flat, LANES), lambda t, *_: (later(t), 0))] + [once(a) for a in weights],
            out_specs=[
                pl.BlockSpec((1, HEADS, pad, 3 * width), lambda t, *_: (attending(t) // HEADS, 0, 0, 0)),
                pl.BlockSpec((1, 1, pad, ctx_pad), lambda t, *_: (attending(t) // HEADS, attending(t) % HEADS, 0, 0)),
                pl.BlockSpec((step * flat, LANES), lambda t, *_: (later(t), 0)),
                rowed(LANES), rowed(model), rowed(LANES),
                full(CHUNKS // 2, 80, model), full(CHUNKS // 2, 80, model), full(LANES, model)],
            scratch_shapes=[
                pltpu.VMEM((blocks, pad, model), bf16), pltpu.VMEM((blocks, pad, LANES), f32), pltpu.VMEM((step * flat, LANES), f32),
                pltpu.VMEM((blocks * step, inner), bf16), pltpu.VMEM((blocks * step, model), bf16),
                pltpu.VMEM((blocks * step, inner), bf16), pltpu.VMEM((blocks * step, model), bf16),
                pltpu.VMEM((blocks * step, model), bf16), pltpu.VMEM((model + LANES, model), f32), pltpu.VMEM((model, inner), f32),
                pltpu.VMEM((inner, model), f32), pltpu.VMEM((8, inner), f32), pltpu.VMEM((8, model), f32)],
        ),
        out_shape=[
            shape((blocks, HEADS, pad, 3 * width), bf16),
            shape((blocks, HEADS, pad, ctx_pad), bf16), shape(cot.shape, bf16), shape((blocks, pad, LANES), f32),
            shape((blocks, pad, model), bf16), shape((blocks, pad, LANES), f32), shape((CHUNKS // 2, 80, model), bf16),
            shape((CHUNKS // 2, 80, model), bf16), shape((LANES, model), f32)],
        compiler_params=params(0),
        cost_estimate=cost(60, 1),
        name="forward",
    )(place, queries, feats, cot, *weights)


def scores_kernel(start, last, ctx_pad, parts, place, e, qkv, back, shift, feats, w_rows, d_rows, *refs):
    block = pl.program_id(0)
    at = pl.program_id(1)
    count = pl.num_programs(1)
    base = start if last else 0
    if last:
        early, (first, keep_o, give_o, rows_o, ds, dox, d_all, fit) = refs[:-8], refs[-8:]
    else:
        early_o, rows_o, ds, dox, d_all, fit = refs
    pad = back.shape[1]
    step = pad // parts
    width = back.shape[2]
    root = 1.0 / math.sqrt(width)
    keys = qkv[0, 0, :ctx_pad, width:2 * width]
    vals = jnp.concatenate([qkv[0, 0, :ctx_pad, 2 * width:], jnp.ones((ctx_pad, width), bf16)], 1)
    lane = lax.broadcasted_iota(jnp.int32, (pad, width), 1)
    moved = jnp.sum(jnp.where(lane == start + at, shift[0], 0.0), 1, keepdims=True)
    top = moved.astype(bf16).astype(f32)
    dox[:, :width] = back[0]
    dox[:, width:] = jnp.where(lane == 0, top, jnp.where(lane == 1, moved - top, 0.0)).astype(bf16)
    spans = [slice(c * step, (c + 1) * step) for c in range(parts)]

    def score(c):
        return dot_nt(dox[spans[c], :], vals)

    ready = score(0)
    for c in range(parts):
        coming = score(c + 1) if c + 1 < parts else None
        ds[spans[c], :] = e[0, 0, spans[c], :] * ready.astype(bf16)
        d_all[spans[c], :width] = (dot(ds[spans[c], :], keys) * root).astype(bf16)
        ready = coming
    d_all[:ctx_pad, 2 * width:] = dot_tn(back[0], e[0, 0]).T.astype(bf16)
    d_all[:ctx_pad, width:2 * width] = (dot_tn(qkv[0, 0, :, :width], ds[...]) * root).T.astype(bf16)
    d_all[ctx_pad:, width:] = jnp.zeros((pad - ctx_pad, 2 * width), bf16)
    fitted = dot_tn(feats[0], d_all[...])
    pair = dot(d_all[...], w_rows[0])
    made = pair[:, :LANES] + pair[:, LANES:]

    @pl.when(at == 0)
    def _():
        rows_o[0] = d_rows[0] + made

    @pl.when(at > 0)
    def _():
        rows_o[0] += made

    @pl.when(block == 0)
    def _():
        fit[base + at] = fitted

    @pl.when(block > 0)
    def _():
        fit[base + at] += fitted

    @pl.when((block == pl.num_programs(0) - 1) & (at == count - 1))
    def _():
        if not last:
            early_o[...] = fit[...]
        else:
            filled = 0
            for ref in early:
                fit[filled:filled + ref.shape[0]] = ref[...]
                filled += ref.shape[0]
            for turn, ref in enumerate((keep_o, give_o)):
                def lay(p, _):
                    chunk = (turn * (CHUNKS // 2) + p) ^ place[2]
                    rows = pl.ds(pl.multiple_of(chunk // HEADS * 16, 16), 16)
                    head = chunk % HEADS
                    ref[p, :, :3 * width] = fit[head, rows, :].astype(bf16)
                    ref[p, :, 3 * width:] = first[rows, pl.ds(pl.multiple_of(head * width, LANES), width)].astype(bf16)
                    return 0

                lax.fori_loop(0, CHUNKS // 2, lay, 0)


def score_grads(place, start, count, e, qkv, back, shift, feats, w_rows, d_rows, early, first):
    blocks, pad, model = back.shape
    ctx_pad = e.shape[3]
    width = model // HEADS
    parts = row_chunks(pad)
    full = lambda *s: pl.BlockSpec(s, lambda *_: (0,) * len(s))
    rowed = pl.BlockSpec((1, pad, LANES), lambda b, h, *_: (b, 0, 0))
    shape = jax.ShapeDtypeStruct
    last = start + count == HEADS
    late = (*early, first) if last else ()
    ends = [shape((CHUNKS // 2, 16, 4 * width), bf16)] * 2 if last else [shape((count, LANES, 3 * width), f32)]
    return pl.pallas_call(
        functools.partial(scores_kernel, start, last, ctx_pad, parts),
        grid_spec=pltpu.PrefetchScalarGridSpec(
            num_scalar_prefetch=1,
            grid=(blocks, count),
            in_specs=[pl.BlockSpec((1, 1, pad, ctx_pad), lambda b, h, *_: (b, start + h, 0, 0)),
                      pl.BlockSpec((1, 1, pad, 3 * width), lambda b, h, *_: (b, start + h, 0, 0)),
                      pl.BlockSpec((1, pad, width), lambda b, h, *_: (b, 0, start + h)),
                      rowed, rowed,
                      pl.BlockSpec((1, 3 * width, 2 * LANES), lambda b, h, *_: (start + h, 0, 0)),
                      rowed] + [full(*a.shape) for a in late],
            out_specs=[full(*end.shape) for end in ends] + [rowed],
            scratch_shapes=[pltpu.VMEM((pad, ctx_pad), bf16), pltpu.VMEM((pad, 2 * width), bf16), pltpu.VMEM((pad, 3 * width), bf16),
                            pltpu.VMEM((HEADS if last else count, LANES, 3 * width), f32)],
        ),
        out_shape=ends + [shape((blocks, pad, LANES), f32)],
        compiler_params=params(0, 0, room=36 << 20),
        cost_estimate=cost(8 * count, 1),
        name="score_grads",
    )(place, e, qkv, back, shift, feats, w_rows, d_rows, *late)


def spread_kernel(span, own, ids, rows, near_o, far_o, *tables):
    blocks = rows.shape[0]
    count, feats, col_width, _ = near_o.shape
    for table in tables:
        table[...] = jnp.zeros_like(table)
    each = len(tables) // blocks if len(tables) > 1 else 1
    run = span // each
    unit = next(u for u in (10, 5, 2, 1) if run % u == 0)

    def add(i, _):
        for u in range(unit):
            for t in range(blocks * each):
                block, at = t // each, t % each * run + i * unit + u
                table = tables[t % len(tables)]
                spot = pl.ds(ids[block * span + at], 1)
                table[spot, :] += rows[block, pl.ds(at, 1), :]
        return 0

    lax.fori_loop(0, run // unit, add, 0)

    def fold(start, out_o, g, _):
        spot = pl.ds(pl.multiple_of((start + g) * own, own), own)
        total = tables[0][spot, :]
        for table in tables[1:]:
            total = total + table[spot, :]
        total = total.T
        for f in range(feats):
            at = f * (col_width + 1)
            out_o[g, f] = total[at:at + col_width].astype(bf16)
        return 0

    for start, out_o in ((0, near_o), (count, far_o)):
        lax.fori_loop(0, count, functools.partial(fold, start, out_o), 0)


def spread(ids, rows, count, feats, col_width, own):
    span = ids.shape[0] // rows.shape[0]
    tables = 4 if count <= 8 and span % 2 == 0 else 1
    return pl.pallas_call(
        functools.partial(spread_kernel, span, own),
        grid_spec=pltpu.PrefetchScalarGridSpec(
            num_scalar_prefetch=1,
            grid=(1,),
            in_specs=[pl.BlockSpec(rows.shape, lambda *_: (0, 0, 0))],
            out_specs=[pl.BlockSpec((count // 2, feats, col_width, own), lambda *_: (0, 0, 0, 0))] * 2,
            scratch_shapes=[pltpu.VMEM((count * own, LANES), f32)] * tables,
        ),
        out_shape=[jax.ShapeDtypeStruct((count // 2, feats, col_width, own), bf16)] * 2,
        compiler_params=params(0, room=(12 << 20) + 16 * count * own * LANES),
        cost_estimate=cost(7, 1),
        name="spread",
    )(ids, rows)


def chosen(p, near, far):
    half = CHUNKS // 2
    at = p % half
    return lambda *spot: jnp.where(p < half, near[(at, *spot)].astype(f32), far[(at, *spot)].astype(f32))


def finish_kernel(place, near, far, near_q, far_q, out_o, in_o, back_o):
    step = pl.program_id(0)
    model = out_o.shape[1]
    each = out_o.shape[0] // 16
    for u in range(each):
        take = chosen((step * each + u) ^ place[0], near, far)
        rows = slice(u * 16, (u + 1) * 16)
        out_o[rows, :] = take(slice(0, 16))
        for j in range(2):
            in_o[rows, j * model:(j + 1) * model] = take(slice(16 + 16 * j, 32 + 16 * j))
        take = chosen((step * each + u) ^ place[1], near_q, far_q)
        back_o[u * 32:(u + 1) * 32, :] = take(slice(None))


def finish(place, *ends):
    model = ends[0].shape[2]
    steps = 4
    shapes = [(model, model), (model, 2 * model), (2 * model, model)]
    return pl.pallas_call(
        finish_kernel,
        grid_spec=pltpu.PrefetchScalarGridSpec(
            num_scalar_prefetch=1,
            grid=(steps,),
            in_specs=[pl.BlockSpec(a.shape, lambda *_: (0, 0, 0)) for a in ends],
            out_specs=[pl.BlockSpec((s[0] // steps, s[1]), lambda i, *_: (i, 0)) for s in shapes],
        ),
        out_shape=[jax.ShapeDtypeStruct(s, f32) for s in shapes],
        compiler_params=params(0, room=16 << 20),
        cost_estimate=cost(5, 1),
        name="finish",
    )(place, *ends)


def finish_tail_kernel(col_width, classes, place, near, far, w_heads, w_all, q_o, k_o, v_o, enc_o, bias_o, mark_o, b_query_o, b_value_o,
                       wide_o, *refs):
    lines, (fit, aug) = refs[:-2], refs[-2:]
    model = q_o.shape[1]
    width = model // HEADS
    for c in range(CHUNKS):
        rows = slice(c // HEADS * 16, c // HEADS * 16 + 16)
        head = c % HEADS
        take = chosen(c ^ place[2], near, far)
        fit[head, rows, :] = take(slice(None), slice(0, 3 * width)).astype(bf16)
        aug[rows, head * width:(head + 1) * width] = take(slice(None), slice(3 * width, None))
    feats = enc_o.shape[0] // col_width
    ones = feats * (col_width + 1) + classes
    for row in range(6):
        lines[row][...] = aug[SMALLS + row:SMALLS + row + 1, :]
    for j in range(2):
        wide_o[:, j * model:(j + 1) * model] = aug[SMALLS + 6 + j:SMALLS + 7 + j, :]
    kind = lax.broadcasted_iota(jnp.int32, (LANES, 3 * width), 0)
    total = aug[...]
    for head in range(HEADS):
        cols = slice(head * width, (head + 1) * width)
        part = fit[head]
        total = total + dot(part, w_heads[head])
        line = part[ones:ones + 1, :].astype(f32)
        b_query_o[:, cols] = line[:, :width]
        b_value_o[:, cols] = line[:, 2 * width:]
        spread_line = jnp.where((kind > ones) & (kind < ones + 3), line, part.astype(f32)).astype(bf16)
        made = dot_tn(w_all[...], spread_line)
        for j, ref in enumerate((q_o, k_o, v_o)):
            ref[:, cols] = made[:, j * width:(j + 1) * width]
    aug[...] = total
    for f in range(feats):
        enc_o[f * col_width:(f + 1) * col_width, :] = aug[f * (col_width + 1):f * (col_width + 1) + col_width, :]
    mark_o[...] = aug[ones - classes:ones, :]
    bias_o[...] = aug[ones:ones + 1, :]


def finish_tail(place, near, far, w_heads, w_all, feat_total, col_width, classes):
    model = w_all.shape[1]
    width = model // HEADS
    shapes = [(model, model)] * 3 + [(feat_total, model), (1, model), (classes, model), (1, model), (1, model), (1, 2 * model)]
    shapes = shapes + [(1, model)] * 6
    full = lambda *s: pl.BlockSpec(s, lambda *_: (0,) * len(s))
    return pl.pallas_call(
        functools.partial(finish_tail_kernel, col_width, classes),
        grid_spec=pltpu.PrefetchScalarGridSpec(
            num_scalar_prefetch=1,
            grid=(1,),
            in_specs=[full(*a.shape) for a in (near, far, w_heads, w_all)],
            out_specs=[full(*s) for s in shapes],
            scratch_shapes=[pltpu.VMEM((HEADS, LANES, 3 * width), bf16), pltpu.VMEM((LANES, model), f32)],
        ),
        out_shape=[jax.ShapeDtypeStruct(s, f32) for s in shapes],
        compiler_params=params(0, room=20 << 20),
        cost_estimate=cost(5, 1),
        name="finish_tail",
    )(place, near, far, w_heads, w_all)


CALLS = ((0, 2), (2, 2))


def swap(value, axis, bit):
    size = lax.axis_size(axis)
    return lax.ppermute(value, axis, [(i, i ^ bit) for i in range(size)])


def rounded(value):
    return lax.reduce_precision(value, 8, 7)


def exchange(value, axis):
    return lax.all_to_all(value, axis, split_axis=0, concat_axis=0, tiled=True)


def added(*values):
    return sum((value.astype(f32) for value in values[1:]), values[0].astype(f32))


def reduce_chunks(keep, give, cut):
    over_core, over_x, over_y = ("feat", 1), ("feat", 2), ("rows", 1)
    came = swap(give, *over_core)
    half = keep.shape[0] // 2
    both = []
    for rows, first, then in ((slice(None, cut), over_x, over_y), (slice(cut, None), over_y, over_x)):
        mine, theirs = added(keep[:half, rows], came[:half, rows]), added(keep[half:, rows], came[half:, rows]).astype(bf16)
        both.append((mine, theirs, first, then))
    yield both[0][1]
    half = half // 2
    last = []
    for mine, theirs, first, then in both:
        came = swap(theirs, *first)
        last.append((added(mine[:half], came[:half]), added(mine[half:], came[half:]).astype(bf16), then))
    yield last[0][1]
    total = jnp.concatenate([added(mine, swap(theirs, *then)) for mine, theirs, then in last], 1).astype(bf16)
    yield total
    own = added(total[0], *[swap(total[at], "rows", 2 * at) for at in range(1, half)]).astype(bf16)
    for bit in range(3, lax.axis_size("rows").bit_length() - 1):
        own = added(own, swap(own, "rows", 1 << bit)).astype(bf16)
    yield own


def gather_chunks(own, cut):
    over_core, over_x, over_y = ("feat", 1), ("feat", 2), ("rows", 1)
    own = jnp.stack([own] + [swap(own, "rows", 2 * at) for at in range(1, 4)])
    parts = []
    for rows, first, then in ((slice(None, cut), over_x, over_y), (slice(cut, None), over_y, over_x)):
        part = own[:, rows]
        parts.append((jnp.concatenate([part, swap(part, *then)], 0), first))
    near = [jnp.concatenate([part, swap(part, *first)], 0) for part, first in parts]
    return near[0], swap(near[0], *over_core), near[1], swap(near[1], *over_core)


def tail_first(keep, give):
    half = keep.shape[0] // 2
    came = swap(give, "feat", 1)
    return added(keep[:half], came[:half]), added(keep[half:], came[half:]).astype(bf16)


def body(
    raw_rows, enc_weight, enc_bias, label_table, w_query, b_query, w_key, w_value, b_value, w_out, b_out,
    gain_one, shift_one, w_in, b_in, w_back, b_back, gain_two, shift_two, members, labels, queries, cotangent,
):
    row_count = lax.axis_size("rows")
    feat_count = lax.axis_size("feat")
    row_index = lax.axis_index("rows")
    feat_index = lax.axis_index("feat")
    local_rows, col_width = raw_rows.shape
    own_rows = local_rows // feat_count
    feat_total = col_width * feat_count
    feat_span = feat_total + feat_count
    model = enc_weight.shape[1]
    width = model // HEADS
    classes = label_table.shape[0]
    blocks, span = members.shape
    ctx_len = labels.shape[1]
    pad = round_up(span, 16)
    row_total = float(local_rows * row_count)
    core, over, up, along = feat_index % 2, feat_index // 2, row_index % 2, row_index // 2 % 4
    place = jnp.stack([core * 16 + over * 8 + up * 4 + along, core * 16 + up * 8 + over * 4 + along, core * 16 + over * 8])
    place = place.astype(jnp.int32)
    row = lambda a: a.reshape(1, -1)

    columns = raw_rows.T
    origin = rounded(jnp.mean(columns, 1, keepdims=True))
    moved = columns - origin
    sums = [origin[:, 0]]
    for value, scales in ((jnp.mean(moved, 1), (1.0, 1024.0, 1048576.0)), (jnp.mean(moved * moved, 1), (0.0625, 64.0, 65536.0))):
        for scale in scales:
            top = lax.reduce_precision(value * scale, 5, 10)
            sums.append(top)
            value = value - top / scale
    moved = moved * SPAN
    notes = jnp.pad(jnp.stack(sums), ((0, 1), (0, 32 - col_width))).reshape(1, 1, 2 * LANES)
    notes = jnp.broadcast_to(jnp.pad(notes, ((0, 0), (0, 0), (0, own_rows - 2 * LANES))), (feat_count, 1, own_rows))
    moved = moved.reshape(col_width, feat_count, own_rows).transpose(1, 0, 2)
    sent = jnp.concatenate([moved, notes], 1).astype(jnp.float16)
    owned = exchange(sent, "feat").reshape(1, feat_span, own_rows)
    near = jnp.concatenate([owned] + [swap(owned, "rows", bits) for bits in (2, 4, 6)], 0)
    for bit in range(3, row_count.bit_length() - 1):
        near = jnp.concatenate([near, swap(near, "rows", 1 << bit)], 0)
    far = swap(near, "rows", 1)
    source = members // local_rows
    source = source ^ row_index
    source = ((source >> 1) & 3) + 4 * (source >> 3) + (source & 1) * (row_count // 2)
    ids = (source * own_rows + members % own_rows).reshape(-1)

    spaced = jnp.pad(enc_weight.reshape(feat_count, col_width, model), ((0, 0), (0, 1), (0, 0))).reshape(feat_span, model)
    w_feat = jnp.pad(spaced, ((0, LANES - feat_span), (0, 0)))
    w_mark = jnp.pad(label_table, ((feat_span, LANES - feat_span - classes), (0, 0)))
    b_enc = row(enc_bias)
    w_embed = jnp.concatenate([w_feat, w_mark], 1)
    terms, left = [], enc_bias
    for _ in range(3):
        terms.append(rounded(left))
        left = left - terms[-1]
    ones = feat_span + classes
    w_all = (w_feat + w_mark).at[ones:ones + 3].set(jnp.stack(terms).astype(bf16))
    marks = jnp.pad(labels, ((0, 0), (0, pad - ctx_len)), constant_values=-1)
    cut = lambda w: w.reshape(model, HEADS, 1, width)
    w_qkv = jnp.concatenate([cut(w_query), cut(w_key), cut(w_value)], 2).reshape(model, 3 * model)
    edge = lambda b: b.reshape(1, HEADS, 1, width)
    b_qkv = jnp.concatenate([edge(b_query), edge(jnp.zeros_like(b_query)), edge(b_value)], 2).reshape(1, 3 * model)
    w_heads = w_qkv.T.reshape(HEADS, 3 * width, model)
    w_feat_t = w_feat.T
    w_rows = jnp.einsum("hkd,df->hkf", w_heads, w_feat_t, preferred_element_type=f32)
    high = rounded(w_rows)
    w_rows = jnp.concatenate([high, w_rows - high], 2).astype(bf16)
    tiles = model // LANES
    flat = cotangent.transpose(1, 0, 2).reshape(span, blocks, tiles, LANES).transpose(0, 2, 1, 3).reshape(-1, LANES)

    feats, stats = fetch(ids, near.astype(f32), far.astype(f32), marks, feat_count, classes)
    stats = lax.dynamic_slice_in_dim(stats, feat_index * (col_width + 1), col_width, 1)
    col_mean, factor = stats[0], stats[1]
    w_out_t = jnp.concatenate([w_out.T, w_feat_t], 1)
    weights = (w_embed, b_enc, w_qkv, b_qkv, w_out, row(b_out), row(gain_one), row(shift_one), w_in, row(b_in),
               w_back, row(b_back), row(gain_two), row(shift_two), w_out_t)
    qkv, expo, layer_out, d_rows, back, shift, keep, give, first = forward(place, queries, feats, flat, weights, ctx_len)
    layer_out = layer_out.reshape(span, tiles, blocks, LANES).transpose(0, 2, 1, 3).reshape(span, blocks, model).transpose(1, 0, 2)

    steps = reduce_chunks(keep, give, 48)
    early = []
    for start, count in CALLS:
        held, back = lax.optimization_barrier((next(steps), back))
        *made, d_rows = score_grads(place, start, count, expo, qkv, back, shift, feats, w_rows, d_rows, early, first)
        early.append(made[0])
    held, d_rows = lax.optimization_barrier((next(steps), d_rows))
    near, far = spread(ids, d_rows, row_count, feat_count, col_width, own_rows)
    own, (keep, give) = next(steps), tail_first(*made)
    give, near, far = lax.optimization_barrier((give, near, far))
    total = added(keep, swap(give, "feat", 2)).astype(bf16)
    d_table = added(near, swap(far, "rows", 1))
    total = added(total, swap(total, "rows", 1)).astype(bf16)
    total, d_table = lax.optimization_barrier((total, d_table))
    for bit in range(row_count.bit_length() - 2, 2, -1):
        half = d_table.shape[0] // 2
        d_table = added(d_table[:half], swap(d_table[half:].astype(bf16), "rows", 1 << bit))
        total = added(total, swap(total, "rows", 1 << bit)).astype(bf16)
    d_low = d_table.astype(bf16)
    d_own = added(d_table[0], *[swap(d_low[at], "rows", 2 * at) for at in range(1, 4)]).astype(bf16)
    for bit in (2, 4):
        total = added(total, swap(total, "rows", bit)).astype(bf16)
    t_near = jnp.concatenate([total, swap(total, "feat", 2)], 0)
    t_far = swap(t_near, "feat", 1)
    d_columns = exchange(d_own, "feat").astype(f32)
    d_columns = d_columns.transpose(1, 0, 2).reshape(col_width, local_rows)
    (g_query, g_key, g_value, g_enc, g_enc_bias, g_table, g_b_query, g_b_value, g_b_in, g_b_out, g_gain_one, g_shift_one,
     g_b_back, g_gain_two, g_shift_two) = finish_tail(place, t_near, t_far, w_heads, w_all, feat_total, col_width, classes)
    ends = gather_chunks(own, 48)
    g_out, g_in, g_back = finish(place, *ends)

    at = feat_index * col_width
    weight = lax.dynamic_slice_in_dim(enc_weight, at, col_width, 0).astype(f32)
    stat_one = jnp.sum(weight * g_enc_bias, 1)
    stat_two = jnp.sum(weight * lax.dynamic_slice_in_dim(g_enc, at, col_width, 0), 1)
    d_spread = -0.5 * stat_two * factor * factor
    d_mean = -factor * stat_one - 2.0 * d_spread * col_mean
    raw_grad = factor[:, None] * d_columns + (d_mean[:, None] + 2.0 * d_spread[:, None] * columns) / row_total
    flatten = lambda a: a.reshape(-1)
    return (
        layer_out, raw_grad.T, g_enc, flatten(g_enc_bias), g_table, g_query, flatten(g_b_query), g_key, g_value,
        flatten(g_b_value), g_out, flatten(g_b_out), flatten(g_gain_one), flatten(g_shift_one), g_in, flatten(g_b_in), g_back,
        flatten(g_b_back), flatten(g_gain_two), flatten(g_shift_two),
    )


def solution(mesh):
    both = ("rows", "feat")
    placed = (P("rows", "feat"),) + (P(),) * 18 + (P(both, None), P(both, None), P(both), P(both, None, None))
    results = (P(both, None, None), P("rows", "feat")) + (P(),) * 18
    return jax.shard_map(body, mesh=mesh, in_specs=placed, out_specs=results, check_vma=False)
```

time: 267 us -> 222 us (0.83); the launches traced: 263 us -> 222 us
  Pallas kernels: 136 us -> 107 us
  local copies, waits for them, and re-layouts: 20.6 us -> 8.89 us
  waiting for transfers between devices: 33 us -> 25.5 us
  other arithmetic: 12.3 us -> 17.5 us
    pallas_call x4 -> x2, Pallas kernels: 49.8 us -> 28.9 us  [score_grads(): pl.pallas_call(functools.partial(scores_kernel, start, last, ctx_pad, par...]
    ppermute x24 -> x32, waiting for transfers between devices: 33 us -> 22 us  [swap(): return lax.ppermute(value, axis, [(i, i ^ bit) for i in range(size)])]
    ppermute x24 -> x32, starting transfers between devices: 46.4 us -> 51.2 us  [swap(): return lax.ppermute(value, axis, [(i, i ^ bit) for i in range(size)])]
    all_to_all x2, waiting for transfers between devices: 0.01 us -> 3.54 us  [exchange(): return lax.all_to_all(value, axis, split_axis=0, concat_axis=0, tiled=True)]
    concatenate x6 -> x7, other arithmetic: 0.2 us -> 3.61 us  [the longest x2 1.13 us: gather_chunks(): jnp.concatenate([part, swap(part, *first)], 0)]
    all_to_all x2, starting transfers between devices: 12.8 us -> 9.71 us  [exchange(): return lax.all_to_all(value, axis, split_axis=0, concat_axis=0, tiled=True)]
    unnamed x43 -> x53, local copies, waits for them, and re-layouts: 8.08 us -> 5.61 us
  transfers between devices with their start and end apart: 26 -> 34, of which waited for: 13 -> 10; matrix products, arithmetic and copies ran while one was open for 8% -> 8% of each run, Pallas kernels for 24% -> 17%
where the time goes in v3:
time: 222 us
  Pallas kernels  107 us (48%)
  starting transfers between devices  60.9 us (27%)
  waiting for transfers between devices  25.5 us (11%)
  other arithmetic  17.5 us (8%)
  local copies, waits for them, and re-layouts  8.89 us (4%)
    pallas_call x1, Pallas kernels, forward(): pl.pallas_call(functools.partial(forward_kernel, blocks, ctx_len, ctx_pad...  61.2 us
    ppermute x32, starting transfers between devices, swap(): return lax.ppermute(value, axis, [(i, i ^ bit) for i in range(size)])  51.2 us
    pallas_call x2, Pallas kernels, score_grads(): pl.pallas_call(functools.partial(scores_kernel, start, last, ctx_pad, par...  28.9 us
    ppermute x32, waiting for transfers between devices, swap(): return lax.ppermute(value, axis, [(i, i ^ bit) for i in range(size)])  22 us
    all_to_all x2, starting transfers between devices, exchange(): return lax.all_to_all(value, axis, split_axis=0, concat_axis=0, tiled=True)  9.71 us
    unnamed x53, local copies, waits for them, and re-layouts  5.61 us
    pallas_call x1, Pallas kernels, fetch(): pl.pallas_call(functools.partial(fetch_kernel, ids.shape[0] // blocks, fe...  5.29 us
    pallas_call x1, Pallas kernels, spread(): pl.pallas_call(functools.partial(spread_kernel, span, own), grid_spec=plt...  5.16 us
  transfers between devices with their start and end apart: 34, of which 10 were waited for; matrix products, arithmetic and copies ran while one was open for 8% of the time, Pallas kernels for 17%

profile of v3, /device:TPU:1, one launch (start us, length us, event | category | flops | bytes accessed | tf_op | source)
XLA Modules:
  0.0 221.7 jit_solution(13497050817011351840)
XLA Ops:
  0.7 1.1 reduce_sum.45
  1.9 1.2 multiply_reduce_fusion
  4.1 4.3 %all-to-all-start = ((f16[4,26,512]{2,1,0:T(8,128)(2,1)}), f16[4,26,512]{2,1,0:T(8,128)(2,1)S(1)}, u32[]{:S(2)}, u32[]{:S(2)}) async-start(f16[4,26,512]{2,1,0:T(8,128)(2,1)} %pad_maximum_fusion.12), calls=%async_computation | async-start | bytes 262144 | tf_op jit(solution)/shard_map/all_to_all | solution.py:653
  11.1 1.2 pad_maximum_fusion
  12.4 3.9 %collective-permute-start.2 = (f16[1,104,512]{2,1,0:T(8,128)(2,1)S(1)}, f16[1,104,512]{2,1,0:T(8,128)(2,1)S(1)}, u32[]{:S(2)}, u32[]{:S(2)}) collective-permute-start(f16[1,104,512]{2,1,0:T(8,128)(2,1)S(1)} %reshape.334), channel_id=1, source_target_pairs={{0,24},{4,28},{8,16},{12,20},{16,8},{20,12},{24,0},{28,4},{1,25},{... | collective-permute-start | bytes 319496 | tf_op jit(solution)/shard_map/ppermute | solution.py:645
  16.7 5.9 %collective-permute-done = f16[1,104,512]{2,1,0:T(8,128)(2,1)S(1)} collective-permute-done((f16[1,104,512]{2,1,0:T(8,128)(2,1)S(1)}, f16[1,104,512]{2,1,0:T(8,128)(2,1)S(1)}, u32[]{:S(2)}, u32[]{:S(2)}) %collective-permute-start) | collective-permute-done | bytes 106528 | tf_op jit(solution)/shard_map/ppermute | solution.py:645
  22.7 2.2 %collective-permute-done.1 = f16[1,104,512]{2,1,0:T(8,128)(2,1)S(1)} collective-permute-done((f16[1,104,512]{2,1,0:T(8,128)(2,1)S(1)}, f16[1,104,512]{2,1,0:T(8,128)(2,1)S(1)}, u32[]{:S(2)}, u32[]{:S(2)}) %collective-permute-start.1) | collective-permute-done | bytes 106528 | tf_op jit(solution)/shard_map/ppermute | solution.py:645
  25.0 1.3 collective-permute-start.3
  27.2 1.6 copy.60.w_qkv
  31.0 4.1 %collective-permute-done.3 = f16[4,104,512]{2,1,0:T(8,128)(2,1)} collective-permute-done((f16[4,104,512]{2,1,0:T(8,128)(2,1)S(1)}, f16[4,104,512]{2,1,0:T(8,128)(2,1)}, u32[]{:S(2)}, u32[]{:S(2)}) %collective-permute-start.3) | collective-permute-done | bytes 426016 | tf_op jit(solution)/shard_map/ppermute | solution.py:645
  35.1 1.1 convert_element_type.166.far
  36.2 5.3 %fetch.1 = (bf16[2,1104,128]{2,1,0:T(8,128)(2,1)S(1)}, f32[8,128]{1,0:T(8,128)S(1)}) custom-call(s32[2200]{0:T(1024)S(1)} %reshape.331.ids, f32[4,104,512]{2,1,0:T(8,128)S(1)} %convert_element_type.165.near, f32[4,104,512]{2,1,0:T(8,128)S(1)} %convert_element_type.166.far, s32[2,1104]{1,0:T(2,128)S(1)} %pad.28.labels), custom_call_target="tpu_custom_call" | custom-call | flops 6000000000 | bytes 1000000 | tf_op jit(solution)/shard_map/fetch/pallas_call | solution.py:117
  42.3 61.2 %forward.1 = (bf16[2,4,1104,384]{3,2,1,0:T(8,128)(2,1)}, bf16[2,4,1104,1024]{3,2,1,0:T(8,128)(2,1)}, bf16[8800,128]{1,0:T(8,128)(2,1)}, f32[2,1104,128]{2,1,0:T(...) custom-call(s32[3]{0:T(128)} %pad_add_fusion.1.place, ...), custom_call_target="tpu_custom_call" | custom-call | flops 60000002048 | bytes 1000000 | tf_op jit(solution)/shard_map/forward/pallas_call | solution.py:350
  103.5 2.3 %collective-permute-start.4 = (bf16[16,80,512]{2,1,0:T(8,128)(2,1)}, bf16[16,80,512]{2,1,0:T(8,128)(2,1)S(1)}, u32[]{:S(2)}, u32[]{:S(2)}) collective-permute-start(bf16[16,80,512]{2,1,0:T(8,128)(2,1)} %get-tuple-element.82), channel_id=1, source_target_pairs={{0,1},{1,0},{2,3},{3,2},{4,5},{5,4},{6,7},{7,6},{8,9},{9,8},{10,11... | collective-permute-start | bytes 3932168 | tf_op jit(solution)/shard_map/ppermute | solution.py:645
  106.9 1.9 collective-permute-done.4
  108.7 1.3 add_convert_fusion
  110.1 1.6 collective-permute-start.5
  111.7 1.2 add_convert_fusion.1
  112.9 1.3 collective-permute-start.8
  114.2 1.6 copy-done.2
  115.9 1.3 copy-done.5
  117.1 14.2 %score_grads.2 = (f32[2,128,384]{2,1,0:T(8,128)S(1)}, f32[2,1104,128]{2,1,0:T(8,128)S(1)}) custom-call(s32[3]{0:T(128)S(1)} %copy-done, bf16[2,4,1104,1024]{3,2,1,0:T(8,128)(2,1)} %get-tuple-element.79.e, bf16[2,4,1104,384]{3,2,1,0:T(8,128)(2,1)S(1)} %copy-done.1, bf16[2,1104,512]{2,1,0:T(8,128)(2,1)S(1)} %copy-done.2, f32[2,1104,128]{2,1,0:T(8,128)S(1)} %copy-done.4, ...), custom_call_target="tpu_custom_call" | custom-call | flops 16000000000 | bytes 1000000 | tf_op jit(solution)/shard_map/score_grads/pallas_call | solution.py:466
  132.0 14.6 %score_grads.3 = (bf16[16,16,512]{2,1,0:T(8,128)(2,1)S(1)}, bf16[16,16,512]{2,1,0:T(8,128)(2,1)S(1)}, f32[2,1104,128]{2,1,0:T(8,128)S(1)}) custom-call(s32[3]{0:T(128)S(1)} %copy-done, bf16[2,4,1104,1024]{3,2,1,0:T(8,128)(2,1)} %get-tuple-element.79.e, bf16[2,4,1104,384]{3,2,1,0:T(8,128)(2,1)S(1)} %copy-done.1, bf16[2,1104,512]{2,1,0:T(8,128)(2,1)S(1)} %copy-done.3, ...), custom_call_target="tpu_custom_call" | custom-call | flops 16000000000 | bytes 1000000 | tf_op jit(solution)/shard_map/score_grads/pallas_call | solution.py:466
  146.6 5.2 %spread.1 = (bf16[4,4,25,512]{3,2,1,0:T(8,128)(2,1)S(1)}, bf16[4,4,25,512]{3,2,1,0:T(8,128)(2,1)S(1)}) custom-call(s32[2200]{0:T(1024)S(1)} %reshape.331.ids, f32[2,1104,128]{2,1,0:T(8,128)S(1)} %get-tuple-element.94.rows), custom_call_target="tpu_custom_call" | custom-call | flops 7000000000 | bytes 1000000 | tf_op jit(solution)/shard_map/spread/pallas_call | solution.py:526
  151.8 1.4 collective-permute-start.6
  153.5 2.3 %collective-permute-start.21 = (bf16[80,512]{1,0:T(8,128)(2,1)S(1)}, bf16[80,512]{1,0:T(8,128)(2,1)S(1)}, u32[]{:S(2)}, u32[]{:S(2)}) collective-permute-start(bf16[80,512]{1,0:T(8,128)(2,1)S(1)} %get-tuple-element.136), channel_id=1, source_target_pairs={{0,16},{4,20},{8,24},{12,28},{16,0},{20,4},{24,8},{28,12},{1,17},{... | collective-permute-start | bytes 245768 | tf_op jit(solution)/shard_map/ppermute | solution.py:645
  155.8 1.2 collective-permute-start.22
  157.0 1.5 collective-permute-start.10
  158.5 1.2 collective-permute-start.12
  159.8 1.1 collective-permute-done.22
  161.0 3.2 %collective-permute-start.25 = (bf16[80,512]{1,0:T(8,128)(2,1)S(1)}, bf16[80,512]{1,0:T(8,128)(2,1)S(1)}, u32[]{:S(2)}, u32[]{:S(2)}) collective-permute-start(bf16[80,512]{1,0:T(8,128)(2,1)S(1)} %fusion.13), channel_id=1, source_target_pairs={{0,24},{4,28},{8,16},{12,20},{16,8},{20,12},{24,0},{28,4},{1,25},{... | collective-permute-start | bytes 245768 | tf_op jit(solution)/shard_map/ppermute | solution.py:645
  165.4 1.3 collective-permute-start.11
  166.7 5.1 %collective-permute-done.24 = bf16[80,512]{1,0:T(8,128)(2,1)S(1)} collective-permute-done((bf16[80,512]{1,0:T(8,128)(2,1)S(1)}, bf16[80,512]{1,0:T(8,128)(2,1)S(1)}, u32[]{:S(2)}, u32[]{:S(2)}) %collective-permute-start.24) | collective-permute-done | bytes 81952 | tf_op jit(solution)/shard_map/ppermute | solution.py:645
  171.9 2.1 collective-permute-start.29
  174.0 1.2 collective-permute-start.26
  176.3 1.3 collective-permute-start.30
  177.7 1.2 collective-permute-done.26
  180.1 1.9 collective-permute-start.17
  182.0 2.6 %collective-permute-start.13 = (bf16[4,25,512]{2,1,0:T(8,128)(2,1)S(1)}, bf16[4,25,512]{2,1,0:T(8,128)(2,1)S(1)}, u32[]{:S(2)}, u32[]{:S(2)}) collective-permute-start(bf16[4,25,512]{2,1,0:T(8,128)(2,1)S(1)} %get-tuple-element.132), channel_id=1, source_target_pairs={{0,8},{4,12},{8,0},{12,4},{16,24},{20,28},{24,16},{28,20},{1,9},{5... | collective-permute-start | bytes 307208 | tf_op jit(solution)/shard_map/ppermute | solution.py:645
  184.7 1.1 collective-permute-start.14
  185.9 12.3 %collective-permute-start.31 = (bf16[16,32,512]{2,1,0:T(8,128)(2,1)S(1)}, bf16[16,32,512]{2,1,0:T(8,128)(2,1)S(1)}, u32[]{:S(2)}, u32[]{:S(2)}) collective-permute-start(bf16[16,32,512]{2,1,0:T(8,128)(2,1)S(1)} %pad_maximum_fusion.5.near_q), channel_id=1, source_target_pairs={{0,1},{1,0},{2,3},{3,2},{4,5},{5,4},{6,7},{7,6},{8,9},{9,8},{10,11... | collective-permute-start | bytes 1572872 | tf_op jit(solution)/shard_map/ppermute | solution.py:645
  198.3 1.7 collective-permute-start.18
  200.7 5.4 %all-to-all-start.1 = ((bf16[4,25,512]{2,1,0:T(8,128)(2,1)}), bf16[4,25,512]{2,1,0:T(8,128)(2,1)}, u32[]{:S(2)}, u32[]{:S(2)}) async-start(bf16[4,25,512]{2,1,0:T(8,128)(2,1)} %fusion.10), calls=%async_computation.1 | async-start | bytes 262144 | tf_op jit(solution)/shard_map/all_to_all | solution.py:653
  206.3 3.5 %all-to-all-done.1 = bf16[4,25,512]{2,1,0:T(8,128)(2,1)} async-done(((bf16[4,25,512]{2,1,0:T(8,128)(2,1)}), bf16[4,25,512]{2,1,0:T(8,128)(2,1)}, u32[]{:S(2)}, u32[]{:S(2)}) %all-to-all-start.1) | async-done | bytes 102432 | tf_op jit(solution)/shard_map/all_to_all | solution.py:653
  211.1 1.1 pad_maximum_fusion.2.near
  212.2 1.1 collective-permute-start.28
  213.3 3.2 %finish_tail.1 = (f32[512,512]{1,0:T(8,128)}, f32[512,512]{1,0:T(8,128)}, f32[512,512]{1,0:T(8,128)}, f32[100,512]{1,0:T(8,128)}, f32[1,512]{1,0:T(1,128)}, /*in...) custom-call(s32[3]{0:T(128)S(1)} %copy-done, ...), custom_call_target="tpu_custom_call" | custom-call | flops 5000000000 | bytes 1000000 | tf_op jit(solution)/shard_map/finish_tail/pallas_call | solution.py:624
  218.4 3.3 %finish.1 = (f32[512,512]{1,0:T(8,128)}, f32[512,1024]{1,0:T(8,128)}, f32[1024,512]{1,0:T(8,128)}) custom-call(s32[3]{0:T(128)S(1)} %copy-done, bf16[16,48,512]{2,1,0:T(8,128)(2,1)S(1)} %pad_maximum_fusion.2.near, bf16[16,48,512]{2,1,0:T(8,128)(2,1)S(1)} %collective-permute-done.28.far, bf16[16,32,512]{2,1,0:T(8,128)(2,1)S(1)} %pad_maximum_fusion.5.near_q, ...), custom_call_target="tpu_custom_call" | custom-call | flops 5000000000 | bytes 1000000 | tf_op jit(solution)/shard_map/finish/pallas_call | solution.py:566
  (153 shorter events, 17.9 us)
Async XLA Ops:
  0.7 7.8 %copy-start.19 = (f32[512]{0:T(512)S(1)}, f32[512]{0:T(512)}, u32[]{:S(2)}) copy-start(f32[512]{0:T(512)} %param.33) | copy-start | bytes 6148
  0.7 7.8 %copy-start.20 = (f32[512]{0:T(512)S(1)}, f32[512]{0:T(512)}, u32[]{:S(2)}) copy-start(f32[512]{0:T(512)} %param.30) | copy-start | bytes 6148
  0.7 8.5 %copy-start.17 = (s32[2,1100]{1,0:T(2,128)S(1)}, s32[2,1100]{1,0:T(2,128)}, u32[]{:S(2)}) copy-start(s32[2,1100]{1,0:T(2,128)} %param.44) | copy-start | bytes 26404
  0.7 8.6 %copy-start.18 = (s32[2,1000]{1,0:T(2,128)S(1)}, s32[2,1000]{1,0:T(2,128)}, u32[]{:S(2)}) copy-start(s32[2,1000]{1,0:T(2,128)} %param.45) | copy-start | bytes 24004
  0.7 8.6 %copy-start.16 = (bf16[100,512]{1,0:T(8,128)(2,1)S(1)}, bf16[100,512]{1,0:T(8,128)(2,1)}, u32[]{:S(2)}) copy-start(bf16[100,512]{1,0:T(8,128)(2,1)} %param.26) | copy-start | bytes 307204
  0.7 8.7 %copy-start.12 = (bf16[512,512]{1,0:T(8,128)(2,1)S(1)}, bf16[512,512]{1,0:T(8,128)(2,1)}, u32[]{:S(2)}) copy-start(bf16[512,512]{1,0:T(8,128)(2,1)} %param.29) | copy-start | bytes 1572868
  3.1 6.6 %copy-start.13 = (bf16[512,512]{1,0:T(8,128)(2,1)S(1)}, bf16[512,512]{1,0:T(8,128)(2,1)}, u32[]{:S(2)}) copy-start(bf16[512,512]{1,0:T(8,128)(2,1)} %param.31) | copy-start | bytes 1572868
  4.1 8.2 %all-to-all-start = ((f16[4,26,512]{2,1,0:T(8,128)(2,1)}), f16[4,26,512]{2,1,0:T(8,128)(2,1)S(1)}, u32[]{:S(2)}, u32[]{:S(2)}) async-start(f16[4,26,512]{2,1,0:T(8,128)(2,1)} %pad_maximum_fusion.12), calls=%async_computation | async-start | bytes 262144 | tf_op jit(solution)/shard_map/all_to_all | solution.py:653
  12.4 12.5 %collective-permute-start.2 = (f16[1,104,512]{2,1,0:T(8,128)(2,1)S(1)}, f16[1,104,512]{2,1,0:T(8,128)(2,1)S(1)}, u32[]{:S(2)}, u32[]{:S(2)}) collective-permute-start(f16[1,104,512]{2,1,0:T(8,128)(2,1)S(1)} %reshape.334), channel_id=1, source_target_pairs={{0,24},{4,28},{8,16},{12,20},{16,8},{20,12},{24,0},{28,4},{1,25},{... | collective-permute-start | bytes 319496 | tf_op jit(solution)/shard_map/ppermute | solution.py:645
  16.3 8.6 %collective-permute-start.1 = (f16[1,104,512]{2,1,0:T(8,128)(2,1)S(1)}, f16[1,104,512]{2,1,0:T(8,128)(2,1)S(1)}, u32[]{:S(2)}, u32[]{:S(2)}) collective-permute-start(f16[1,104,512]{2,1,0:T(8,128)(2,1)S(1)} %reshape.334), channel_id=1, source_target_pairs={{0,16},{4,20},{8,24},{12,28},{16,0},{20,4},{24,8},{28,12},{1,17},{... | collective-permute-start | bytes 319496 | tf_op jit(solution)/shard_map/ppermute | solution.py:645
  16.3 6.3 %collective-permute-start = (f16[1,104,512]{2,1,0:T(8,128)(2,1)S(1)}, f16[1,104,512]{2,1,0:T(8,128)(2,1)S(1)}, u32[]{:S(2)}, u32[]{:S(2)}) collective-permute-start(f16[1,104,512]{2,1,0:T(8,128)(2,1)S(1)} %reshape.334), channel_id=1, source_target_pairs={{0,8},{4,12},{8,0},{12,4},{16,24},{20,28},{24,16},{28,20},{1,9},{5... | collective-permute-start | bytes 319496 | tf_op jit(solution)/shard_map/ppermute | solution.py:645
  25.0 10.1 %collective-permute-start.3 = (f16[4,104,512]{2,1,0:T(8,128)(2,1)S(1)}, f16[4,104,512]{2,1,0:T(8,128)(2,1)}, u32[]{:S(2)}, u32[]{:S(2)}) collective-permute-start(f16[4,104,512]{2,1,0:T(8,128)(2,1)S(1)} %constant_dynamic-update-slice_fusion), channel_id=1, source_target_pairs={{0,4},{4,0},{8,12},{12,8},{16,20},{20,16},{24,28},{28,24},{1,5},{5... | collective-permute-start | bytes 1277960 | tf_op jit(solution)/shard_map/ppermute | solution.py:645
  42.3 63.6 %copy-start.21 = (f32[512]{0:T(512)S(1)}, f32[512]{0:T(512)}, u32[]{:S(2)}) copy-start(f32[512]{0:T(512)} %param.27) | copy-start | bytes 6148
  103.5 5.2 %collective-permute-start.4 = (bf16[16,80,512]{2,1,0:T(8,128)(2,1)}, bf16[16,80,512]{2,1,0:T(8,128)(2,1)S(1)}, u32[]{:S(2)}, u32[]{:S(2)}) collective-permute-start(bf16[16,80,512]{2,1,0:T(8,128)(2,1)} %get-tuple-element.82), channel_id=1, source_target_pairs={{0,1},{1,0},{2,3},{3,2},{4,5},{5,4},{6,7},{7,6},{8,9},{9,8},{10,11... | collective-permute-start | bytes 3932168 | tf_op jit(solution)/shard_map/ppermute | solution.py:645
  106.1 8.1 %copy-start.1 = (bf16[2,4,1104,384]{3,2,1,0:T(8,128)(2,1)S(1)}, bf16[2,4,1104,384]{3,2,1,0:T(8,128)(2,1)}, u32[]{:S(2)}) copy-start(bf16[2,4,1104,384]{3,2,1,0:T(8,128)(2,1)} %get-tuple-element.80.qkv) | copy-start | bytes 20348932
  110.1 4.2 %copy-start = (s32[3]{0:T(128)S(1)}, s32[3]{0:T(128)}, u32[]{:S(2)}) copy-start(s32[3]{0:T(128)} %pad_add_fusion.1.place) | copy-start | bytes 40
  110.1 4.1 %copy-start.4 = (f32[2,1104,128]{2,1,0:T(8,128)S(1)}, f32[2,1104,128]{2,1,0:T(8,128)}, u32[]{:S(2)}) copy-start(f32[2,1104,128]{2,1,0:T(8,128)} %get-tuple-element.86.shift) | copy-start | bytes 3391492
  110.1 21.5 %collective-permute-start.5 = (bf16[8,48,512]{2,1,0:T(8,128)(2,1)S(1)}, bf16[8,48,512]{2,1,0:T(8,128)(2,1)S(1)}, u32[]{:S(2)}, u32[]{:S(2)}) collective-permute-start(bf16[8,48,512]{2,1,0:T(8,128)(2,1)S(1)} %get-tuple-element.128), channel_id=1, source_target_pairs={{0,2},{1,3},{2,0},{3,1},{4,6},{5,7},{6,4},{7,5},{8,10},{9,11},{10,... | collective-permute-start | bytes 1179656 | tf_op jit(solution)/shard_map/ppermute | solution.py:645
  112.9 18.4 %collective-permute-start.8 = (bf16[8,32,512]{2,1,0:T(8,128)(2,1)S(1)}, bf16[8,32,512]{2,1,0:T(8,128)(2,1)S(1)}, u32[]{:S(2)}, u32[]{:S(2)}) collective-permute-start(bf16[8,32,512]{2,1,0:T(8,128)(2,1)S(1)} %get-tuple-element.126), channel_id=1, source_target_pairs={{0,4},{4,0},{8,12},{12,8},{16,20},{20,16},{24,28},{28,24},{1,5},{5... | collective-permute-start | bytes 786440 | tf_op jit(solution)/shard_map/ppermute | solution.py:645
  117.1 14.8 %copy-start.3 = (bf16[2,1104,512]{2,1,0:T(8,128)(2,1)S(1)}, bf16[2,1104,512]{2,1,0:T(8,128)(2,1)}, u32[]{:S(2)}) copy-start(bf16[2,1104,512]{2,1,0:T(8,128)(2,1)} %get-tuple-element.85.back) | copy-start | bytes 6782980
  117.1 14.8 %copy-start.8 = (f32[128,512]{1,0:T(8,128)S(1)}, f32[128,512]{1,0:T(8,128)}, u32[]{:S(2)}) copy-start(f32[128,512]{1,0:T(8,128)} %get-tuple-element.90.refs_1_) | copy-start | bytes 786436
  131.4 21.8 %collective-permute-start.9 = (bf16[4,32,512]{2,1,0:T(8,128)(2,1)S(1)}, bf16[4,32,512]{2,1,0:T(8,128)(2,1)S(1)}, u32[]{:S(2)}, u32[]{:S(2)}) collective-permute-start(bf16[4,32,512]{2,1,0:T(8,128)(2,1)S(1)} %fusion.4), channel_id=1, source_target_pairs={{0,2},{1,3},{2,0},{3,1},{4,6},{5,7},{6,4},{7,5},{8,10},{9,11},{10,... | collective-permute-start | bytes 393224 | tf_op jit(solution)/shard_map/ppermute | solution.py:645
  131.7 21.6 %collective-permute-start.7 = (bf16[4,48,512]{2,1,0:T(8,128)(2,1)S(1)}, bf16[4,48,512]{2,1,0:T(8,128)(2,1)S(1)}, u32[]{:S(2)}, u32[]{:S(2)}) collective-permute-start(bf16[4,48,512]{2,1,0:T(8,128)(2,1)S(1)} %fusion.3), channel_id=1, source_target_pairs={{0,4},{4,0},{8,12},{12,8},{16,20},{20,16},{24,28},{28,24},{1,5},{5... | collective-permute-start | bytes 589832 | tf_op jit(solution)/shard_map/ppermute | solution.py:645
  151.8 5.2 %collective-permute-start.6 = (bf16[16,16,512]{2,1,0:T(8,128)(2,1)S(1)}, bf16[16,16,512]{2,1,0:T(8,128)(2,1)S(1)}, u32[]{:S(2)}, u32[]{:S(2)}) collective-permute-start(bf16[16,16,512]{2,1,0:T(8,128)(2,1)S(1)} %get-tuple-element.92), channel_id=1, source_target_pairs={{0,1},{1,0},{2,3},{3,2},{4,5},{5,4},{6,7},{7,6},{8,9},{9,8},{10,11... | collective-permute-start | bytes 786440 | tf_op jit(solution)/shard_map/ppermute | solution.py:645
  153.4 6.4 %collective-permute-start.20 = (bf16[80,512]{1,0:T(8,128)(2,1)S(1)}, bf16[80,512]{1,0:T(8,128)(2,1)S(1)}, u32[]{:S(2)}, u32[]{:S(2)}) collective-permute-start(bf16[80,512]{1,0:T(8,128)(2,1)S(1)} %get-tuple-element.135), channel_id=1, source_target_pairs={{0,8},{4,12},{8,0},{12,4},{16,24},{20,28},{24,16},{28,20},{1,9},{5... | collective-permute-start | bytes 245768 | tf_op jit(solution)/shard_map/ppermute | solution.py:645
  153.5 6.3 %collective-permute-start.21 = (bf16[80,512]{1,0:T(8,128)(2,1)S(1)}, bf16[80,512]{1,0:T(8,128)(2,1)S(1)}, u32[]{:S(2)}, u32[]{:S(2)}) collective-permute-start(bf16[80,512]{1,0:T(8,128)(2,1)S(1)} %get-tuple-element.136), channel_id=1, source_target_pairs={{0,16},{4,20},{8,24},{12,28},{16,0},{20,4},{24,8},{28,12},{1,17},{... | collective-permute-start | bytes 245768 | tf_op jit(solution)/shard_map/ppermute | solution.py:645
  155.8 5.2 %collective-permute-start.22 = (bf16[80,512]{1,0:T(8,128)(2,1)S(1)}, bf16[80,512]{1,0:T(8,128)(2,1)S(1)}, u32[]{:S(2)}, u32[]{:S(2)}) collective-permute-start(bf16[80,512]{1,0:T(8,128)(2,1)S(1)} %get-tuple-element.137), channel_id=1, source_target_pairs={{0,24},{4,28},{8,16},{12,20},{16,8},{20,12},{24,0},{28,4},{1,25},{... | collective-permute-start | bytes 245768 | tf_op jit(solution)/shard_map/ppermute | solution.py:645
  157.0 8.3 %collective-permute-start.10 = (bf16[8,16,512]{2,1,0:T(8,128)(2,1)S(1)}, bf16[8,16,512]{2,1,0:T(8,128)(2,1)S(1)}, u32[]{:S(2)}, u32[]{:S(2)}) collective-permute-start(bf16[8,16,512]{2,1,0:T(8,128)(2,1)S(1)} %add_convert_fusion.6), channel_id=1, source_target_pairs={{0,2},{1,3},{2,0},{3,1},{4,6},{5,7},{6,4},{7,5},{8,10},{9,11},{10,... | collective-permute-start | bytes 393224 | tf_op jit(solution)/shard_map/ppermute | solution.py:645
  158.5 16.7 %collective-permute-start.12 = (bf16[4,4,25,512]{3,2,1,0:T(8,128)(2,1)S(1)}, bf16[4,4,25,512]{3,2,1,0:T(8,128)(2,1)S(1)}, u32[]{:S(2)}, u32[]{:S(2)}) collective-permute-start(bf16[4,4,25,512]{3,2,1,0:T(8,128)(2,1)S(1)} %get-tuple-element.99), channel_id=1, source_target_pairs={{0,4},{4,0},{8,12},{12,8},{16,20},{20,16},{24,28},{28,24},{1,5},{5... | collective-permute-start | bytes 1228808 | tf_op jit(solution)/shard_map/ppermute | solution.py:645
  161.0 5.7 %collective-permute-start.25 = (bf16[80,512]{1,0:T(8,128)(2,1)S(1)}, bf16[80,512]{1,0:T(8,128)(2,1)S(1)}, u32[]{:S(2)}, u32[]{:S(2)}) collective-permute-start(bf16[80,512]{1,0:T(8,128)(2,1)S(1)} %fusion.13), channel_id=1, source_target_pairs={{0,24},{4,28},{8,16},{12,20},{16,8},{20,12},{24,0},{28,4},{1,25},{... | collective-permute-start | bytes 245768 | tf_op jit(solution)/shard_map/ppermute | solution.py:645
  164.2 7.6 %collective-permute-start.24 = (bf16[80,512]{1,0:T(8,128)(2,1)S(1)}, bf16[80,512]{1,0:T(8,128)(2,1)S(1)}, u32[]{:S(2)}, u32[]{:S(2)}) collective-permute-start(bf16[80,512]{1,0:T(8,128)(2,1)S(1)} %fusion.13), channel_id=1, source_target_pairs={{0,16},{4,20},{8,24},{12,28},{16,0},{20,4},{24,8},{28,12},{1,17},{... | collective-permute-start | bytes 245768 | tf_op jit(solution)/shard_map/ppermute | solution.py:645
  165.2 6.6 %collective-permute-start.23 = (bf16[80,512]{1,0:T(8,128)(2,1)S(1)}, bf16[80,512]{1,0:T(8,128)(2,1)S(1)}, u32[]{:S(2)}, u32[]{:S(2)}) collective-permute-start(bf16[80,512]{1,0:T(8,128)(2,1)S(1)} %fusion.13), channel_id=1, source_target_pairs={{0,8},{4,12},{8,0},{12,4},{16,24},{20,28},{24,16},{28,20},{1,9},{5... | collective-permute-start | bytes 245768 | tf_op jit(solution)/shard_map/ppermute | solution.py:645
  165.4 9.8 %collective-permute-start.11 = (bf16[8,16,512]{2,1,0:T(8,128)(2,1)S(1)}, bf16[8,16,512]{2,1,0:T(8,128)(2,1)S(1)}, u32[]{:S(2)}, u32[]{:S(2)}) collective-permute-start(bf16[8,16,512]{2,1,0:T(8,128)(2,1)S(1)} %add_convert_fusion.5), channel_id=1, source_target_pairs={{0,4},{4,0},{8,12},{12,8},{16,20},{20,16},{24,28},{28,24},{1,5},{5... | collective-permute-start | bytes 393224 | tf_op jit(solution)/shard_map/ppermute | solution.py:645
  171.9 4.4 %collective-permute-start.29 = (bf16[4,32,512]{2,1,0:T(8,128)(2,1)S(1)}, bf16[4,32,512]{2,1,0:T(8,128)(2,1)S(1)}, u32[]{:S(2)}, u32[]{:S(2)}) collective-permute-start(bf16[4,32,512]{2,1,0:T(8,128)(2,1)S(1)} %pad_maximum_fusion.11), channel_id=1, source_target_pairs={{0,2},{1,3},{2,0},{3,1},{4,6},{5,7},{6,4},{7,5},{8,10},{9,11},{10,... | collective-permute-start | bytes 393224 | tf_op jit(solution)/shard_map/ppermute | solution.py:645
  174.0 4.9 %collective-permute-start.26 = (bf16[4,48,512]{2,1,0:T(8,128)(2,1)S(1)}, bf16[4,48,512]{2,1,0:T(8,128)(2,1)S(1)}, u32[]{:S(2)}, u32[]{:S(2)}) collective-permute-start(bf16[4,48,512]{2,1,0:T(8,128)(2,1)S(1)} %slice.170), channel_id=1, source_target_pairs={{0,4},{4,0},{8,12},{12,8},{16,20},{20,16},{24,28},{28,24},{1,5},{5... | collective-permute-start | bytes 589832 | tf_op jit(solution)/shard_map/ppermute | solution.py:645
  175.4 4.6 %collective-permute-start.16 = (bf16[8,16,512]{2,1,0:T(8,128)(2,1)S(1)}, bf16[8,16,512]{2,1,0:T(8,128)(2,1)S(1)}, u32[]{:S(2)}, u32[]{:S(2)}) collective-permute-start(bf16[8,16,512]{2,1,0:T(8,128)(2,1)S(1)} %add_convert_fusion.4), channel_id=1, source_target_pairs={{0,8},{4,12},{8,0},{12,4},{16,24},{20,28},{24,16},{28,20},{1,9},{5... | collective-permute-start | bytes 393224 | tf_op jit(solution)/shard_map/ppermute | solution.py:645
  176.3 8.4 %collective-permute-start.30 = (bf16[8,32,512]{2,1,0:T(8,128)(2,1)S(1)}, bf16[8,32,512]{2,1,0:T(8,128)(2,1)S(1)}, u32[]{:S(2)}, u32[]{:S(2)}) collective-permute-start(bf16[8,32,512]{2,1,0:T(8,128)(2,1)S(1)} %pad_maximum_fusion.10), channel_id=1, source_target_pairs={{0,4},{4,0},{8,12},{12,8},{16,20},{20,16},{24,28},{28,24},{1,5},{5... | collective-permute-start | bytes 786440 | tf_op jit(solution)/shard_map/ppermute | solution.py:645
  179.7 31.5 %collective-permute-start.27 = (bf16[8,48,512]{2,1,0:T(8,128)(2,1)}, bf16[8,48,512]{2,1,0:T(8,128)(2,1)}, u32[]{:S(2)}, u32[]{:S(2)}) collective-permute-start(bf16[8,48,512]{2,1,0:T(8,128)(2,1)} %pad_maximum_fusion.6), channel_id=1, source_target_pairs={{0,2},{1,3},{2,0},{3,1},{4,6},{5,7},{6,4},{7,5},{8,10},{9,11},{10,... | collective-permute-start | bytes 1179656 | tf_op jit(solution)/shard_map/ppermute | solution.py:645
  180.1 5.9 %collective-permute-start.17 = (bf16[8,16,512]{2,1,0:T(8,128)(2,1)S(1)}, bf16[8,16,512]{2,1,0:T(8,128)(2,1)S(1)}, u32[]{:S(2)}, u32[]{:S(2)}) collective-permute-start(bf16[8,16,512]{2,1,0:T(8,128)(2,1)S(1)} %add_convert_fusion.3), channel_id=1, source_target_pairs={{0,16},{4,20},{8,24},{12,28},{16,0},{20,4},{24,8},{28,12},{1,17},{... | collective-permute-start | bytes 393224 | tf_op jit(solution)/shard_map/ppermute | solution.py:645
  182.0 16.3 %collective-permute-start.13 = (bf16[4,25,512]{2,1,0:T(8,128)(2,1)S(1)}, bf16[4,25,512]{2,1,0:T(8,128)(2,1)S(1)}, u32[]{:S(2)}, u32[]{:S(2)}) collective-permute-start(bf16[4,25,512]{2,1,0:T(8,128)(2,1)S(1)} %get-tuple-element.132), channel_id=1, source_target_pairs={{0,8},{4,12},{8,0},{12,4},{16,24},{20,28},{24,16},{28,20},{1,9},{5... | collective-permute-start | bytes 307208 | tf_op jit(solution)/shard_map/ppermute | solution.py:645
  184.6 15.4 %collective-permute-start.15 = (bf16[4,25,512]{2,1,0:T(8,128)(2,1)S(1)}, bf16[4,25,512]{2,1,0:T(8,128)(2,1)S(1)}, u32[]{:S(2)}, u32[]{:S(2)}) collective-permute-start(bf16[4,25,512]{2,1,0:T(8,128)(2,1)S(1)} %get-tuple-element.133), channel_id=1, source_target_pairs={{0,24},{4,28},{8,16},{12,20},{16,8},{20,12},{24,0},{28,4},{1,25},{... | collective-permute-start | bytes 307208 | tf_op jit(solution)/shard_map/ppermute | solution.py:645
  184.7 15.3 %collective-permute-start.14 = (bf16[4,25,512]{2,1,0:T(8,128)(2,1)S(1)}, bf16[4,25,512]{2,1,0:T(8,128)(2,1)S(1)}, u32[]{:S(2)}, u32[]{:S(2)}) collective-permute-start(bf16[4,25,512]{2,1,0:T(8,128)(2,1)S(1)} %get-tuple-element.134), channel_id=1, source_target_pairs={{0,16},{4,20},{8,24},{12,28},{16,0},{20,4},{24,8},{28,12},{1,17},{... | collective-permute-start | bytes 307208 | tf_op jit(solution)/shard_map/ppermute | solution.py:645
  185.9 32.5 %collective-permute-start.31 = (bf16[16,32,512]{2,1,0:T(8,128)(2,1)S(1)}, bf16[16,32,512]{2,1,0:T(8,128)(2,1)S(1)}, u32[]{:S(2)}, u32[]{:S(2)}) collective-permute-start(bf16[16,32,512]{2,1,0:T(8,128)(2,1)S(1)} %pad_maximum_fusion.5.near_q), channel_id=1, source_target_pairs={{0,1},{1,0},{2,3},{3,2},{4,5},{5,4},{6,7},{7,6},{8,9},{9,8},{10,11... | collective-permute-start | bytes 1572872 | tf_op jit(solution)/shard_map/ppermute | solution.py:645
  198.3 7.9 %collective-permute-start.18 = (bf16[8,16,512]{2,1,0:T(8,128)(2,1)S(1)}, bf16[8,16,512]{2,1,0:T(8,128)(2,1)S(1)}, u32[]{:S(2)}, u32[]{:S(2)}) collective-permute-start(bf16[8,16,512]{2,1,0:T(8,128)(2,1)S(1)} %add_convert_fusion.2), channel_id=1, source_target_pairs={{0,2},{1,3},{2,0},{3,1},{4,6},{5,7},{6,4},{7,5},{8,10},{9,11},{10,... | collective-permute-start | bytes 393224 | tf_op jit(solution)/shard_map/ppermute | solution.py:645
  200.7 9.1 %all-to-all-start.1 = ((bf16[4,25,512]{2,1,0:T(8,128)(2,1)}), bf16[4,25,512]{2,1,0:T(8,128)(2,1)}, u32[]{:S(2)}, u32[]{:S(2)}) async-start(bf16[4,25,512]{2,1,0:T(8,128)(2,1)} %fusion.10), calls=%async_computation.1 | async-start | bytes 262144 | tf_op jit(solution)/shard_map/all_to_all | solution.py:653
  206.2 7.1 %collective-permute-start.19 = (bf16[16,16,512]{2,1,0:T(8,128)(2,1)S(1)}, bf16[16,16,512]{2,1,0:T(8,128)(2,1)S(1)}, u32[]{:S(2)}, u32[]{:S(2)}) collective-permute-start(bf16[16,16,512]{2,1,0:T(8,128)(2,1)S(1)} %pad_maximum_fusion.9.near), channel_id=1, source_target_pairs={{0,1},{1,0},{2,3},{3,2},{4,5},{5,4},{6,7},{7,6},{8,9},{9,8},{10,11... | collective-permute-start | bytes 786440 | tf_op jit(solution)/shard_map/ppermute | solution.py:645
  212.2 5.4 %copy-start.9 = (f32[2048,25]{0,1:T(8,128)S(1)}, f32[2048,25]{0,1:T(8,128)}, u32[]{:S(2)}) copy-start(f32[2048,25]{0,1:T(8,128)} %param.25) | copy-start | bytes 614404
  212.2 6.2 %collective-permute-start.28 = (bf16[16,48,512]{2,1,0:T(8,128)(2,1)S(1)}, bf16[16,48,512]{2,1,0:T(8,128)(2,1)S(1)}, u32[]{:S(2)}, u32[]{:S(2)}) collective-permute-start(bf16[16,48,512]{2,1,0:T(8,128)(2,1)S(1)} %pad_maximum_fusion.2.near), channel_id=1, source_target_pairs={{0,1},{1,0},{2,3},{3,2},{4,5},{5,4},{6,7},{7,6},{8,9},{9,8},{10,11... | collective-permute-start | bytes 2359304 | tf_op jit(solution)/shard_map/ppermute | solution.py:645
  (8 other events, 12.9 us)

commit v4 on v3

--- a/solution.py
+++ b/solution.py
@@ -14,7 +14,7 @@
 CHUNKS = 32
 SMALLS = 120
 SPAN = 64.0
-VMEM_LIMIT = 60 * 1024 * 1024
+VMEM_LIMIT = 54 * 1024 * 1024
 f32 = jnp.float32
 bf16 = jnp.bfloat16
 
@@ -153,7 +153,7 @@
 def forward_kernel(blocks, ctx_len, ctx_pad, parts,
                    place, queries, feats, cot, w_embed, b_enc, w_qkv, b_qkv, w_out, b_out, gain_one, shift_one,
                    w_in, b_in, w_back, b_back, gain_two, shift_two, w_out_t,
-                   qkv_o, e_o, out_o, rows_o, back_o, shift_o, keep_o, give_o, aug_o,
+                   qkv_o, e_o, out_o, rows_o, back_o, keep_o, give_o, aug_o,
                    mixed, inv, out_f, act_s, norm_s, d_hid_s, d_bra_s, d_att_s, g_out, g_in, g_back, wide, narrow):
     tick = pl.program_id(0)
     pad = qkv_o.shape[2]
@@ -168,15 +168,15 @@
 
         @pl.when(head == 0)
         def _():
-            def project(c, _):
-                rows = pl.ds(pl.multiple_of(c * step, 16), step)
+            def project(c):
+                rows = slice(c * step, (c + 1) * step)
                 low = embed(feats[block, rows, :], w_embed, b_enc).astype(bf16)
                 made = (dot(low, w_qkv[...]) + b_qkv[...]).astype(bf16)
                 for h in range(HEADS):
                     qkv_o[0, h, rows, :] = made[:, h * 3 * width:(h + 1) * 3 * width]
-                return 0
-
-            lax.fori_loop(0, parts, project, 0)
+
+            for c in range(parts):
+                project(c)
 
         factor = math.log2(math.e) / math.sqrt(width)
         keys = qkv_o[0, head, :ctx_pad, width:2 * width]
@@ -198,19 +198,16 @@
                 e_o[0, 0, spans[c], edge:] = jnp.exp2((rear - most) * factor).astype(bf16)
             e_o[0, 0, spans[c], :edge] = jnp.exp2((front - most) * factor).astype(bf16)
 
-        def mix(c):
-            summed = dot(e_o[0, 0, spans[c], :], vals)
-            inverse = 1.0 / summed[:, width:]
-            lane = lax.broadcasted_iota(jnp.int32, (step, LANES), 1)
-            inv[block, spans[c], :] = jnp.where(lane == head, inverse[:, :LANES], inv[block, spans[c], :])
-            mixed[block, spans[c], cols] = (summed[:, :width] * inverse).astype(bf16)
-
         ready = score(0)
         for c in range(parts):
             coming = score(c + 1) if c + 1 < parts else None
             weigh(c, ready)
-            mix(c)
             ready = coming
+        summed = dot(e_o[0, 0], vals)
+        inverse = 1.0 / summed[:, width:]
+        lane = lax.broadcasted_iota(jnp.int32, (pad, LANES), 1)
+        inv[block] = jnp.where(lane == head, inverse[:, :LANES], inv[block])
+        mixed[block, :, cols] = (summed[:, :width] * inverse).astype(bf16)
 
     @pl.when(tick >= blocks * HEADS)
     def _():
@@ -280,7 +277,7 @@
             yield
             both = dot(d_att_s[here, :], w_out_t[...])
             yield
-            rows_o[block] = both[:, model:]
+            row_part = both[:, model:]
             back = both[:, :model].astype(bf16).astype(f32)
             lane = lax.broadcasted_iota(jnp.int32, (step, LANES), 1)
             shifts = jnp.zeros((step, LANES), f32)
@@ -289,8 +286,8 @@
                 scaled = (back[:, cols] * inv[block, rows, h:h + 1]).astype(bf16)
                 back_o[block, :, cols] = scaled
                 moved = jnp.sum(scaled.astype(f32) * mixed_low[:, cols].astype(f32), 1, keepdims=True)
-                shifts = jnp.where(lane == h, -moved, shifts)
-            shift_o[block] = shifts
+                shifts = jnp.where(lane == SMALLS + h, -moved, shifts)
+            rows_o[block] = row_part + shifts
             yield
 
         flows = [flow(block) for block in range(blocks)]
@@ -357,7 +354,7 @@
                 pl.BlockSpec((1, HEADS, pad, 3 * width), lambda t, *_: (attending(t) // HEADS, 0, 0, 0)),
                 pl.BlockSpec((1, 1, pad, ctx_pad), lambda t, *_: (attending(t) // HEADS, attending(t) % HEADS, 0, 0)),
                 pl.BlockSpec((step * flat, LANES), lambda t, *_: (later(t), 0)),
-                rowed(LANES), rowed(model), rowed(LANES),
+                rowed(LANES), rowed(model),
                 full(CHUNKS // 2, 80, model), full(CHUNKS // 2, 80, model), full(LANES, model)],
             scratch_shapes=[
                 pltpu.VMEM((blocks, pad, model), bf16), pltpu.VMEM((blocks, pad, LANES), f32), pltpu.VMEM((step * flat, LANES), f32),
@@ -369,7 +366,7 @@
         out_shape=[
             shape((blocks, HEADS, pad, 3 * width), bf16),
             shape((blocks, HEADS, pad, ctx_pad), bf16), shape(cot.shape, bf16), shape((blocks, pad, LANES), f32),
-            shape((blocks, pad, model), bf16), shape((blocks, pad, LANES), f32), shape((CHUNKS // 2, 80, model), bf16),
+            shape((blocks, pad, model), bf16), shape((CHUNKS // 2, 80, model), bf16),
             shape((CHUNKS // 2, 80, model), bf16), shape((LANES, model), f32)],
         compiler_params=params(0),
         cost_estimate=cost(60, 1),
@@ -377,7 +374,7 @@
     )(place, queries, feats, cot, *weights)
 
 
-def scores_kernel(start, last, ctx_pad, parts, place, e, qkv, back, shift, feats, w_rows, d_rows, *refs):
+def scores_kernel(start, last, ctx_pad, parts, place, e, qkv, back, feats, w_rows, d_rows, *refs):
     block = pl.program_id(0)
     at = pl.program_id(1)
     count = pl.num_programs(1)
@@ -393,7 +390,7 @@
     keys = qkv[0, 0, :ctx_pad, width:2 * width]
     vals = jnp.concatenate([qkv[0, 0, :ctx_pad, 2 * width:], jnp.ones((ctx_pad, width), bf16)], 1)
     lane = lax.broadcasted_iota(jnp.int32, (pad, width), 1)
-    moved = jnp.sum(jnp.where(lane == start + at, shift[0], 0.0), 1, keepdims=True)
+    moved = jnp.sum(jnp.where(lane == SMALLS + start + at, d_rows[0], 0.0), 1, keepdims=True)
     top = moved.astype(bf16).astype(f32)
     dox[:, :width] = back[0]
     dox[:, width:] = jnp.where(lane == 0, top, jnp.where(lane == 1, moved - top, 0.0)).astype(bf16)
@@ -452,7 +449,7 @@
                 lax.fori_loop(0, CHUNKS // 2, lay, 0)
 
 
-def score_grads(place, start, count, e, qkv, back, shift, feats, w_rows, d_rows, early, first):
+def score_grads(place, start, count, e, qkv, back, feats, w_rows, d_rows, early, first):
     blocks, pad, model = back.shape
     ctx_pad = e.shape[3]
     width = model // HEADS
@@ -471,7 +468,7 @@
             in_specs=[pl.BlockSpec((1, 1, pad, ctx_pad), lambda b, h, *_: (b, start + h, 0, 0)),
                       pl.BlockSpec((1, 1, pad, 3 * width), lambda b, h, *_: (b, start + h, 0, 0)),
                       pl.BlockSpec((1, pad, width), lambda b, h, *_: (b, 0, start + h)),
-                      rowed, rowed,
+                      rowed,
                       pl.BlockSpec((1, 3 * width, 2 * LANES), lambda b, h, *_: (start + h, 0, 0)),
                       rowed] + [full(*a.shape) for a in late],
             out_specs=[full(*end.shape) for end in ends] + [rowed],
@@ -482,7 +479,7 @@
         compiler_params=params(0, 0, room=36 << 20),
         cost_estimate=cost(8 * count, 1),
         name="score_grads",
-    )(place, e, qkv, back, shift, feats, w_rows, d_rows, *late)
+    )(place, e, qkv, back, feats, w_rows, d_rows, *late)
 
 
 def spread_kernel(span, own, ids, rows, near_o, far_o, *tables):
@@ -775,14 +772,14 @@
     w_out_t = jnp.concatenate([w_out.T, w_feat_t], 1)
     weights = (w_embed, b_enc, w_qkv, b_qkv, w_out, row(b_out), row(gain_one), row(shift_one), w_in, row(b_in),
                w_back, row(b_back), row(gain_two), row(shift_two), w_out_t)
-    qkv, expo, layer_out, d_rows, back, shift, keep, give, first = forward(place, queries, feats, flat, weights, ctx_len)
+    qkv, expo, layer_out, d_rows, back, keep, give, first = forward(place, queries, feats, flat, weights, ctx_len)
     layer_out = layer_out.reshape(span, tiles, blocks, LANES).transpose(0, 2, 1, 3).reshape(span, blocks, model).transpose(1, 0, 2)
 
     steps = reduce_chunks(keep, give, 48)
     early = []
     for start, count in CALLS:
         held, back = lax.optimization_barrier((next(steps), back))
-        *made, d_rows = score_grads(place, start, count, expo, qkv, back, shift, feats, w_rows, d_rows, early, first)
+        *made, d_rows = score_grads(place, start, count, expo, qkv, back, feats, w_rows, d_rows, early, first)
         early.append(made[0])
     held, d_rows = lax.optimization_barrier((next(steps), d_rows))
     near, far = spread(ids, d_rows, row_count, feat_count, col_width, own_rows)

time: 222 us -> 219 us (0.986)
    unnamed x53 -> x51, local copies, waits for them, and re-layouts: 5.61 us -> 4.35 us
where the time goes in v4:
time: 219 us
  Pallas kernels  105 us (48%)
  starting transfers between devices  61 us (28%)
  waiting for transfers between devices  25.5 us (12%)
  other arithmetic  17.5 us (8%)
  local copies, waits for them, and re-layouts  7.64 us (3%)
    pallas_call x1, Pallas kernels, forward(): pl.pallas_call(functools.partial(forward_kernel, blocks, ctx_len, ctx_pad...  59.4 us
    ppermute x32, starting transfers between devices, swap(): return lax.ppermute(value, axis, [(i, i ^ bit) for i in range(size)])  51.2 us
    pallas_call x2, Pallas kernels, score_grads(): pl.pallas_call(functools.partial(scores_kernel, start, last, ctx_pad, par...  28.8 us
    ppermute x32, waiting for transfers between devices, swap(): return lax.ppermute(value, axis, [(i, i ^ bit) for i in range(size)])  22 us
    all_to_all x2, starting transfers between devices, exchange(): return lax.all_to_all(value, axis, split_axis=0, concat_axis=0, tiled=True)  9.73 us
    pallas_call x1, Pallas kernels, fetch(): pl.pallas_call(functools.partial(fetch_kernel, ids.shape[0] // blocks, fe...  5.3 us
    pallas_call x1, Pallas kernels, spread(): pl.pallas_call(functools.partial(spread_kernel, span, own), grid_spec=plt...  5.16 us
  transfers between devices with their start and end apart: 34, of which 10 were waited for; matrix products, arithmetic and copies ran while one was open for 8% of the time, Pallas kernels for 17%

profile of v4, /device:TPU:1, one launch (start us, length us, event | category | flops | bytes accessed | tf_op | source)
XLA Modules:
  0.0 218.7 jit_solution(7970141072057006964)
XLA Ops:
  0.7 1.1 reduce_sum.45
  1.9 1.2 multiply_reduce_fusion
  4.1 4.3 %all-to-all-start = ((f16[4,26,512]{2,1,0:T(8,128)(2,1)}), f16[4,26,512]{2,1,0:T(8,128)(2,1)S(1)}, u32[]{:S(2)}, u32[]{:S(2)}) async-start(f16[4,26,512]{2,1,0:T(8,128)(2,1)} %pad_maximum_fusion.12), calls=%async_computation | async-start | bytes 262144 | tf_op jit(solution)/shard_map/all_to_all | solution.py:650
  11.1 1.2 pad_maximum_fusion
  12.4 3.9 %collective-permute-start.2 = (f16[1,104,512]{2,1,0:T(8,128)(2,1)S(1)}, f16[1,104,512]{2,1,0:T(8,128)(2,1)S(1)}, u32[]{:S(2)}, u32[]{:S(2)}) collective-permute-start(f16[1,104,512]{2,1,0:T(8,128)(2,1)S(1)} %reshape.334), channel_id=1, source_target_pairs={{0,24},{4,28},{8,16},{12,20},{16,8},{20,12},{24,0},{28,4},{1,25},{... | collective-permute-start | bytes 319496 | tf_op jit(solution)/shard_map/ppermute | solution.py:642
  16.7 5.9 %collective-permute-done = f16[1,104,512]{2,1,0:T(8,128)(2,1)S(1)} collective-permute-done((f16[1,104,512]{2,1,0:T(8,128)(2,1)S(1)}, f16[1,104,512]{2,1,0:T(8,128)(2,1)S(1)}, u32[]{:S(2)}, u32[]{:S(2)}) %collective-permute-start) | collective-permute-done | bytes 106528 | tf_op jit(solution)/shard_map/ppermute | solution.py:642
  22.7 2.2 %collective-permute-done.1 = f16[1,104,512]{2,1,0:T(8,128)(2,1)S(1)} collective-permute-done((f16[1,104,512]{2,1,0:T(8,128)(2,1)S(1)}, f16[1,104,512]{2,1,0:T(8,128)(2,1)S(1)}, u32[]{:S(2)}, u32[]{:S(2)}) %collective-permute-start.1) | collective-permute-done | bytes 106528 | tf_op jit(solution)/shard_map/ppermute | solution.py:642
  25.0 1.3 collective-permute-start.3
  27.2 1.6 copy.60.w_qkv
  31.0 4.1 %collective-permute-done.3 = f16[4,104,512]{2,1,0:T(8,128)(2,1)} collective-permute-done((f16[4,104,512]{2,1,0:T(8,128)(2,1)S(1)}, f16[4,104,512]{2,1,0:T(8,128)(2,1)}, u32[]{:S(2)}, u32[]{:S(2)}) %collective-permute-start.3) | collective-permute-done | bytes 426016 | tf_op jit(solution)/shard_map/ppermute | solution.py:642
  35.1 1.1 convert_element_type.166.far
  36.2 5.3 %fetch.1 = (bf16[2,1104,128]{2,1,0:T(8,128)(2,1)S(1)}, f32[8,128]{1,0:T(8,128)S(1)}) custom-call(s32[2200]{0:T(1024)S(1)} %reshape.331.ids, f32[4,104,512]{2,1,0:T(8,128)S(1)} %convert_element_type.165.near, f32[4,104,512]{2,1,0:T(8,128)S(1)} %convert_element_type.166.far, s32[2,1104]{1,0:T(2,128)S(1)} %pad.28.labels), custom_call_target="tpu_custom_call" | custom-call | flops 6000000000 | bytes 1000000 | tf_op jit(solution)/shard_map/fetch/pallas_call | solution.py:117
  42.3 59.4 %forward.1 = (bf16[2,4,1104,384]{3,2,1,0:T(8,128)(2,1)}, bf16[2,4,1104,1024]{3,2,1,0:T(8,128)(2,1)}, bf16[8800,128]{1,0:T(8,128)(2,1)}, f32[2,1104,128]{2,1,0:T(...) custom-call(s32[3]{0:T(128)} %pad_add_fusion.1.place, ...), custom_call_target="tpu_custom_call" | custom-call | flops 60000002048 | bytes 1000000 | tf_op jit(solution)/shard_map/forward/pallas_call | solution.py:347
  101.7 2.3 %collective-permute-start.4 = (bf16[16,80,512]{2,1,0:T(8,128)(2,1)}, bf16[16,80,512]{2,1,0:T(8,128)(2,1)S(1)}, u32[]{:S(2)}, u32[]{:S(2)}) collective-permute-start(bf16[16,80,512]{2,1,0:T(8,128)(2,1)} %get-tuple-element.81), channel_id=1, source_target_pairs={{0,1},{1,0},{2,3},{3,2},{4,5},{5,4},{6,7},{7,6},{8,9},{9,8},{10,11... | collective-permute-start | bytes 3932168 | tf_op jit(solution)/shard_map/ppermute | solution.py:642
  105.0 1.9 collective-permute-done.4
  106.9 1.3 add_convert_fusion
  108.3 1.6 collective-permute-start.5
  109.9 1.2 add_convert_fusion.1
  111.1 1.3 collective-permute-start.8
  112.4 1.6 copy-done.2
  114.0 14.2 %score_grads.2 = (f32[2,128,384]{2,1,0:T(8,128)S(1)}, f32[2,1104,128]{2,1,0:T(8,128)S(1)}) custom-call(s32[3]{0:T(128)S(1)} %copy-done, bf16[2,4,1104,1024]{3,2,1,0:T(8,128)(2,1)} %get-tuple-element.78.e, bf16[2,4,1104,384]{3,2,1,0:T(8,128)(2,1)S(1)} %copy-done.1, bf16[2,1104,512]{2,1,0:T(8,128)(2,1)S(1)} %copy-done.2, bf16[2,1104,128]{2,1,0:T(8,128)(2,1)S(1)} %copy-done.5, ...), custom_call_target="tpu_custom_call" | custom-call | flops 16000000000 | bytes 1000000 | tf_op jit(solution)/shard_map/score_grads/pallas_call | solution.py:463
  128.9 14.6 %score_grads.3 = (bf16[16,16,512]{2,1,0:T(8,128)(2,1)S(1)}, bf16[16,16,512]{2,1,0:T(8,128)(2,1)S(1)}, f32[2,1104,128]{2,1,0:T(8,128)S(1)}) custom-call(s32[3]{0:T(128)S(1)} %copy-done, bf16[2,4,1104,1024]{3,2,1,0:T(8,128)(2,1)} %get-tuple-element.78.e, bf16[2,4,1104,384]{3,2,1,0:T(8,128)(2,1)S(1)} %copy-done.1, bf16[2,1104,512]{2,1,0:T(8,128)(2,1)S(1)} %copy-done.3, ...), custom_call_target="tpu_custom_call" | custom-call | flops 16000000000 | bytes 1000000 | tf_op jit(solution)/shard_map/score_grads/pallas_call | solution.py:463
  143.5 5.2 %spread.1 = (bf16[4,4,25,512]{3,2,1,0:T(8,128)(2,1)S(1)}, bf16[4,4,25,512]{3,2,1,0:T(8,128)(2,1)S(1)}) custom-call(s32[2200]{0:T(1024)S(1)} %reshape.331.ids, f32[2,1104,128]{2,1,0:T(8,128)S(1)} %get-tuple-element.92.rows), custom_call_target="tpu_custom_call" | custom-call | flops 7000000000 | bytes 1000000 | tf_op jit(solution)/shard_map/spread/pallas_call | solution.py:523
  148.7 1.5 collective-permute-start.6
  150.4 2.3 %collective-permute-start.21 = (bf16[80,512]{1,0:T(8,128)(2,1)S(1)}, bf16[80,512]{1,0:T(8,128)(2,1)S(1)}, u32[]{:S(2)}, u32[]{:S(2)}) collective-permute-start(bf16[80,512]{1,0:T(8,128)(2,1)S(1)} %get-tuple-element.134), channel_id=1, source_target_pairs={{0,16},{4,20},{8,24},{12,28},{16,0},{20,4},{24,8},{28,12},{1,17},{... | collective-permute-start | bytes 245768 | tf_op jit(solution)/shard_map/ppermute | solution.py:642
  152.7 1.3 collective-permute-start.22
  154.0 1.5 collective-permute-start.10
  155.5 1.2 collective-permute-start.12
  156.7 1.1 collective-permute-done.22
  157.9 3.2 %collective-permute-start.25 = (bf16[80,512]{1,0:T(8,128)(2,1)S(1)}, bf16[80,512]{1,0:T(8,128)(2,1)S(1)}, u32[]{:S(2)}, u32[]{:S(2)}) collective-permute-start(bf16[80,512]{1,0:T(8,128)(2,1)S(1)} %fusion.13), channel_id=1, source_target_pairs={{0,24},{4,28},{8,16},{12,20},{16,8},{20,12},{24,0},{28,4},{1,25},{... | collective-permute-start | bytes 245768 | tf_op jit(solution)/shard_map/ppermute | solution.py:642
  162.3 1.3 collective-permute-start.11
  163.6 5.1 %collective-permute-done.24 = bf16[80,512]{1,0:T(8,128)(2,1)S(1)} collective-permute-done((bf16[80,512]{1,0:T(8,128)(2,1)S(1)}, bf16[80,512]{1,0:T(8,128)(2,1)S(1)}, u32[]{:S(2)}, u32[]{:S(2)}) %collective-permute-start.24) | collective-permute-done | bytes 81952 | tf_op jit(solution)/shard_map/ppermute | solution.py:642
  168.8 2.1 collective-permute-start.29
  170.9 1.2 collective-permute-start.26
  173.3 1.3 collective-permute-start.30
  174.6 1.2 collective-permute-done.26
  177.0 1.9 collective-permute-start.17
  178.9 2.7 %collective-permute-start.13 = (bf16[4,25,512]{2,1,0:T(8,128)(2,1)S(1)}, bf16[4,25,512]{2,1,0:T(8,128)(2,1)S(1)}, u32[]{:S(2)}, u32[]{:S(2)}) collective-permute-start(bf16[4,25,512]{2,1,0:T(8,128)(2,1)S(1)} %get-tuple-element.130), channel_id=1, source_target_pairs={{0,8},{4,12},{8,0},{12,4},{16,24},{20,28},{24,16},{28,20},{1,9},{5... | collective-permute-start | bytes 307208 | tf_op jit(solution)/shard_map/ppermute | solution.py:642
  181.6 1.2 collective-permute-start.14
  182.9 12.3 %collective-permute-start.31 = (bf16[16,32,512]{2,1,0:T(8,128)(2,1)S(1)}, bf16[16,32,512]{2,1,0:T(8,128)(2,1)S(1)}, u32[]{:S(2)}, u32[]{:S(2)}) collective-permute-start(bf16[16,32,512]{2,1,0:T(8,128)(2,1)S(1)} %pad_maximum_fusion.5.near_q), channel_id=1, source_target_pairs={{0,1},{1,0},{2,3},{3,2},{4,5},{5,4},{6,7},{7,6},{8,9},{9,8},{10,11... | collective-permute-start | bytes 1572872 | tf_op jit(solution)/shard_map/ppermute | solution.py:642
  195.2 1.7 collective-permute-start.18
  197.6 5.5 %all-to-all-start.1 = ((bf16[4,25,512]{2,1,0:T(8,128)(2,1)}), bf16[4,25,512]{2,1,0:T(8,128)(2,1)}, u32[]{:S(2)}, u32[]{:S(2)}) async-start(bf16[4,25,512]{2,1,0:T(8,128)(2,1)} %fusion.10), calls=%async_computation.1 | async-start | bytes 262144 | tf_op jit(solution)/shard_map/all_to_all | solution.py:650
  203.3 3.5 %all-to-all-done.1 = bf16[4,25,512]{2,1,0:T(8,128)(2,1)} async-done(((bf16[4,25,512]{2,1,0:T(8,128)(2,1)}), bf16[4,25,512]{2,1,0:T(8,128)(2,1)}, u32[]{:S(2)}, u32[]{:S(2)}) %all-to-all-start.1) | async-done | bytes 102432 | tf_op jit(solution)/shard_map/all_to_all | solution.py:650
  208.1 1.1 pad_maximum_fusion.2.near
  209.2 1.1 collective-permute-start.28
  210.3 3.2 %finish_tail.1 = (f32[512,512]{1,0:T(8,128)}, f32[512,512]{1,0:T(8,128)}, f32[512,512]{1,0:T(8,128)}, f32[100,512]{1,0:T(8,128)}, f32[1,512]{1,0:T(1,128)}, /*in...) custom-call(s32[3]{0:T(128)S(1)} %copy-done, ...), custom_call_target="tpu_custom_call" | custom-call | flops 5000000000 | bytes 1000000 | tf_op jit(solution)/shard_map/finish_tail/pallas_call | solution.py:621
  213.5 1.1 fusion.25
  215.4 3.3 %finish.1 = (f32[512,512]{1,0:T(8,128)}, f32[512,1024]{1,0:T(8,128)}, f32[1024,512]{1,0:T(8,128)}) custom-call(s32[3]{0:T(128)S(1)} %copy-done, bf16[16,48,512]{2,1,0:T(8,128)(2,1)S(1)} %pad_maximum_fusion.2.near, bf16[16,48,512]{2,1,0:T(8,128)(2,1)S(1)} %collective-permute-done.28.far, bf16[16,32,512]{2,1,0:T(8,128)(2,1)S(1)} %pad_maximum_fusion.5.near_q, ...), custom_call_target="tpu_custom_call" | custom-call | flops 5000000000 | bytes 1000000 | tf_op jit(solution)/shard_map/finish/pallas_call | solution.py:563
  (151 shorter events, 16.8 us)
Async XLA Ops:
  0.7 7.8 %copy-start.18 = (f32[512]{0:T(512)S(1)}, f32[512]{0:T(512)}, u32[]{:S(2)}) copy-start(f32[512]{0:T(512)} %param.33) | copy-start | bytes 6148
  0.7 7.8 %copy-start.19 = (f32[512]{0:T(512)S(1)}, f32[512]{0:T(512)}, u32[]{:S(2)}) copy-start(f32[512]{0:T(512)} %param.30) | copy-start | bytes 6148
  0.7 8.5 %copy-start.16 = (s32[2,1100]{1,0:T(2,128)S(1)}, s32[2,1100]{1,0:T(2,128)}, u32[]{:S(2)}) copy-start(s32[2,1100]{1,0:T(2,128)} %param.44) | copy-start | bytes 26404
  0.7 8.6 %copy-start.17 = (s32[2,1000]{1,0:T(2,128)S(1)}, s32[2,1000]{1,0:T(2,128)}, u32[]{:S(2)}) copy-start(s32[2,1000]{1,0:T(2,128)} %param.45) | copy-start | bytes 24004
  0.7 8.6 %copy-start.15 = (bf16[100,512]{1,0:T(8,128)(2,1)S(1)}, bf16[100,512]{1,0:T(8,128)(2,1)}, u32[]{:S(2)}) copy-start(bf16[100,512]{1,0:T(8,128)(2,1)} %param.26) | copy-start | bytes 307204
  0.7 8.7 %copy-start.11 = (bf16[512,512]{1,0:T(8,128)(2,1)S(1)}, bf16[512,512]{1,0:T(8,128)(2,1)}, u32[]{:S(2)}) copy-start(bf16[512,512]{1,0:T(8,128)(2,1)} %param.29) | copy-start | bytes 1572868
  3.1 6.6 %copy-start.12 = (bf16[512,512]{1,0:T(8,128)(2,1)S(1)}, bf16[512,512]{1,0:T(8,128)(2,1)}, u32[]{:S(2)}) copy-start(bf16[512,512]{1,0:T(8,128)(2,1)} %param.31) | copy-start | bytes 1572868
  4.1 8.2 %all-to-all-start = ((f16[4,26,512]{2,1,0:T(8,128)(2,1)}), f16[4,26,512]{2,1,0:T(8,128)(2,1)S(1)}, u32[]{:S(2)}, u32[]{:S(2)}) async-start(f16[4,26,512]{2,1,0:T(8,128)(2,1)} %pad_maximum_fusion.12), calls=%async_computation | async-start | bytes 262144 | tf_op jit(solution)/shard_map/all_to_all | solution.py:650
  12.4 12.5 %collective-permute-start.2 = (f16[1,104,512]{2,1,0:T(8,128)(2,1)S(1)}, f16[1,104,512]{2,1,0:T(8,128)(2,1)S(1)}, u32[]{:S(2)}, u32[]{:S(2)}) collective-permute-start(f16[1,104,512]{2,1,0:T(8,128)(2,1)S(1)} %reshape.334), channel_id=1, source_target_pairs={{0,24},{4,28},{8,16},{12,20},{16,8},{20,12},{24,0},{28,4},{1,25},{... | collective-permute-start | bytes 319496 | tf_op jit(solution)/shard_map/ppermute | solution.py:642
  16.3 8.6 %collective-permute-start.1 = (f16[1,104,512]{2,1,0:T(8,128)(2,1)S(1)}, f16[1,104,512]{2,1,0:T(8,128)(2,1)S(1)}, u32[]{:S(2)}, u32[]{:S(2)}) collective-permute-start(f16[1,104,512]{2,1,0:T(8,128)(2,1)S(1)} %reshape.334), channel_id=1, source_target_pairs={{0,16},{4,20},{8,24},{12,28},{16,0},{20,4},{24,8},{28,12},{1,17},{... | collective-permute-start | bytes 319496 | tf_op jit(solution)/shard_map/ppermute | solution.py:642
  16.3 6.3 %collective-permute-start = (f16[1,104,512]{2,1,0:T(8,128)(2,1)S(1)}, f16[1,104,512]{2,1,0:T(8,128)(2,1)S(1)}, u32[]{:S(2)}, u32[]{:S(2)}) collective-permute-start(f16[1,104,512]{2,1,0:T(8,128)(2,1)S(1)} %reshape.334), channel_id=1, source_target_pairs={{0,8},{4,12},{8,0},{12,4},{16,24},{20,28},{24,16},{28,20},{1,9},{5... | collective-permute-start | bytes 319496 | tf_op jit(solution)/shard_map/ppermute | solution.py:642
  25.0 10.1 %collective-permute-start.3 = (f16[4,104,512]{2,1,0:T(8,128)(2,1)S(1)}, f16[4,104,512]{2,1,0:T(8,128)(2,1)}, u32[]{:S(2)}, u32[]{:S(2)}) collective-permute-start(f16[4,104,512]{2,1,0:T(8,128)(2,1)S(1)} %constant_dynamic-update-slice_fusion), channel_id=1, source_target_pairs={{0,4},{4,0},{8,12},{12,8},{16,20},{20,16},{24,28},{28,24},{1,5},{5... | collective-permute-start | bytes 1277960 | tf_op jit(solution)/shard_map/ppermute | solution.py:642
  42.3 61.7 %copy-start.20 = (f32[512]{0:T(512)S(1)}, f32[512]{0:T(512)}, u32[]{:S(2)}) copy-start(f32[512]{0:T(512)} %param.27) | copy-start | bytes 6148
  101.7 5.2 %collective-permute-start.4 = (bf16[16,80,512]{2,1,0:T(8,128)(2,1)}, bf16[16,80,512]{2,1,0:T(8,128)(2,1)S(1)}, u32[]{:S(2)}, u32[]{:S(2)}) collective-permute-start(bf16[16,80,512]{2,1,0:T(8,128)(2,1)} %get-tuple-element.81), channel_id=1, source_target_pairs={{0,1},{1,0},{2,3},{3,2},{4,5},{5,4},{6,7},{7,6},{8,9},{9,8},{10,11... | collective-permute-start | bytes 3932168 | tf_op jit(solution)/shard_map/ppermute | solution.py:642
  104.3 8.1 %copy-start.1 = (bf16[2,4,1104,384]{3,2,1,0:T(8,128)(2,1)S(1)}, bf16[2,4,1104,384]{3,2,1,0:T(8,128)(2,1)}, u32[]{:S(2)}) copy-start(bf16[2,4,1104,384]{3,2,1,0:T(8,128)(2,1)} %get-tuple-element.79.qkv) | copy-start | bytes 20348932
  108.3 4.1 %copy-start = (s32[3]{0:T(128)S(1)}, s32[3]{0:T(128)}, u32[]{:S(2)}) copy-start(s32[3]{0:T(128)} %pad_add_fusion.1.place) | copy-start | bytes 40
  108.3 4.1 %copy-start.5 = (bf16[2,1104,128]{2,1,0:T(8,128)(2,1)S(1)}, bf16[2,1104,128]{2,1,0:T(8,128)(2,1)}, u32[]{:S(2)}) copy-start(bf16[2,1104,128]{2,1,0:T(8,128)(2,1)} %copy-done.4) | copy-start | bytes 1695748
  108.3 20.2 %collective-permute-start.5 = (bf16[8,48,512]{2,1,0:T(8,128)(2,1)S(1)}, bf16[8,48,512]{2,1,0:T(8,128)(2,1)S(1)}, u32[]{:S(2)}, u32[]{:S(2)}) collective-permute-start(bf16[8,48,512]{2,1,0:T(8,128)(2,1)S(1)} %get-tuple-element.126), channel_id=1, source_target_pairs={{0,2},{1,3},{2,0},{3,1},{4,6},{5,7},{6,4},{7,5},{8,10},{9,11},{10,... | collective-permute-start | bytes 1179656 | tf_op jit(solution)/shard_map/ppermute | solution.py:642
  111.1 17.2 %collective-permute-start.8 = (bf16[8,32,512]{2,1,0:T(8,128)(2,1)S(1)}, bf16[8,32,512]{2,1,0:T(8,128)(2,1)S(1)}, u32[]{:S(2)}, u32[]{:S(2)}) collective-permute-start(bf16[8,32,512]{2,1,0:T(8,128)(2,1)S(1)} %get-tuple-element.124), channel_id=1, source_target_pairs={{0,4},{4,0},{8,12},{12,8},{16,20},{20,16},{24,28},{28,24},{1,5},{5... | collective-permute-start | bytes 786440 | tf_op jit(solution)/shard_map/ppermute | solution.py:642
  114.0 14.8 %copy-start.3 = (bf16[2,1104,512]{2,1,0:T(8,128)(2,1)S(1)}, bf16[2,1104,512]{2,1,0:T(8,128)(2,1)}, u32[]{:S(2)}) copy-start(bf16[2,1104,512]{2,1,0:T(8,128)(2,1)} %get-tuple-element.84.back) | copy-start | bytes 6782980
  114.0 14.8 %copy-start.7 = (f32[128,512]{1,0:T(8,128)S(1)}, f32[128,512]{1,0:T(8,128)}, u32[]{:S(2)}) copy-start(f32[128,512]{1,0:T(8,128)} %get-tuple-element.88.refs_1_) | copy-start | bytes 786436
  128.3 21.8 %collective-permute-start.9 = (bf16[4,32,512]{2,1,0:T(8,128)(2,1)S(1)}, bf16[4,32,512]{2,1,0:T(8,128)(2,1)S(1)}, u32[]{:S(2)}, u32[]{:S(2)}) collective-permute-start(bf16[4,32,512]{2,1,0:T(8,128)(2,1)S(1)} %fusion.4), channel_id=1, source_target_pairs={{0,2},{1,3},{2,0},{3,1},{4,6},{5,7},{6,4},{7,5},{8,10},{9,11},{10,... | collective-permute-start | bytes 393224 | tf_op jit(solution)/shard_map/ppermute | solution.py:642
  128.6 21.6 %collective-permute-start.7 = (bf16[4,48,512]{2,1,0:T(8,128)(2,1)S(1)}, bf16[4,48,512]{2,1,0:T(8,128)(2,1)S(1)}, u32[]{:S(2)}, u32[]{:S(2)}) collective-permute-start(bf16[4,48,512]{2,1,0:T(8,128)(2,1)S(1)} %fusion.3), channel_id=1, source_target_pairs={{0,4},{4,0},{8,12},{12,8},{16,20},{20,16},{24,28},{28,24},{1,5},{5... | collective-permute-start | bytes 589832 | tf_op jit(solution)/shard_map/ppermute | solution.py:642
  148.7 5.3 %collective-permute-start.6 = (bf16[16,16,512]{2,1,0:T(8,128)(2,1)S(1)}, bf16[16,16,512]{2,1,0:T(8,128)(2,1)S(1)}, u32[]{:S(2)}, u32[]{:S(2)}) collective-permute-start(bf16[16,16,512]{2,1,0:T(8,128)(2,1)S(1)} %get-tuple-element.90), channel_id=1, source_target_pairs={{0,1},{1,0},{2,3},{3,2},{4,5},{5,4},{6,7},{7,6},{8,9},{9,8},{10,11... | collective-permute-start | bytes 786440 | tf_op jit(solution)/shard_map/ppermute | solution.py:642
  150.3 6.4 %collective-permute-start.20 = (bf16[80,512]{1,0:T(8,128)(2,1)S(1)}, bf16[80,512]{1,0:T(8,128)(2,1)S(1)}, u32[]{:S(2)}, u32[]{:S(2)}) collective-permute-start(bf16[80,512]{1,0:T(8,128)(2,1)S(1)} %get-tuple-element.133), channel_id=1, source_target_pairs={{0,8},{4,12},{8,0},{12,4},{16,24},{20,28},{24,16},{28,20},{1,9},{5... | collective-permute-start | bytes 245768 | tf_op jit(solution)/shard_map/ppermute | solution.py:642
  150.4 6.3 %collective-permute-start.21 = (bf16[80,512]{1,0:T(8,128)(2,1)S(1)}, bf16[80,512]{1,0:T(8,128)(2,1)S(1)}, u32[]{:S(2)}, u32[]{:S(2)}) collective-permute-start(bf16[80,512]{1,0:T(8,128)(2,1)S(1)} %get-tuple-element.134), channel_id=1, source_target_pairs={{0,16},{4,20},{8,24},{12,28},{16,0},{20,4},{24,8},{28,12},{1,17},{... | collective-permute-start | bytes 245768 | tf_op jit(solution)/shard_map/ppermute | solution.py:642
  152.7 5.2 %collective-permute-start.22 = (bf16[80,512]{1,0:T(8,128)(2,1)S(1)}, bf16[80,512]{1,0:T(8,128)(2,1)S(1)}, u32[]{:S(2)}, u32[]{:S(2)}) collective-permute-start(bf16[80,512]{1,0:T(8,128)(2,1)S(1)} %get-tuple-element.135), channel_id=1, source_target_pairs={{0,24},{4,28},{8,16},{12,20},{16,8},{20,12},{24,0},{28,4},{1,25},{... | collective-permute-start | bytes 245768 | tf_op jit(solution)/shard_map/ppermute | solution.py:642
  154.0 8.3 %collective-permute-start.10 = (bf16[8,16,512]{2,1,0:T(8,128)(2,1)S(1)}, bf16[8,16,512]{2,1,0:T(8,128)(2,1)S(1)}, u32[]{:S(2)}, u32[]{:S(2)}) collective-permute-start(bf16[8,16,512]{2,1,0:T(8,128)(2,1)S(1)} %add_convert_fusion.6), channel_id=1, source_target_pairs={{0,2},{1,3},{2,0},{3,1},{4,6},{5,7},{6,4},{7,5},{8,10},{9,11},{10,... | collective-permute-start | bytes 393224 | tf_op jit(solution)/shard_map/ppermute | solution.py:642
  155.5 16.7 %collective-permute-start.12 = (bf16[4,4,25,512]{3,2,1,0:T(8,128)(2,1)S(1)}, bf16[4,4,25,512]{3,2,1,0:T(8,128)(2,1)S(1)}, u32[]{:S(2)}, u32[]{:S(2)}) collective-permute-start(bf16[4,4,25,512]{3,2,1,0:T(8,128)(2,1)S(1)} %get-tuple-element.97), channel_id=1, source_target_pairs={{0,4},{4,0},{8,12},{12,8},{16,20},{20,16},{24,28},{28,24},{1,5},{5... | collective-permute-start | bytes 1228808 | tf_op jit(solution)/shard_map/ppermute | solution.py:642
  157.9 5.7 %collective-permute-start.25 = (bf16[80,512]{1,0:T(8,128)(2,1)S(1)}, bf16[80,512]{1,0:T(8,128)(2,1)S(1)}, u32[]{:S(2)}, u32[]{:S(2)}) collective-permute-start(bf16[80,512]{1,0:T(8,128)(2,1)S(1)} %fusion.13), channel_id=1, source_target_pairs={{0,24},{4,28},{8,16},{12,20},{16,8},{20,12},{24,0},{28,4},{1,25},{... | collective-permute-start | bytes 245768 | tf_op jit(solution)/shard_map/ppermute | solution.py:642
  161.1 7.6 %collective-permute-start.24 = (bf16[80,512]{1,0:T(8,128)(2,1)S(1)}, bf16[80,512]{1,0:T(8,128)(2,1)S(1)}, u32[]{:S(2)}, u32[]{:S(2)}) collective-permute-start(bf16[80,512]{1,0:T(8,128)(2,1)S(1)} %fusion.13), channel_id=1, source_target_pairs={{0,16},{4,20},{8,24},{12,28},{16,0},{20,4},{24,8},{28,12},{1,17},{... | collective-permute-start | bytes 245768 | tf_op jit(solution)/shard_map/ppermute | solution.py:642
  162.2 6.5 %collective-permute-start.23 = (bf16[80,512]{1,0:T(8,128)(2,1)S(1)}, bf16[80,512]{1,0:T(8,128)(2,1)S(1)}, u32[]{:S(2)}, u32[]{:S(2)}) collective-permute-start(bf16[80,512]{1,0:T(8,128)(2,1)S(1)} %fusion.13), channel_id=1, source_target_pairs={{0,8},{4,12},{8,0},{12,4},{16,24},{20,28},{24,16},{28,20},{1,9},{5... | collective-permute-start | bytes 245768 | tf_op jit(solution)/shard_map/ppermute | solution.py:642
  162.3 9.8 %collective-permute-start.11 = (bf16[8,16,512]{2,1,0:T(8,128)(2,1)S(1)}, bf16[8,16,512]{2,1,0:T(8,128)(2,1)S(1)}, u32[]{:S(2)}, u32[]{:S(2)}) collective-permute-start(bf16[8,16,512]{2,1,0:T(8,128)(2,1)S(1)} %add_convert_fusion.5), channel_id=1, source_target_pairs={{0,4},{4,0},{8,12},{12,8},{16,20},{20,16},{24,28},{28,24},{1,5},{5... | collective-permute-start | bytes 393224 | tf_op jit(solution)/shard_map/ppermute | solution.py:642
  168.8 4.5 %collective-permute-start.29 = (bf16[4,32,512]{2,1,0:T(8,128)(2,1)S(1)}, bf16[4,32,512]{2,1,0:T(8,128)(2,1)S(1)}, u32[]{:S(2)}, u32[]{:S(2)}) collective-permute-start(bf16[4,32,512]{2,1,0:T(8,128)(2,1)S(1)} %pad_maximum_fusion.11), channel_id=1, source_target_pairs={{0,2},{1,3},{2,0},{3,1},{4,6},{5,7},{6,4},{7,5},{8,10},{9,11},{10,... | collective-permute-start | bytes 393224 | tf_op jit(solution)/shard_map/ppermute | solution.py:642
  170.9 4.9 %collective-permute-start.26 = (bf16[4,48,512]{2,1,0:T(8,128)(2,1)S(1)}, bf16[4,48,512]{2,1,0:T(8,128)(2,1)S(1)}, u32[]{:S(2)}, u32[]{:S(2)}) collective-permute-start(bf16[4,48,512]{2,1,0:T(8,128)(2,1)S(1)} %slice.170), channel_id=1, source_target_pairs={{0,4},{4,0},{8,12},{12,8},{16,20},{20,16},{24,28},{28,24},{1,5},{5... | collective-permute-start | bytes 589832 | tf_op jit(solution)/shard_map/ppermute | solution.py:642
  172.3 4.6 %collective-permute-start.16 = (bf16[8,16,512]{2,1,0:T(8,128)(2,1)S(1)}, bf16[8,16,512]{2,1,0:T(8,128)(2,1)S(1)}, u32[]{:S(2)}, u32[]{:S(2)}) collective-permute-start(bf16[8,16,512]{2,1,0:T(8,128)(2,1)S(1)} %add_convert_fusion.4), channel_id=1, source_target_pairs={{0,8},{4,12},{8,0},{12,4},{16,24},{20,28},{24,16},{28,20},{1,9},{5... | collective-permute-start | bytes 393224 | tf_op jit(solution)/shard_map/ppermute | solution.py:642
  173.3 8.4 %collective-permute-start.30 = (bf16[8,32,512]{2,1,0:T(8,128)(2,1)S(1)}, bf16[8,32,512]{2,1,0:T(8,128)(2,1)S(1)}, u32[]{:S(2)}, u32[]{:S(2)}) collective-permute-start(bf16[8,32,512]{2,1,0:T(8,128)(2,1)S(1)} %pad_maximum_fusion.10), channel_id=1, source_target_pairs={{0,4},{4,0},{8,12},{12,8},{16,20},{20,16},{24,28},{28,24},{1,5},{5... | collective-permute-start | bytes 786440 | tf_op jit(solution)/shard_map/ppermute | solution.py:642
  176.6 31.5 %collective-permute-start.27 = (bf16[8,48,512]{2,1,0:T(8,128)(2,1)}, bf16[8,48,512]{2,1,0:T(8,128)(2,1)}, u32[]{:S(2)}, u32[]{:S(2)}) collective-permute-start(bf16[8,48,512]{2,1,0:T(8,128)(2,1)} %pad_maximum_fusion.6), channel_id=1, source_target_pairs={{0,2},{1,3},{2,0},{3,1},{4,6},{5,7},{6,4},{7,5},{8,10},{9,11},{10,... | collective-permute-start | bytes 1179656 | tf_op jit(solution)/shard_map/ppermute | solution.py:642
  177.0 5.9 %collective-permute-start.17 = (bf16[8,16,512]{2,1,0:T(8,128)(2,1)S(1)}, bf16[8,16,512]{2,1,0:T(8,128)(2,1)S(1)}, u32[]{:S(2)}, u32[]{:S(2)}) collective-permute-start(bf16[8,16,512]{2,1,0:T(8,128)(2,1)S(1)} %add_convert_fusion.3), channel_id=1, source_target_pairs={{0,16},{4,20},{8,24},{12,28},{16,0},{20,4},{24,8},{28,12},{1,17},{... | collective-permute-start | bytes 393224 | tf_op jit(solution)/shard_map/ppermute | solution.py:642
  178.9 16.3 %collective-permute-start.13 = (bf16[4,25,512]{2,1,0:T(8,128)(2,1)S(1)}, bf16[4,25,512]{2,1,0:T(8,128)(2,1)S(1)}, u32[]{:S(2)}, u32[]{:S(2)}) collective-permute-start(bf16[4,25,512]{2,1,0:T(8,128)(2,1)S(1)} %get-tuple-element.130), channel_id=1, source_target_pairs={{0,8},{4,12},{8,0},{12,4},{16,24},{20,28},{24,16},{28,20},{1,9},{5... | collective-permute-start | bytes 307208 | tf_op jit(solution)/shard_map/ppermute | solution.py:642
  181.5 15.4 %collective-permute-start.15 = (bf16[4,25,512]{2,1,0:T(8,128)(2,1)S(1)}, bf16[4,25,512]{2,1,0:T(8,128)(2,1)S(1)}, u32[]{:S(2)}, u32[]{:S(2)}) collective-permute-start(bf16[4,25,512]{2,1,0:T(8,128)(2,1)S(1)} %get-tuple-element.131), channel_id=1, source_target_pairs={{0,24},{4,28},{8,16},{12,20},{16,8},{20,12},{24,0},{28,4},{1,25},{... | collective-permute-start | bytes 307208 | tf_op jit(solution)/shard_map/ppermute | solution.py:642
  181.6 15.3 %collective-permute-start.14 = (bf16[4,25,512]{2,1,0:T(8,128)(2,1)S(1)}, bf16[4,25,512]{2,1,0:T(8,128)(2,1)S(1)}, u32[]{:S(2)}, u32[]{:S(2)}) collective-permute-start(bf16[4,25,512]{2,1,0:T(8,128)(2,1)S(1)} %get-tuple-element.132), channel_id=1, source_target_pairs={{0,16},{4,20},{8,24},{12,28},{16,0},{20,4},{24,8},{28,12},{1,17},{... | collective-permute-start | bytes 307208 | tf_op jit(solution)/shard_map/ppermute | solution.py:642
  182.9 32.5 %collective-permute-start.31 = (bf16[16,32,512]{2,1,0:T(8,128)(2,1)S(1)}, bf16[16,32,512]{2,1,0:T(8,128)(2,1)S(1)}, u32[]{:S(2)}, u32[]{:S(2)}) collective-permute-start(bf16[16,32,512]{2,1,0:T(8,128)(2,1)S(1)} %pad_maximum_fusion.5.near_q), channel_id=1, source_target_pairs={{0,1},{1,0},{2,3},{3,2},{4,5},{5,4},{6,7},{7,6},{8,9},{9,8},{10,11... | collective-permute-start | bytes 1572872 | tf_op jit(solution)/shard_map/ppermute | solution.py:642
  195.2 7.9 %collective-permute-start.18 = (bf16[8,16,512]{2,1,0:T(8,128)(2,1)S(1)}, bf16[8,16,512]{2,1,0:T(8,128)(2,1)S(1)}, u32[]{:S(2)}, u32[]{:S(2)}) collective-permute-start(bf16[8,16,512]{2,1,0:T(8,128)(2,1)S(1)} %add_convert_fusion.2), channel_id=1, source_target_pairs={{0,2},{1,3},{2,0},{3,1},{4,6},{5,7},{6,4},{7,5},{8,10},{9,11},{10,... | collective-permute-start | bytes 393224 | tf_op jit(solution)/shard_map/ppermute | solution.py:642
  197.6 9.2 %all-to-all-start.1 = ((bf16[4,25,512]{2,1,0:T(8,128)(2,1)}), bf16[4,25,512]{2,1,0:T(8,128)(2,1)}, u32[]{:S(2)}, u32[]{:S(2)}) async-start(bf16[4,25,512]{2,1,0:T(8,128)(2,1)} %fusion.10), calls=%async_computation.1 | async-start | bytes 262144 | tf_op jit(solution)/shard_map/all_to_all | solution.py:650
  203.1 7.1 %collective-permute-start.19 = (bf16[16,16,512]{2,1,0:T(8,128)(2,1)S(1)}, bf16[16,16,512]{2,1,0:T(8,128)(2,1)S(1)}, u32[]{:S(2)}, u32[]{:S(2)}) collective-permute-start(bf16[16,16,512]{2,1,0:T(8,128)(2,1)S(1)} %pad_maximum_fusion.9.near), channel_id=1, source_target_pairs={{0,1},{1,0},{2,3},{3,2},{4,5},{5,4},{6,7},{7,6},{8,9},{9,8},{10,11... | collective-permute-start | bytes 786440 | tf_op jit(solution)/shard_map/ppermute | solution.py:642
  209.2 5.4 %copy-start.8 = (f32[2048,25]{0,1:T(8,128)S(1)}, f32[2048,25]{0,1:T(8,128)}, u32[]{:S(2)}) copy-start(f32[2048,25]{0,1:T(8,128)} %param.25) | copy-start | bytes 614404
  209.2 6.2 %collective-permute-start.28 = (bf16[16,48,512]{2,1,0:T(8,128)(2,1)S(1)}, bf16[16,48,512]{2,1,0:T(8,128)(2,1)S(1)}, u32[]{:S(2)}, u32[]{:S(2)}) collective-permute-start(bf16[16,48,512]{2,1,0:T(8,128)(2,1)S(1)} %pad_maximum_fusion.2.near), channel_id=1, source_target_pairs={{0,1},{1,0},{2,3},{3,2},{4,5},{5,4},{6,7},{7,6},{8,9},{9,8},{10,11... | collective-permute-start | bytes 2359304 | tf_op jit(solution)/shard_map/ppermute | solution.py:642
  (7 other events, 11.6 us)

commit v5 on v4

--- a/solution.py
+++ b/solution.py
@@ -787,7 +787,7 @@
     give, near, far = lax.optimization_barrier((give, near, far))
     total = added(keep, swap(give, "feat", 2)).astype(bf16)
     d_table = added(near, swap(far, "rows", 1))
-    total = added(total, swap(total, "rows", 1)).astype(bf16)
+    total = added(total, swap(total, "rows", 2)).astype(bf16)
     total, d_table = lax.optimization_barrier((total, d_table))
     for bit in range(row_count.bit_length() - 2, 2, -1):
         half = d_table.shape[0] // 2
@@ -795,7 +795,7 @@
         total = added(total, swap(total, "rows", 1 << bit)).astype(bf16)
     d_low = d_table.astype(bf16)
     d_own = added(d_table[0], *[swap(d_low[at], "rows", 2 * at) for at in range(1, 4)]).astype(bf16)
-    for bit in (2, 4):
+    for bit in (4, 1):
         total = added(total, swap(total, "rows", bit)).astype(bf16)
     t_near = jnp.concatenate([total, swap(total, "feat", 2)], 0)
     t_far = swap(t_near, "feat", 1)

time: 219 us -> 218 us (level)
  starting transfers between devices: 61 us -> 48.2 us
  waiting for transfers between devices: 25.5 us -> 36.4 us
    ppermute x32, starting transfers between devices: 51.2 us -> 37.9 us  [swap(): return lax.ppermute(value, axis, [(i, i ^ bit) for i in range(size)])]
    ppermute x32, waiting for transfers between devices: 22 us -> 32.6 us  [swap(): return lax.ppermute(value, axis, [(i, i ^ bit) for i in range(size)])]
  transfers between devices with their start and end apart: 34 -> 34, of which waited for: 10 -> 12; matrix products, arithmetic and copies ran while one was open for 8% -> 8% of each run, Pallas kernels for 17% -> 17%
where the time goes in v5:
time: 218 us; the launch traced here: 217 us
  Pallas kernels  105 us (48%)
  starting transfers between devices  48.2 us (22%)
  waiting for transfers between devices  36.4 us (17%)
  other arithmetic  17.5 us (8%)
  local copies, waits for them, and re-layouts  7.64 us (4%)
    pallas_call x1, Pallas kernels, forward(): pl.pallas_call(functools.partial(forward_kernel, blocks, ctx_len, ctx_pad...  59.4 us
    ppermute x32, starting transfers between devices, swap(): return lax.ppermute(value, axis, [(i, i ^ bit) for i in range(size)])  37.9 us
    ppermute x32, waiting for transfers between devices, swap(): return lax.ppermute(value, axis, [(i, i ^ bit) for i in range(size)])  32.6 us
    pallas_call x2, Pallas kernels, score_grads(): pl.pallas_call(functools.partial(scores_kernel, start, last, ctx_pad, par...  28.8 us
    all_to_all x2, starting transfers between devices, exchange(): return lax.all_to_all(value, axis, split_axis=0, concat_axis=0, tiled=True)  10.3 us
    pallas_call x1, Pallas kernels, fetch(): pl.pallas_call(functools.partial(fetch_kernel, ids.shape[0] // blocks, fe...  5.29 us
    pallas_call x1, Pallas kernels, spread(): pl.pallas_call(functools.partial(spread_kernel, span, own), grid_spec=plt...  5.16 us
  transfers between devices with their start and end apart: 34, of which 12 were waited for; matrix products, arithmetic and copies ran while one was open for 8% of the time, Pallas kernels for 17%

profile of v5, /device:TPU:1, one launch (start us, length us, event | category | flops | bytes accessed | tf_op | source)
XLA Modules:
  0.0 216.8 jit_solution(10698002099810018432)
XLA Ops:
  0.7 1.1 reduce_sum.45
  1.9 1.2 multiply_reduce_fusion
  4.1 4.3 %all-to-all-start = ((f16[4,26,512]{2,1,0:T(8,128)(2,1)}), f16[4,26,512]{2,1,0:T(8,128)(2,1)S(1)}, u32[]{:S(2)}, u32[]{:S(2)}) async-start(f16[4,26,512]{2,1,0:T(8,128)(2,1)} %pad_maximum_fusion.12), calls=%async_computation | async-start | bytes 262144 | tf_op jit(solution)/shard_map/all_to_all | solution.py:650
  11.1 1.2 pad_maximum_fusion
  12.4 3.9 %collective-permute-start.2 = (f16[1,104,512]{2,1,0:T(8,128)(2,1)S(1)}, f16[1,104,512]{2,1,0:T(8,128)(2,1)S(1)}, u32[]{:S(2)}, u32[]{:S(2)}) collective-permute-start(f16[1,104,512]{2,1,0:T(8,128)(2,1)S(1)} %reshape.334), channel_id=1, source_target_pairs={{0,24},{4,28},{8,16},{12,20},{16,8},{20,12},{24,0},{28,4},{1,25},{... | collective-permute-start | bytes 319496 | tf_op jit(solution)/shard_map/ppermute | solution.py:642
  16.7 5.9 %collective-permute-done = f16[1,104,512]{2,1,0:T(8,128)(2,1)S(1)} collective-permute-done((f16[1,104,512]{2,1,0:T(8,128)(2,1)S(1)}, f16[1,104,512]{2,1,0:T(8,128)(2,1)S(1)}, u32[]{:S(2)}, u32[]{:S(2)}) %collective-permute-start) | collective-permute-done | bytes 106528 | tf_op jit(solution)/shard_map/ppermute | solution.py:642
  22.7 2.2 %collective-permute-done.1 = f16[1,104,512]{2,1,0:T(8,128)(2,1)S(1)} collective-permute-done((f16[1,104,512]{2,1,0:T(8,128)(2,1)S(1)}, f16[1,104,512]{2,1,0:T(8,128)(2,1)S(1)}, u32[]{:S(2)}, u32[]{:S(2)}) %collective-permute-start.1) | collective-permute-done | bytes 106528 | tf_op jit(solution)/shard_map/ppermute | solution.py:642
  25.0 1.3 collective-permute-start.3
  27.2 1.6 copy.60.w_qkv
  31.0 4.1 %collective-permute-done.3 = f16[4,104,512]{2,1,0:T(8,128)(2,1)} collective-permute-done((f16[4,104,512]{2,1,0:T(8,128)(2,1)S(1)}, f16[4,104,512]{2,1,0:T(8,128)(2,1)}, u32[]{:S(2)}, u32[]{:S(2)}) %collective-permute-start.3) | collective-permute-done | bytes 426016 | tf_op jit(solution)/shard_map/ppermute | solution.py:642
  35.1 1.1 convert_element_type.166.far
  36.2 5.3 %fetch.1 = (bf16[2,1104,128]{2,1,0:T(8,128)(2,1)S(1)}, f32[8,128]{1,0:T(8,128)S(1)}) custom-call(s32[2200]{0:T(1024)S(1)} %reshape.331.ids, f32[4,104,512]{2,1,0:T(8,128)S(1)} %convert_element_type.165.near, f32[4,104,512]{2,1,0:T(8,128)S(1)} %convert_element_type.166.far, s32[2,1104]{1,0:T(2,128)S(1)} %pad.28.labels), custom_call_target="tpu_custom_call" | custom-call | flops 6000000000 | bytes 1000000 | tf_op jit(solution)/shard_map/fetch/pallas_call | solution.py:117
  42.3 59.4 %forward.1 = (bf16[2,4,1104,384]{3,2,1,0:T(8,128)(2,1)}, bf16[2,4,1104,1024]{3,2,1,0:T(8,128)(2,1)}, bf16[8800,128]{1,0:T(8,128)(2,1)}, f32[2,1104,128]{2,1,0:T(...) custom-call(s32[3]{0:T(128)} %pad_add_fusion.1.place, ...), custom_call_target="tpu_custom_call" | custom-call | flops 60000002048 | bytes 1000000 | tf_op jit(solution)/shard_map/forward/pallas_call | solution.py:347
  101.7 2.3 %collective-permute-start.4 = (bf16[16,80,512]{2,1,0:T(8,128)(2,1)}, bf16[16,80,512]{2,1,0:T(8,128)(2,1)S(1)}, u32[]{:S(2)}, u32[]{:S(2)}) collective-permute-start(bf16[16,80,512]{2,1,0:T(8,128)(2,1)} %get-tuple-element.81), channel_id=1, source_target_pairs={{0,1},{1,0},{2,3},{3,2},{4,5},{5,4},{6,7},{7,6},{8,9},{9,8},{10,11... | collective-permute-start | bytes 3932168 | tf_op jit(solution)/shard_map/ppermute | solution.py:642
  105.0 1.9 collective-permute-done.4
  106.9 1.3 add_convert_fusion
  108.3 1.6 collective-permute-start.5
  109.9 1.2 add_convert_fusion.1
  111.1 1.3 collective-permute-start.8
  112.4 1.6 copy-done.2
  114.0 14.2 %score_grads.2 = (f32[2,128,384]{2,1,0:T(8,128)S(1)}, f32[2,1104,128]{2,1,0:T(8,128)S(1)}) custom-call(s32[3]{0:T(128)S(1)} %copy-done, bf16[2,4,1104,1024]{3,2,1,0:T(8,128)(2,1)} %get-tuple-element.78.e, bf16[2,4,1104,384]{3,2,1,0:T(8,128)(2,1)S(1)} %copy-done.1, bf16[2,1104,512]{2,1,0:T(8,128)(2,1)S(1)} %copy-done.2, bf16[2,1104,128]{2,1,0:T(8,128)(2,1)S(1)} %copy-done.5, ...), custom_call_target="tpu_custom_call" | custom-call | flops 16000000000 | bytes 1000000 | tf_op jit(solution)/shard_map/score_grads/pallas_call | solution.py:463
  128.9 14.6 %score_grads.3 = (bf16[16,16,512]{2,1,0:T(8,128)(2,1)S(1)}, bf16[16,16,512]{2,1,0:T(8,128)(2,1)S(1)}, f32[2,1104,128]{2,1,0:T(8,128)S(1)}) custom-call(s32[3]{0:T(128)S(1)} %copy-done, bf16[2,4,1104,1024]{3,2,1,0:T(8,128)(2,1)} %get-tuple-element.78.e, bf16[2,4,1104,384]{3,2,1,0:T(8,128)(2,1)S(1)} %copy-done.1, bf16[2,1104,512]{2,1,0:T(8,128)(2,1)S(1)} %copy-done.3, ...), custom_call_target="tpu_custom_call" | custom-call | flops 16000000000 | bytes 1000000 | tf_op jit(solution)/shard_map/score_grads/pallas_call | solution.py:463
  143.5 5.2 %spread.1 = (bf16[4,4,25,512]{3,2,1,0:T(8,128)(2,1)S(1)}, bf16[4,4,25,512]{3,2,1,0:T(8,128)(2,1)S(1)}) custom-call(s32[2200]{0:T(1024)S(1)} %reshape.331.ids, f32[2,1104,128]{2,1,0:T(8,128)S(1)} %get-tuple-element.92.rows), custom_call_target="tpu_custom_call" | custom-call | flops 7000000000 | bytes 1000000 | tf_op jit(solution)/shard_map/spread/pallas_call | solution.py:523
  148.7 1.5 collective-permute-start.6
  150.4 2.3 %collective-permute-start.21 = (bf16[80,512]{1,0:T(8,128)(2,1)S(1)}, bf16[80,512]{1,0:T(8,128)(2,1)S(1)}, u32[]{:S(2)}, u32[]{:S(2)}) collective-permute-start(bf16[80,512]{1,0:T(8,128)(2,1)S(1)} %get-tuple-element.134), channel_id=1, source_target_pairs={{0,16},{4,20},{8,24},{12,28},{16,0},{20,4},{24,8},{28,12},{1,17},{... | collective-permute-start | bytes 245768 | tf_op jit(solution)/shard_map/ppermute | solution.py:642
  152.7 1.3 collective-permute-start.22
  154.0 1.5 collective-permute-start.10
  155.5 1.2 collective-permute-start.12
  156.7 1.1 collective-permute-done.22
  157.9 3.2 %collective-permute-start.25 = (bf16[80,512]{1,0:T(8,128)(2,1)S(1)}, bf16[80,512]{1,0:T(8,128)(2,1)S(1)}, u32[]{:S(2)}, u32[]{:S(2)}) collective-permute-start(bf16[80,512]{1,0:T(8,128)(2,1)S(1)} %fusion.13), channel_id=1, source_target_pairs={{0,24},{4,28},{8,16},{12,20},{16,8},{20,12},{24,0},{28,4},{1,25},{... | collective-permute-start | bytes 245768 | tf_op jit(solution)/shard_map/ppermute | solution.py:642
  162.3 1.4 collective-permute-start.11
  163.7 4.9 %collective-permute-done.24 = bf16[80,512]{1,0:T(8,128)(2,1)S(1)} collective-permute-done((bf16[80,512]{1,0:T(8,128)(2,1)S(1)}, bf16[80,512]{1,0:T(8,128)(2,1)S(1)}, u32[]{:S(2)}, u32[]{:S(2)}) %collective-permute-start.24) | collective-permute-done | bytes 81952 | tf_op jit(solution)/shard_map/ppermute | solution.py:642
  168.8 2.1 collective-permute-start.29
  170.9 1.2 collective-permute-start.26
  173.3 1.3 collective-permute-start.30
  174.6 1.1 collective-permute-done.26
  176.9 3.5 %collective-permute-done.16 = bf16[8,16,512]{2,1,0:T(8,128)(2,1)S(1)} collective-permute-done((bf16[8,16,512]{2,1,0:T(8,128)(2,1)S(1)}, bf16[8,16,512]{2,1,0:T(8,128)(2,1)S(1)}, u32[]{:S(2)}, u32[]{:S(2)}) %collective-permute-start.16) | collective-permute-done | bytes 131104 | tf_op jit(solution)/shard_map/ppermute | solution.py:642
  180.9 2.4 %collective-permute-start.15 = (bf16[4,25,512]{2,1,0:T(8,128)(2,1)S(1)}, bf16[4,25,512]{2,1,0:T(8,128)(2,1)S(1)}, u32[]{:S(2)}, u32[]{:S(2)}) collective-permute-start(bf16[4,25,512]{2,1,0:T(8,128)(2,1)S(1)} %get-tuple-element.131), channel_id=1, source_target_pairs={{0,24},{4,28},{8,16},{12,20},{16,8},{20,12},{24,0},{28,4},{1,25},{... | collective-permute-start | bytes 307208 | tf_op jit(solution)/shard_map/ppermute | solution.py:642
  183.6 1.4 collective-permute-done.17
  184.9 2.2 collective-permute-start.31
  188.1 6.2 %collective-permute-done.14 = bf16[4,25,512]{2,1,0:T(8,128)(2,1)S(1)} collective-permute-done((bf16[4,25,512]{2,1,0:T(8,128)(2,1)S(1)}, bf16[4,25,512]{2,1,0:T(8,128)(2,1)S(1)}, u32[]{:S(2)}, u32[]{:S(2)}) %collective-permute-start.14) | collective-permute-done | bytes 102432 | tf_op jit(solution)/shard_map/ppermute | solution.py:642
  195.0 6.0 %all-to-all-start.1 = ((bf16[4,25,512]{2,1,0:T(8,128)(2,1)}), bf16[4,25,512]{2,1,0:T(8,128)(2,1)}, u32[]{:S(2)}, u32[]{:S(2)}) async-start(bf16[4,25,512]{2,1,0:T(8,128)(2,1)} %fusion.10), calls=%async_computation.1 | async-start | bytes 262144 | tf_op jit(solution)/shard_map/all_to_all | solution.py:650
  201.2 3.8 %all-to-all-done.1 = bf16[4,25,512]{2,1,0:T(8,128)(2,1)} async-done(((bf16[4,25,512]{2,1,0:T(8,128)(2,1)}), bf16[4,25,512]{2,1,0:T(8,128)(2,1)}, u32[]{:S(2)}, u32[]{:S(2)}) %all-to-all-start.1) | async-done | bytes 102432 | tf_op jit(solution)/shard_map/all_to_all | solution.py:650
  206.2 1.1 pad_maximum_fusion.2.near
  207.3 1.1 collective-permute-start.28
  208.4 3.2 %finish_tail.1 = (f32[512,512]{1,0:T(8,128)}, f32[512,512]{1,0:T(8,128)}, f32[512,512]{1,0:T(8,128)}, f32[100,512]{1,0:T(8,128)}, f32[1,512]{1,0:T(1,128)}, /*in...) custom-call(s32[3]{0:T(128)S(1)} %copy-done, ...), custom_call_target="tpu_custom_call" | custom-call | flops 5000000000 | bytes 1000000 | tf_op jit(solution)/shard_map/finish_tail/pallas_call | solution.py:621
  211.6 1.1 fusion.25
  213.5 3.3 %finish.1 = (f32[512,512]{1,0:T(8,128)}, f32[512,1024]{1,0:T(8,128)}, f32[1024,512]{1,0:T(8,128)}) custom-call(s32[3]{0:T(128)S(1)} %copy-done, bf16[16,48,512]{2,1,0:T(8,128)(2,1)S(1)} %pad_maximum_fusion.2.near, bf16[16,48,512]{2,1,0:T(8,128)(2,1)S(1)} %collective-permute-done.28.far, bf16[16,32,512]{2,1,0:T(8,128)(2,1)S(1)} %pad_maximum_fusion.5.near_q, ...), custom_call_target="tpu_custom_call" | custom-call | flops 5000000000 | bytes 1000000 | tf_op jit(solution)/shard_map/finish/pallas_call | solution.py:563
  (151 shorter events, 18.3 us)
Async XLA Ops:
  0.7 7.8 %copy-start.18 = (f32[512]{0:T(512)S(1)}, f32[512]{0:T(512)}, u32[]{:S(2)}) copy-start(f32[512]{0:T(512)} %param.33) | copy-start | bytes 6148
  0.7 7.8 %copy-start.19 = (f32[512]{0:T(512)S(1)}, f32[512]{0:T(512)}, u32[]{:S(2)}) copy-start(f32[512]{0:T(512)} %param.30) | copy-start | bytes 6148
  0.7 8.5 %copy-start.16 = (s32[2,1100]{1,0:T(2,128)S(1)}, s32[2,1100]{1,0:T(2,128)}, u32[]{:S(2)}) copy-start(s32[2,1100]{1,0:T(2,128)} %param.44) | copy-start | bytes 26404
  0.7 8.6 %copy-start.17 = (s32[2,1000]{1,0:T(2,128)S(1)}, s32[2,1000]{1,0:T(2,128)}, u32[]{:S(2)}) copy-start(s32[2,1000]{1,0:T(2,128)} %param.45) | copy-start | bytes 24004
  0.7 8.6 %copy-start.15 = (bf16[100,512]{1,0:T(8,128)(2,1)S(1)}, bf16[100,512]{1,0:T(8,128)(2,1)}, u32[]{:S(2)}) copy-start(bf16[100,512]{1,0:T(8,128)(2,1)} %param.26) | copy-start | bytes 307204
  0.7 8.7 %copy-start.11 = (bf16[512,512]{1,0:T(8,128)(2,1)S(1)}, bf16[512,512]{1,0:T(8,128)(2,1)}, u32[]{:S(2)}) copy-start(bf16[512,512]{1,0:T(8,128)(2,1)} %param.29) | copy-start | bytes 1572868
  3.1 6.6 %copy-start.12 = (bf16[512,512]{1,0:T(8,128)(2,1)S(1)}, bf16[512,512]{1,0:T(8,128)(2,1)}, u32[]{:S(2)}) copy-start(bf16[512,512]{1,0:T(8,128)(2,1)} %param.31) | copy-start | bytes 1572868
  4.1 8.2 %all-to-all-start = ((f16[4,26,512]{2,1,0:T(8,128)(2,1)}), f16[4,26,512]{2,1,0:T(8,128)(2,1)S(1)}, u32[]{:S(2)}, u32[]{:S(2)}) async-start(f16[4,26,512]{2,1,0:T(8,128)(2,1)} %pad_maximum_fusion.12), calls=%async_computation | async-start | bytes 262144 | tf_op jit(solution)/shard_map/all_to_all | solution.py:650
  12.4 12.5 %collective-permute-start.2 = (f16[1,104,512]{2,1,0:T(8,128)(2,1)S(1)}, f16[1,104,512]{2,1,0:T(8,128)(2,1)S(1)}, u32[]{:S(2)}, u32[]{:S(2)}) collective-permute-start(f16[1,104,512]{2,1,0:T(8,128)(2,1)S(1)} %reshape.334), channel_id=1, source_target_pairs={{0,24},{4,28},{8,16},{12,20},{16,8},{20,12},{24,0},{28,4},{1,25},{... | collective-permute-start | bytes 319496 | tf_op jit(solution)/shard_map/ppermute | solution.py:642
  16.3 8.6 %collective-permute-start.1 = (f16[1,104,512]{2,1,0:T(8,128)(2,1)S(1)}, f16[1,104,512]{2,1,0:T(8,128)(2,1)S(1)}, u32[]{:S(2)}, u32[]{:S(2)}) collective-permute-start(f16[1,104,512]{2,1,0:T(8,128)(2,1)S(1)} %reshape.334), channel_id=1, source_target_pairs={{0,16},{4,20},{8,24},{12,28},{16,0},{20,4},{24,8},{28,12},{1,17},{... | collective-permute-start | bytes 319496 | tf_op jit(solution)/shard_map/ppermute | solution.py:642
  16.3 6.3 %collective-permute-start = (f16[1,104,512]{2,1,0:T(8,128)(2,1)S(1)}, f16[1,104,512]{2,1,0:T(8,128)(2,1)S(1)}, u32[]{:S(2)}, u32[]{:S(2)}) collective-permute-start(f16[1,104,512]{2,1,0:T(8,128)(2,1)S(1)} %reshape.334), channel_id=1, source_target_pairs={{0,8},{4,12},{8,0},{12,4},{16,24},{20,28},{24,16},{28,20},{1,9},{5... | collective-permute-start | bytes 319496 | tf_op jit(solution)/shard_map/ppermute | solution.py:642
  25.0 10.1 %collective-permute-start.3 = (f16[4,104,512]{2,1,0:T(8,128)(2,1)S(1)}, f16[4,104,512]{2,1,0:T(8,128)(2,1)}, u32[]{:S(2)}, u32[]{:S(2)}) collective-permute-start(f16[4,104,512]{2,1,0:T(8,128)(2,1)S(1)} %constant_dynamic-update-slice_fusion), channel_id=1, source_target_pairs={{0,4},{4,0},{8,12},{12,8},{16,20},{20,16},{24,28},{28,24},{1,5},{5... | collective-permute-start | bytes 1277960 | tf_op jit(solution)/shard_map/ppermute | solution.py:642
  42.3 61.7 %copy-start.20 = (f32[512]{0:T(512)S(1)}, f32[512]{0:T(512)}, u32[]{:S(2)}) copy-start(f32[512]{0:T(512)} %param.27) | copy-start | bytes 6148
  101.7 5.2 %collective-permute-start.4 = (bf16[16,80,512]{2,1,0:T(8,128)(2,1)}, bf16[16,80,512]{2,1,0:T(8,128)(2,1)S(1)}, u32[]{:S(2)}, u32[]{:S(2)}) collective-permute-start(bf16[16,80,512]{2,1,0:T(8,128)(2,1)} %get-tuple-element.81), channel_id=1, source_target_pairs={{0,1},{1,0},{2,3},{3,2},{4,5},{5,4},{6,7},{7,6},{8,9},{9,8},{10,11... | collective-permute-start | bytes 3932168 | tf_op jit(solution)/shard_map/ppermute | solution.py:642
  104.3 8.1 %copy-start.1 = (bf16[2,4,1104,384]{3,2,1,0:T(8,128)(2,1)S(1)}, bf16[2,4,1104,384]{3,2,1,0:T(8,128)(2,1)}, u32[]{:S(2)}) copy-start(bf16[2,4,1104,384]{3,2,1,0:T(8,128)(2,1)} %get-tuple-element.79.qkv) | copy-start | bytes 20348932
  108.3 4.1 %copy-start = (s32[3]{0:T(128)S(1)}, s32[3]{0:T(128)}, u32[]{:S(2)}) copy-start(s32[3]{0:T(128)} %pad_add_fusion.1.place) | copy-start | bytes 40
  108.3 4.1 %copy-start.5 = (bf16[2,1104,128]{2,1,0:T(8,128)(2,1)S(1)}, bf16[2,1104,128]{2,1,0:T(8,128)(2,1)}, u32[]{:S(2)}) copy-start(bf16[2,1104,128]{2,1,0:T(8,128)(2,1)} %copy-done.4) | copy-start | bytes 1695748
  108.3 20.2 %collective-permute-start.5 = (bf16[8,48,512]{2,1,0:T(8,128)(2,1)S(1)}, bf16[8,48,512]{2,1,0:T(8,128)(2,1)S(1)}, u32[]{:S(2)}, u32[]{:S(2)}) collective-permute-start(bf16[8,48,512]{2,1,0:T(8,128)(2,1)S(1)} %get-tuple-element.126), channel_id=1, source_target_pairs={{0,2},{1,3},{2,0},{3,1},{4,6},{5,7},{6,4},{7,5},{8,10},{9,11},{10,... | collective-permute-start | bytes 1179656 | tf_op jit(solution)/shard_map/ppermute | solution.py:642
  111.1 17.2 %collective-permute-start.8 = (bf16[8,32,512]{2,1,0:T(8,128)(2,1)S(1)}, bf16[8,32,512]{2,1,0:T(8,128)(2,1)S(1)}, u32[]{:S(2)}, u32[]{:S(2)}) collective-permute-start(bf16[8,32,512]{2,1,0:T(8,128)(2,1)S(1)} %get-tuple-element.124), channel_id=1, source_target_pairs={{0,4},{4,0},{8,12},{12,8},{16,20},{20,16},{24,28},{28,24},{1,5},{5... | collective-permute-start | bytes 786440 | tf_op jit(solution)/shard_map/ppermute | solution.py:642
  114.0 14.8 %copy-start.3 = (bf16[2,1104,512]{2,1,0:T(8,128)(2,1)S(1)}, bf16[2,1104,512]{2,1,0:T(8,128)(2,1)}, u32[]{:S(2)}) copy-start(bf16[2,1104,512]{2,1,0:T(8,128)(2,1)} %get-tuple-element.84.back) | copy-start | bytes 6782980
  114.0 14.8 %copy-start.7 = (f32[128,512]{1,0:T(8,128)S(1)}, f32[128,512]{1,0:T(8,128)}, u32[]{:S(2)}) copy-start(f32[128,512]{1,0:T(8,128)} %get-tuple-element.88.refs_1_) | copy-start | bytes 786436
  128.3 21.8 %collective-permute-start.9 = (bf16[4,32,512]{2,1,0:T(8,128)(2,1)S(1)}, bf16[4,32,512]{2,1,0:T(8,128)(2,1)S(1)}, u32[]{:S(2)}, u32[]{:S(2)}) collective-permute-start(bf16[4,32,512]{2,1,0:T(8,128)(2,1)S(1)} %fusion.4), channel_id=1, source_target_pairs={{0,2},{1,3},{2,0},{3,1},{4,6},{5,7},{6,4},{7,5},{8,10},{9,11},{10,... | collective-permute-start | bytes 393224 | tf_op jit(solution)/shard_map/ppermute | solution.py:642
  128.6 21.6 %collective-permute-start.7 = (bf16[4,48,512]{2,1,0:T(8,128)(2,1)S(1)}, bf16[4,48,512]{2,1,0:T(8,128)(2,1)S(1)}, u32[]{:S(2)}, u32[]{:S(2)}) collective-permute-start(bf16[4,48,512]{2,1,0:T(8,128)(2,1)S(1)} %fusion.3), channel_id=1, source_target_pairs={{0,4},{4,0},{8,12},{12,8},{16,20},{20,16},{24,28},{28,24},{1,5},{5... | collective-permute-start | bytes 589832 | tf_op jit(solution)/shard_map/ppermute | solution.py:642
  148.7 5.3 %collective-permute-start.6 = (bf16[16,16,512]{2,1,0:T(8,128)(2,1)S(1)}, bf16[16,16,512]{2,1,0:T(8,128)(2,1)S(1)}, u32[]{:S(2)}, u32[]{:S(2)}) collective-permute-start(bf16[16,16,512]{2,1,0:T(8,128)(2,1)S(1)} %get-tuple-element.90), channel_id=1, source_target_pairs={{0,1},{1,0},{2,3},{3,2},{4,5},{5,4},{6,7},{7,6},{8,9},{9,8},{10,11... | collective-permute-start | bytes 786440 | tf_op jit(solution)/shard_map/ppermute | solution.py:642
  150.3 6.4 %collective-permute-start.20 = (bf16[80,512]{1,0:T(8,128)(2,1)S(1)}, bf16[80,512]{1,0:T(8,128)(2,1)S(1)}, u32[]{:S(2)}, u32[]{:S(2)}) collective-permute-start(bf16[80,512]{1,0:T(8,128)(2,1)S(1)} %get-tuple-element.133), channel_id=1, source_target_pairs={{0,8},{4,12},{8,0},{12,4},{16,24},{20,28},{24,16},{28,20},{1,9},{5... | collective-permute-start | bytes 245768 | tf_op jit(solution)/shard_map/ppermute | solution.py:642
  150.4 6.3 %collective-permute-start.21 = (bf16[80,512]{1,0:T(8,128)(2,1)S(1)}, bf16[80,512]{1,0:T(8,128)(2,1)S(1)}, u32[]{:S(2)}, u32[]{:S(2)}) collective-permute-start(bf16[80,512]{1,0:T(8,128)(2,1)S(1)} %get-tuple-element.134), channel_id=1, source_target_pairs={{0,16},{4,20},{8,24},{12,28},{16,0},{20,4},{24,8},{28,12},{1,17},{... | collective-permute-start | bytes 245768 | tf_op jit(solution)/shard_map/ppermute | solution.py:642
  152.7 5.2 %collective-permute-start.22 = (bf16[80,512]{1,0:T(8,128)(2,1)S(1)}, bf16[80,512]{1,0:T(8,128)(2,1)S(1)}, u32[]{:S(2)}, u32[]{:S(2)}) collective-permute-start(bf16[80,512]{1,0:T(8,128)(2,1)S(1)} %get-tuple-element.135), channel_id=1, source_target_pairs={{0,24},{4,28},{8,16},{12,20},{16,8},{20,12},{24,0},{28,4},{1,25},{... | collective-permute-start | bytes 245768 | tf_op jit(solution)/shard_map/ppermute | solution.py:642
  154.0 8.3 %collective-permute-start.10 = (bf16[8,16,512]{2,1,0:T(8,128)(2,1)S(1)}, bf16[8,16,512]{2,1,0:T(8,128)(2,1)S(1)}, u32[]{:S(2)}, u32[]{:S(2)}) collective-permute-start(bf16[8,16,512]{2,1,0:T(8,128)(2,1)S(1)} %add_convert_fusion.6), channel_id=1, source_target_pairs={{0,2},{1,3},{2,0},{3,1},{4,6},{5,7},{6,4},{7,5},{8,10},{9,11},{10,... | collective-permute-start | bytes 393224 | tf_op jit(solution)/shard_map/ppermute | solution.py:642
  155.5 16.7 %collective-permute-start.12 = (bf16[4,4,25,512]{3,2,1,0:T(8,128)(2,1)S(1)}, bf16[4,4,25,512]{3,2,1,0:T(8,128)(2,1)S(1)}, u32[]{:S(2)}, u32[]{:S(2)}) collective-permute-start(bf16[4,4,25,512]{3,2,1,0:T(8,128)(2,1)S(1)} %get-tuple-element.97), channel_id=1, source_target_pairs={{0,4},{4,0},{8,12},{12,8},{16,20},{20,16},{24,28},{28,24},{1,5},{5... | collective-permute-start | bytes 1228808 | tf_op jit(solution)/shard_map/ppermute | solution.py:642
  157.9 5.9 %collective-permute-start.25 = (bf16[80,512]{1,0:T(8,128)(2,1)S(1)}, bf16[80,512]{1,0:T(8,128)(2,1)S(1)}, u32[]{:S(2)}, u32[]{:S(2)}) collective-permute-start(bf16[80,512]{1,0:T(8,128)(2,1)S(1)} %fusion.13), channel_id=1, source_target_pairs={{0,24},{4,28},{8,16},{12,20},{16,8},{20,12},{24,0},{28,4},{1,25},{... | collective-permute-start | bytes 245768 | tf_op jit(solution)/shard_map/ppermute | solution.py:642
  161.1 7.6 %collective-permute-start.24 = (bf16[80,512]{1,0:T(8,128)(2,1)S(1)}, bf16[80,512]{1,0:T(8,128)(2,1)S(1)}, u32[]{:S(2)}, u32[]{:S(2)}) collective-permute-start(bf16[80,512]{1,0:T(8,128)(2,1)S(1)} %fusion.13), channel_id=1, source_target_pairs={{0,16},{4,20},{8,24},{12,28},{16,0},{20,4},{24,8},{28,12},{1,17},{... | collective-permute-start | bytes 245768 | tf_op jit(solution)/shard_map/ppermute | solution.py:642
  162.2 6.5 %collective-permute-start.23 = (bf16[80,512]{1,0:T(8,128)(2,1)S(1)}, bf16[80,512]{1,0:T(8,128)(2,1)S(1)}, u32[]{:S(2)}, u32[]{:S(2)}) collective-permute-start(bf16[80,512]{1,0:T(8,128)(2,1)S(1)} %fusion.13), channel_id=1, source_target_pairs={{0,8},{4,12},{8,0},{12,4},{16,24},{20,28},{24,16},{28,20},{1,9},{5... | collective-permute-start | bytes 245768 | tf_op jit(solution)/shard_map/ppermute | solution.py:642
  162.3 9.8 %collective-permute-start.11 = (bf16[8,16,512]{2,1,0:T(8,128)(2,1)S(1)}, bf16[8,16,512]{2,1,0:T(8,128)(2,1)S(1)}, u32[]{:S(2)}, u32[]{:S(2)}) collective-permute-start(bf16[8,16,512]{2,1,0:T(8,128)(2,1)S(1)} %add_convert_fusion.5), channel_id=1, source_target_pairs={{0,8},{4,12},{8,0},{12,4},{16,24},{20,28},{24,16},{28,20},{1,9},{5... | collective-permute-start | bytes 393224 | tf_op jit(solution)/shard_map/ppermute | solution.py:642
  168.8 4.5 %collective-permute-start.29 = (bf16[4,32,512]{2,1,0:T(8,128)(2,1)S(1)}, bf16[4,32,512]{2,1,0:T(8,128)(2,1)S(1)}, u32[]{:S(2)}, u32[]{:S(2)}) collective-permute-start(bf16[4,32,512]{2,1,0:T(8,128)(2,1)S(1)} %pad_maximum_fusion.11), channel_id=1, source_target_pairs={{0,2},{1,3},{2,0},{3,1},{4,6},{5,7},{6,4},{7,5},{8,10},{9,11},{10,... | collective-permute-start | bytes 393224 | tf_op jit(solution)/shard_map/ppermute | solution.py:642
  170.9 4.8 %collective-permute-start.26 = (bf16[4,48,512]{2,1,0:T(8,128)(2,1)S(1)}, bf16[4,48,512]{2,1,0:T(8,128)(2,1)S(1)}, u32[]{:S(2)}, u32[]{:S(2)}) collective-permute-start(bf16[4,48,512]{2,1,0:T(8,128)(2,1)S(1)} %slice.170), channel_id=1, source_target_pairs={{0,4},{4,0},{8,12},{12,8},{16,20},{20,16},{24,28},{28,24},{1,5},{5... | collective-permute-start | bytes 589832 | tf_op jit(solution)/shard_map/ppermute | solution.py:642
  172.3 8.1 %collective-permute-start.16 = (bf16[8,16,512]{2,1,0:T(8,128)(2,1)S(1)}, bf16[8,16,512]{2,1,0:T(8,128)(2,1)S(1)}, u32[]{:S(2)}, u32[]{:S(2)}) collective-permute-start(bf16[8,16,512]{2,1,0:T(8,128)(2,1)S(1)} %add_convert_fusion.4), channel_id=1, source_target_pairs={{0,16},{4,20},{8,24},{12,28},{16,0},{20,4},{24,8},{28,12},{1,17},{... | collective-permute-start | bytes 393224 | tf_op jit(solution)/shard_map/ppermute | solution.py:642
  173.3 10.0 %collective-permute-start.30 = (bf16[8,32,512]{2,1,0:T(8,128)(2,1)S(1)}, bf16[8,32,512]{2,1,0:T(8,128)(2,1)S(1)}, u32[]{:S(2)}, u32[]{:S(2)}) collective-permute-start(bf16[8,32,512]{2,1,0:T(8,128)(2,1)S(1)} %pad_maximum_fusion.10), channel_id=1, source_target_pairs={{0,4},{4,0},{8,12},{12,8},{16,20},{20,16},{24,28},{28,24},{1,5},{5... | collective-permute-start | bytes 786440 | tf_op jit(solution)/shard_map/ppermute | solution.py:642
  176.5 29.7 %collective-permute-start.27 = (bf16[8,48,512]{2,1,0:T(8,128)(2,1)}, bf16[8,48,512]{2,1,0:T(8,128)(2,1)}, u32[]{:S(2)}, u32[]{:S(2)}) collective-permute-start(bf16[8,48,512]{2,1,0:T(8,128)(2,1)} %pad_maximum_fusion.6), channel_id=1, source_target_pairs={{0,2},{1,3},{2,0},{3,1},{4,6},{5,7},{6,4},{7,5},{8,10},{9,11},{10,... | collective-permute-start | bytes 1179656 | tf_op jit(solution)/shard_map/ppermute | solution.py:642
  180.5 4.5 %collective-permute-start.17 = (bf16[8,16,512]{2,1,0:T(8,128)(2,1)S(1)}, bf16[8,16,512]{2,1,0:T(8,128)(2,1)S(1)}, u32[]{:S(2)}, u32[]{:S(2)}) collective-permute-start(bf16[8,16,512]{2,1,0:T(8,128)(2,1)S(1)} %add_convert_fusion.3), channel_id=1, source_target_pairs={{0,4},{4,0},{8,12},{12,8},{16,20},{20,16},{24,28},{28,24},{1,5},{5... | collective-permute-start | bytes 393224 | tf_op jit(solution)/shard_map/ppermute | solution.py:642
  180.8 6.3 %collective-permute-start.13 = (bf16[4,25,512]{2,1,0:T(8,128)(2,1)S(1)}, bf16[4,25,512]{2,1,0:T(8,128)(2,1)S(1)}, u32[]{:S(2)}, u32[]{:S(2)}) collective-permute-start(bf16[4,25,512]{2,1,0:T(8,128)(2,1)S(1)} %get-tuple-element.130), channel_id=1, source_target_pairs={{0,8},{4,12},{8,0},{12,4},{16,24},{20,28},{24,16},{28,20},{1,9},{5... | collective-permute-start | bytes 307208 | tf_op jit(solution)/shard_map/ppermute | solution.py:642
  180.9 7.2 %collective-permute-start.15 = (bf16[4,25,512]{2,1,0:T(8,128)(2,1)S(1)}, bf16[4,25,512]{2,1,0:T(8,128)(2,1)S(1)}, u32[]{:S(2)}, u32[]{:S(2)}) collective-permute-start(bf16[4,25,512]{2,1,0:T(8,128)(2,1)S(1)} %get-tuple-element.131), channel_id=1, source_target_pairs={{0,24},{4,28},{8,16},{12,20},{16,8},{20,12},{24,0},{28,4},{1,25},{... | collective-permute-start | bytes 307208 | tf_op jit(solution)/shard_map/ppermute | solution.py:642
  183.2 11.0 %collective-permute-start.14 = (bf16[4,25,512]{2,1,0:T(8,128)(2,1)S(1)}, bf16[4,25,512]{2,1,0:T(8,128)(2,1)S(1)}, u32[]{:S(2)}, u32[]{:S(2)}) collective-permute-start(bf16[4,25,512]{2,1,0:T(8,128)(2,1)S(1)} %get-tuple-element.132), channel_id=1, source_target_pairs={{0,16},{4,20},{8,24},{12,28},{16,0},{20,4},{24,8},{28,12},{1,17},{... | collective-permute-start | bytes 307208 | tf_op jit(solution)/shard_map/ppermute | solution.py:642
  184.9 28.6 %collective-permute-start.31 = (bf16[16,32,512]{2,1,0:T(8,128)(2,1)S(1)}, bf16[16,32,512]{2,1,0:T(8,128)(2,1)S(1)}, u32[]{:S(2)}, u32[]{:S(2)}) collective-permute-start(bf16[16,32,512]{2,1,0:T(8,128)(2,1)S(1)} %pad_maximum_fusion.5.near_q), channel_id=1, source_target_pairs={{0,1},{1,0},{2,3},{3,2},{4,5},{5,4},{6,7},{7,6},{8,9},{9,8},{10,11... | collective-permute-start | bytes 1572872 | tf_op jit(solution)/shard_map/ppermute | solution.py:642
  187.1 13.9 %collective-permute-start.18 = (bf16[8,16,512]{2,1,0:T(8,128)(2,1)S(1)}, bf16[8,16,512]{2,1,0:T(8,128)(2,1)S(1)}, u32[]{:S(2)}, u32[]{:S(2)}) collective-permute-start(bf16[8,16,512]{2,1,0:T(8,128)(2,1)S(1)} %add_convert_fusion.2), channel_id=1, source_target_pairs={{0,2},{1,3},{2,0},{3,1},{4,6},{5,7},{6,4},{7,5},{8,10},{9,11},{10,... | collective-permute-start | bytes 393224 | tf_op jit(solution)/shard_map/ppermute | solution.py:642
  195.0 10.0 %all-to-all-start.1 = ((bf16[4,25,512]{2,1,0:T(8,128)(2,1)}), bf16[4,25,512]{2,1,0:T(8,128)(2,1)}, u32[]{:S(2)}, u32[]{:S(2)}) async-start(bf16[4,25,512]{2,1,0:T(8,128)(2,1)} %fusion.10), calls=%async_computation.1 | async-start | bytes 262144 | tf_op jit(solution)/shard_map/all_to_all | solution.py:650
  201.0 7.4 %collective-permute-start.19 = (bf16[16,16,512]{2,1,0:T(8,128)(2,1)S(1)}, bf16[16,16,512]{2,1,0:T(8,128)(2,1)S(1)}, u32[]{:S(2)}, u32[]{:S(2)}) collective-permute-start(bf16[16,16,512]{2,1,0:T(8,128)(2,1)S(1)} %pad_maximum_fusion.9.near), channel_id=1, source_target_pairs={{0,1},{1,0},{2,3},{3,2},{4,5},{5,4},{6,7},{7,6},{8,9},{9,8},{10,11... | collective-permute-start | bytes 786440 | tf_op jit(solution)/shard_map/ppermute | solution.py:642
  207.3 5.4 %copy-start.8 = (f32[2048,25]{0,1:T(8,128)S(1)}, f32[2048,25]{0,1:T(8,128)}, u32[]{:S(2)}) copy-start(f32[2048,25]{0,1:T(8,128)} %param.25) | copy-start | bytes 614404
  207.3 6.2 %collective-permute-start.28 = (bf16[16,48,512]{2,1,0:T(8,128)(2,1)S(1)}, bf16[16,48,512]{2,1,0:T(8,128)(2,1)S(1)}, u32[]{:S(2)}, u32[]{:S(2)}) collective-permute-start(bf16[16,48,512]{2,1,0:T(8,128)(2,1)S(1)} %pad_maximum_fusion.2.near), channel_id=1, source_target_pairs={{0,1},{1,0},{2,3},{3,2},{4,5},{5,4},{6,7},{7,6},{8,9},{9,8},{10,11... | collective-permute-start | bytes 2359304 | tf_op jit(solution)/shard_map/ppermute | solution.py:642
  (7 other events, 11.6 us)
